TPU v7x, 32 devices: a whole 2x2x4 slice. The times are simulated.
32 devices in a mesh: grp: 2 (over y), ctx: 4 (over z), tp: 2 (over x), sub: 2 (over core).
Axes of the slice: x: 2, y: 2, z: 4, core: 2. Of those that a mesh axis runs over, the one named last changes fastest.
Arguments:
- queries: bfloat16 [2048, 8192], P(('grp', 'ctx', 'sub'), 'tp'), parts along dimension 0
- keys: bfloat16 [2048, 1024], P(('grp', 'ctx', 'sub'), 'tp'), parts along dimension 0
- values: bfloat16 [2048, 1024], P(('grp', 'ctx', 'sub'), 'tp'), parts along dimension 0, may hold values from -6 to 6
- beacon_keys: bfloat16 [1024, 1024], P(('grp', 'ctx', 'sub'), 'tp'), parts along dimension 0, may hold values from -6 to 6
- beacon_values: bfloat16 [1024, 1024], P(('grp', 'ctx', 'sub'), 'tp'), parts along dimension 0, may hold values from -6 to 6
- grad_out: bfloat16 [2048, 8192], P(('grp', 'ctx', 'sub'), 'tp'), parts along dimension 0, may hold values from -6 to 6
- ratios: int32 [8], P('grp'), parts along dimension 0, may hold values from 2 to 32, as said below
Outputs:
- grad_queries: bfloat16 [2048, 8192], P(('grp', 'ctx', 'sub'), 'tp'), parts along dimension 0
- grad_keys: bfloat16 [2048, 1024], P(('grp', 'ctx', 'sub'), 'tp'), parts along dimension 0
- grad_values: bfloat16 [2048, 1024], P(('grp', 'ctx', 'sub'), 'tp'), parts along dimension 0
- grad_beacon_keys: bfloat16 [1024, 1024], P(('grp', 'ctx', 'sub'), 'tp'), parts along dimension 0
- grad_beacon_values: bfloat16 [1024, 1024], P(('grp', 'ctx', 'sub'), 'tp'), parts along dimension 0
There are 2 independent parts, one for each index of `grp`. A program takes and returns all parts, laid end to end along the dimension named above; each array names one. Nothing has to cross between parts.
Inputs may be any that keep to these rules, and one draw needn't show every extreme that they name: `ratios`: every ratio is a power of two, and some span other than the last has ratio 2, so that it fills all 128 of its slots.
All inputs are finite; a program needn't handle non-finite values.
Results may differ from a plain program's by a relative error of at most 0.012.
The roundings to bfloat16 on the way count: a program that leaves them out, or rounds other values in their place, can miss the bound.
Values may be sent and summed in bfloat16 or wider, within the bound.
No kernel may reach another device: no remote copies, remote signals or barrier semaphores. Data moves between devices by JAX's collectives and lax.ppermute only.
A program may use at most 64 MiB of HBM per device.

v0:
```python
import functools
import math

import jax
import jax.numpy as jnp
from jax import lax
from jax.experimental import pallas as pl
from jax.experimental.pallas import tpu as pltpu
from jax.sharding import PartitionSpec as P

DH = 128
SPAN = 256
SLOTS = SPAN // 2
HALF = SLOTS // 2
NT = (((1,), (1,)), ((), ()))
HIDDEN = -3e38
JOIN = 4
BLOCK = 16
SCALE = DH ** (-0.5)
LOG_SCALE = SCALE * math.log2(math.e)


def interleave(first, second):
    few, many = sorted((first, second), key=len)
    done = 0
    for index, step in enumerate(few):
        step()
        upto = len(many) * (index + 1) // len(few)
        for other in many[done:upto]:
            other()
        done = upto
    for other in many[done:]:
        other()


def pipeline(chunks, products, softmax, gradients):
    for step in products(0):
        step()
    for chunk in range(chunks):
        matrix = gradients(chunk - 1) if chunk > 0 else []
        matrix = matrix + (products(chunk + 1) if chunk + 1 < chunks else [])
        interleave(matrix, softmax(chunk))
    for step in gradients(chunks - 1):
        step()


def head_cols(head):
    return slice(head * DH, (head + 1) * DH)


def joined(buf, chunk, start, count):
    first = chunk * JOIN + start
    return jnp.concatenate([buf[:, head_cols(first + i)] for i in range(count)], axis=0)


def pair_products(key_buf, value_buf, q_buf, g_buf, chunk, head, score_ref, signal_ref):
    rows = q_buf.shape[0]
    at = [lax.broadcasted_iota(jnp.int32, (rows, DH), axis) for axis in range(2)]
    one_hot = jnp.where(at[0] == at[1], 1.0, 0.0).astype(jnp.bfloat16)
    one_hot = jnp.concatenate([one_hot] * 2, axis=0)

    def score(start):
        queries = jnp.concatenate([joined(q_buf, chunk, start, 2), one_hot], axis=1)
        cols = slice(start * rows, (start + 2) * rows)
        score_ref[:, cols] = lax.dot_general(key_buf[head], queries, NT, preferred_element_type=jnp.float32)

    def signal(start):
        cols = slice(start * rows, (start + 2) * rows)
        signal_ref[:, cols] = lax.dot_general(
            value_buf[head], joined(g_buf, chunk, start, 2), NT, preferred_element_type=jnp.float32
        )

    return [functools.partial(f, start) for f in (score, signal) for start in range(0, JOIN, 2)]


def mask_of(seen):
    return jnp.where(seen, 0.0, HIDDEN).astype(jnp.bfloat16)


def place(key_buf, value_buf, at, keys, values, mask):
    size = mask.shape[0]
    for head in range(key_buf.shape[0]):
        key_buf[head, at : at + size, :DH] = keys[:, head_cols(head)]
        key_buf[head, at : at + size, DH:] = mask
        value_buf[head, at : at + size, :] = values[:, head_cols(head)]


def spread(x):
    return jnp.broadcast_to(x, (8, x.shape[1]))


def exponentials(chunk, grown_out, top_out, total_out):
    score_ref = grown_out.at[chunk]
    columns, width = score_ref.shape
    state = {"top": jnp.full((8, width), HIDDEN, jnp.float32)}

    def top(at):
        for i in range(at, at + BLOCK, 8):
            state["top"] = jnp.maximum(state["top"], score_ref[i : i + 8, :])

    def end_top():
        state["top"] = spread(jnp.max(state["top"], axis=0, keepdims=True))
        top_out[chunk] = state["top"]
        state["total"] = jnp.zeros((8, width), jnp.float32)

    def grow(at):
        for i in range(at, at + BLOCK, 8):
            grown = jnp.exp2((score_ref[i : i + 8, :] - state["top"]) * LOG_SCALE)
            score_ref[i : i + 8, :] = grown
            state["total"] = state["total"] + grown

    def end_grow():
        total_out[chunk] = spread(jnp.sum(state["total"], axis=0, keepdims=True))

    blocks = range(0, columns, BLOCK)
    return [functools.partial(top, at) for at in blocks] + [end_top] + [functools.partial(grow, at) for at in blocks] + [end_grow]


def near_kernel(
    shifts, group, ratios, q_hbm, g_hbm, key_hbm, value_hbm, other_key, other_value, q_buf, g_buf, mask_out, grown_out,
    signal_out, top_out, total_out, own_key, own_value, key_buf, value_buf, sem,
):
    rows = q_buf.shape[0]
    heads = key_buf.shape[0]
    per_head = group // JOIN
    sub = lax.axis_index("sub")
    pairs = [(key_hbm, own_key), (value_hbm, own_value)]
    for head in range(heads):
        cols = slice(head * group * DH, (head + 1) * group * DH)
        pairs += [(q_hbm.at[:, cols], q_buf.at[:, cols]), (g_hbm.at[:, cols], g_buf.at[:, cols])]
    loads = [pltpu.make_async_copy(*pair, sem.at[i]) for i, pair in enumerate(pairs)]
    for load in loads:
        load.start()
    key_at = lax.broadcasted_iota(jnp.int32, (rows, DH), 0)
    token_at = lax.broadcasted_iota(jnp.int32, (rows, DH), 1)
    place(key_buf, value_buf, rows, other_key, other_value, mask_of(key_at < sub * rows))
    here = lax.axis_index("ctx")
    slot_at = lax.broadcasted_iota(jnp.int32, (HALF, DH), 0)
    for shift in range(shifts):
        owner = jnp.maximum(here - 1 - shift, 0)
        live = jnp.where(here > shift, SPAN // ratios[owner], 0)
        for side, first in enumerate((sub * HALF, (1 - sub) * HALF)):
            at = (2 * shift + side) * HALF
            mask_out[at : at + HALF, :] = mask_of(slot_at < live - first)
    loads[0].wait()
    loads[1].wait()
    place(key_buf, value_buf, 0, own_key, own_value, mask_of(key_at <= token_at))

    def products(chunk):
        head = chunk // per_head
        if chunk % per_head == 0:
            loads[2 + 2 * head].wait()
            loads[3 + 2 * head].wait()
        return pair_products(
            key_buf, value_buf, q_buf, g_buf, chunk, head, grown_out.at[chunk], signal_out.at[chunk]
        )

    pipeline(
        heads * per_head,
        products,
        lambda chunk: exponentials(chunk, grown_out, top_out, total_out),
        lambda chunk: [],
    )


def place_far(key_buf, value_buf, far, mask):
    wide = far[0].shape[1] // 2
    for index, source in enumerate(far):
        at = index * HALF
        place(key_buf, value_buf, at, source.at[:, :wide], source.at[:, wide:], mask[at : at + HALF, :])


def far_kernel(shifts, group, q_buf, g_buf, far_mask, near_grown, near_signal, near_top, near_total, *refs):
    far, refs = refs[: 2 * shifts], refs[2 * shifts :]
    share_out, delta_out, slopes_out, own_outs, sent_out = refs[0], refs[1], refs[2], refs[3 : 3 + shifts], refs[3 + shifts]
    refs = refs[4 + shifts :]
    (key_buf, value_buf, dk_buf, dv_buf), sets = refs[:4], (refs[4:7], refs[7:10])
    rows = q_buf.shape[0]
    heads, columns = key_buf.shape[:2]
    wide = heads * DH
    per_head = group // JOIN
    chunks = heads * per_head
    width = JOIN * rows
    place_far(key_buf, value_buf, far, far_mask)

    def products(chunk):
        score_ref, signal_ref, _ = sets[chunk % 2]
        return pair_products(key_buf, value_buf, q_buf, g_buf, chunk, chunk // per_head, score_ref, signal_ref)

    def softmax(chunk):
        score_ref, signal_ref, weight_ref = sets[chunk % 2]
        slope_ref = slopes_out.at[chunk]
        state = {"top": near_top[chunk]}

        def top(at):
            for i in range(at, at + BLOCK, 8):
                state["top"] = jnp.maximum(state["top"], score_ref[i : i + 8, :])

        def end_top():
            state["top"] = spread(jnp.max(state["top"], axis=0, keepdims=True))
            state["total"] = jnp.zeros((8, width), jnp.float32)

        def grow(at):
            for i in range(at, at + BLOCK, 8):
                grown = jnp.exp2((score_ref[i : i + 8, :] - state["top"]) * LOG_SCALE)
                score_ref[i : i + 8, :] = grown
                state["total"] = state["total"] + grown

        def end_grow():
            total = spread(jnp.sum(state["total"], axis=0, keepdims=True))
            shrink = jnp.exp2((near_top[chunk] - state["top"]) * LOG_SCALE)
            state["far"] = 1.0 / (near_total[chunk] * shrink + total)
            state["near"] = shrink * state["far"]
            share_out[chunk] = state["near"]
            state["delta"] = jnp.zeros((8, width), jnp.float32)

        def weigh(grown, signal, share, at):
            probs = [grown[i : i + 8, :] * state[share] for i in range(at, at + BLOCK, 8)]
            weights = jnp.concatenate(probs, axis=0).astype(jnp.bfloat16)
            if share == "far":
                weight_ref[at : at + BLOCK, :] = weights
            terms = weights.astype(jnp.float32) * signal[at : at + BLOCK, :]
            for i in range(0, BLOCK, 8):
                state["delta"] = state["delta"] + terms[i : i + 8]

        def end_weigh():
            state["delta"] = spread(jnp.sum(state["delta"], axis=0, keepdims=True))
            delta_out[chunk] = state["delta"]

        def slope(at):
            slopes = []
            for i in range(at, at + BLOCK, 8):
                probs = score_ref[i : i + 8, :] * state["far"]
                slopes.append(probs * (signal_ref[i : i + 8, :] - state["delta"]))
            slope_ref[at : at + BLOCK, :] = jnp.concatenate(slopes, axis=0).astype(jnp.bfloat16)

        grown, signal = near_grown.at[chunk], near_signal.at[chunk]
        blocks = range(0, columns, BLOCK)
        steps = [functools.partial(top, at) for at in blocks] + [end_top]
        steps += [functools.partial(grow, at) for at in blocks] + [end_grow]
        steps += [functools.partial(weigh, score_ref, signal_ref, "far", at) for at in blocks]
        steps += [functools.partial(weigh, grown, signal, "near", at) for at in range(0, 2 * rows, BLOCK)] + [end_weigh]
        return steps + [functools.partial(slope, at) for at in blocks]

    def gradients(chunk):
        weight_ref = sets[chunk % 2][2]
        head = chunk // per_head
        last = chunk % per_head == per_head - 1

        def collect(total_ref, buf, left, side, factor):
            total = None
            for start in range(0, JOIN, 2):
                cols = slice(start * rows, (start + 2) * rows)
                part = jnp.dot(left(cols), joined(buf, chunk, start, 2), preferred_element_type=jnp.float32)
                total = part if total is None else total + part
            if chunk % per_head:
                total = total + total_ref[...]
            if not last:
                total_ref[...] = total
                return
            cols = slice(side * wide + head * DH, side * wide + (head + 1) * DH)
            for shift, out in enumerate(own_outs):
                at = shift * SLOTS
                out[:, cols] = total[at : at + HALF] * factor
                sent = total[at + HALF : at + SLOTS] * factor
                sent_out[shift * HALF : (shift + 1) * HALF, cols] = sent.astype(sent_out.dtype)

        return [
            functools.partial(collect, dk_buf, q_buf, lambda cols: slopes_out[chunk, :, cols], 0, SCALE),
            functools.partial(collect, dv_buf, g_buf, lambda cols: weight_ref[:, cols], 1, 1.0),
        ]

    pipeline(chunks, products, softmax, gradients)


def near_gradients_kernel(group, q_buf, g_buf, grown, signal, share, delta, slopes_out, own_out, sent_out, *sets):
    rows = q_buf.shape[0]
    wide = own_out.shape[1] // 2
    per_head = group // JOIN
    chunks = wide // DH * per_head
    near = 2 * rows
    totals = {}

    def softmax(chunk):
        weight_ref = sets[chunk % 2]

        def work(at):
            weights, slopes = [], []
            for i in range(at, at + BLOCK, 8):
                probs = grown[chunk, i : i + 8, :] * share[chunk]
                weights.append(probs)
                slopes.append(probs * (signal[chunk, i : i + 8, :] - delta[chunk]))
            weight_ref[at : at + BLOCK, :] = jnp.concatenate(weights, axis=0).astype(jnp.bfloat16)
            slopes_out[chunk, at : at + BLOCK, :] = jnp.concatenate(slopes, axis=0).astype(jnp.bfloat16)

        return [functools.partial(work, at) for at in range(0, near, BLOCK)]

    def gradients(chunk):
        weight_ref = sets[chunk % 2]
        head = chunk // per_head

        def collect(left, buf, side, factor):
            total = totals.pop(side, None)
            for start in range(0, JOIN, 2):
                cols = slice(start * rows, (start + 2) * rows)
                part = jnp.dot(left(cols), joined(buf, chunk, start, 2), preferred_element_type=jnp.float32)
                total = part if total is None else total + part
            if chunk % per_head < per_head - 1:
                totals[side] = total
                return
            cols = slice(side * wide + head * DH, side * wide + (head + 1) * DH)
            own_out[:, cols] = total[:rows] * factor
            sent_out[:, cols] = (total[rows:] * factor).astype(sent_out.dtype)

        return [
            functools.partial(collect, lambda cols: slopes_out[chunk, :, cols], q_buf, 0, SCALE),
            functools.partial(collect, lambda cols: weight_ref[:, cols], g_buf, 1, 1.0),
        ]

    pipeline(chunks, lambda chunk: [], softmax, gradients)


def query_gradients_kernel(group, near_slopes, far_slopes, key_hbm, other_key, *refs):
    far, (dq_hbm, own_key, key_buf, turned_buf, dq_buf, in_sem, out_sem) = refs[:-7], refs[-7:]
    rows = dq_buf.shape[0]
    heads = key_buf.shape[0]
    near = 2 * rows
    per_head = group // JOIN
    load = pltpu.make_async_copy(key_hbm, own_key, in_sem)
    load.start()
    at = rows
    for piece in (other_key, *far):
        size = piece.shape[0]
        for head in range(heads):
            key_buf[head, at : at + size, :] = piece[:, head_cols(head)]
        at += size
    load.wait()
    stores = []
    for head in range(heads):
        key_buf[head, :rows, :] = own_key[:, head_cols(head)]
        turned_buf[head] = key_buf[head].T
        for chunk in range(head * per_head, (head + 1) * per_head):
            for start in range(0, JOIN, 2):
                cols = slice(start * rows, (start + 2) * rows)
                turned = jnp.dot(
                    turned_buf[head, :, :near], near_slopes[chunk, :, cols], preferred_element_type=jnp.float32
                ) + jnp.dot(turned_buf[head, :, near:], far_slopes[chunk, :, cols], preferred_element_type=jnp.float32)
                for i in range(2):
                    dq = turned[:, i * rows : (i + 1) * rows].T * SCALE
                    dq_buf[:, head_cols(chunk * JOIN + start + i)] = dq.astype(jnp.bfloat16)
        cols = slice(head * group * DH, (head + 1) * group * DH)
        stores.append(pltpu.make_async_copy(dq_buf.at[:, cols], dq_hbm.at[:, cols], out_sem.at[head]))
        stores[-1].start()
    for store in stores:
        store.wait()


def in_hbm(x):
    return pltpu.with_memory_space_constraint(x, pltpu.HBM)


def call(kernel, operands, spaces, outs, out_spaces, scratch, limit, products):
    return list(pl.pallas_call(
        kernel,
        out_shape=[jax.ShapeDtypeStruct(*x) for x in outs],
        in_specs=[pl.BlockSpec(memory_space=x) for x in spaces],
        out_specs=[pl.BlockSpec(memory_space=x) for x in out_spaces],
        scratch_shapes=scratch,
        compiler_params=pltpu.CompilerParams(vmem_limit_bytes=limit * 1024 * 1024),
        cost_estimate=pl.CostEstimate(flops=products, bytes_accessed=products // 256, transcendentals=products // 512),
    )(*operands))


def local(queries, keys, values, beacon_keys, beacon_values, grad_out, ratios):
    bf16, f32 = jnp.bfloat16, jnp.float32
    hbm, vmem = pltpu.HBM, pltpu.VMEM
    spans = ratios.shape[0]
    rows, wide = keys.shape
    heads = wide // DH
    group = queries.shape[1] // wide
    chunks = heads * group // JOIN
    width = JOIN * rows
    last = spans - 1
    near, columns = 2 * rows, SLOTS * last
    swap = [(0, 1), (1, 0)]
    shifts = range(1, spans)
    order = sorted(shifts, key=lambda k: abs(2 * k - spans))

    def up(k):
        return [(i, (i + k) % spans) for i in range(spans)]

    left = lax.broadcasted_iota(jnp.int32, (beacon_keys.shape[0], 2 * wide), 1) < wide
    beacons = jnp.where(left, jnp.pad(beacon_keys, ((0, 0), (0, wide))), jnp.pad(beacon_values, ((0, 0), (wide, 0))))
    near_keys, near_values, beacons = lax.optimization_barrier((keys, values, beacons))
    own = {k: lax.ppermute(beacons, "ctx", up(k)) for k in reversed(order)}
    other_key, other_value = (lax.ppermute(x, "sub", swap) for x in (near_keys, near_values))

    product = queries.shape[1] * rows * 2

    def stats_of(size):
        return [((chunks, size, width), f32)] * 2 + [((chunks, 8, width), f32)] * 2

    q_in, g_in, far_mask, *near_stats = call(
        functools.partial(near_kernel, last, group),
        [ratios, in_hbm(queries), in_hbm(grad_out), in_hbm(keys), in_hbm(values), other_key, other_value],
        [pltpu.SMEM] + [hbm] * 4 + [vmem] * 2,
        [(queries.shape, bf16)] * 2 + [((columns, DH), bf16)] + stats_of(near),
        [vmem] * 7,
        [vmem(keys.shape, bf16)] * 2
        + [vmem((heads, near, 2 * DH), bf16), vmem((heads, near, DH), bf16)]
        + [pltpu.SemaphoreType.DMA((2 + 2 * heads,))],
        8,
        2 * product * near,
    )
    first = order[0]
    own[first], near_stats[2] = lax.optimization_barrier((own[first], near_stats[2]))
    other = {k: lax.ppermute(own[k], "sub", swap) for k in order}
    far = [x[k] for k in shifts for x in (own, other)]
    sets = [vmem((columns, width), f32)] * 2 + [vmem((columns, width), bf16)]
    share, delta, far_slopes, *grads, sent = call(
        functools.partial(far_kernel, last, group),
        [q_in, g_in, far_mask, *near_stats, *far],
        [vmem] * (7 + len(far)),
        [((chunks, 8, width), f32)] * 2
        + [((chunks, columns, width), bf16)]
        + [((HALF, 2 * wide), f32)] * last
        + [((HALF * last, 2 * wide), bf16)],
        [vmem] * (4 + last),
        [vmem((heads, columns, 2 * DH), bf16), vmem((heads, columns, DH), bf16)]
        + [vmem((columns, DH), f32)] * 2
        + sets * 2,
        16,
        4 * product * columns,
    )
    got = lax.ppermute(sent, "sub", swap)
    pairs = {k: grads[k - 1] + got[HALF * (k - 1) : HALF * k].astype(f32) for k in range(1, spans)}
    pairs = {k: x.astype(bf16) for k, x in pairs.items()}
    pairs, delta = lax.optimization_barrier((pairs, delta))
    sums = [lax.ppermute(pairs[k], "ctx", up(-k)) for k in order]
    near_slopes, near_grad, near_sent = call(
        functools.partial(near_gradients_kernel, group),
        [q_in, g_in, near_stats[0], near_stats[1], share, delta],
        [vmem] * 6,
        [((chunks, near, width), bf16), ((rows, 2 * wide), f32), ((rows, 2 * wide), bf16)],
        [vmem] * 3,
        [vmem((near, width), bf16)] * 2,
        8,
        product,
    )
    (grad_queries,) = call(
        functools.partial(query_gradients_kernel, group),
        [near_slopes, far_slopes, in_hbm(keys), other_key, *far],
        [vmem] * 2 + [hbm] + [vmem] * (1 + 2 * last),
        [(queries.shape, bf16)],
        [hbm],
        [
            vmem(keys.shape, bf16),
            vmem((heads, near + columns, DH), bf16),
            vmem((heads, DH, near + columns), bf16),
            vmem(queries.shape, bf16),
            pltpu.SemaphoreType.DMA,
            pltpu.SemaphoreType.DMA((heads,)),
        ],
        12,
        product,
    )
    near_total = (near_grad + lax.ppermute(near_sent, "sub", swap).astype(f32)).astype(bf16)
    near_outs = near_total[:, :wide], near_total[:, wide:]
    sums, grad_queries = lax.optimization_barrier((sums, grad_queries))
    beacon_total = functools.reduce(jnp.add, [x.astype(f32) for x in sums]).astype(bf16)
    return grad_queries, *near_outs, beacon_total[:, :wide], beacon_total[:, wide:]


def solution(mesh):
    rows = P(("grp", "ctx", "sub"), "tp")
    return jax.shard_map(
        local,
        mesh=mesh,
        in_specs=(rows,) * 6 + (P("grp"),),
        out_specs=(rows,) * 5,
        check_vma=False,
    )
```

profile of v0, /device:TPU:0, one launch (start us, length us, event | category | flops | bytes accessed | tf_op | source)
XLA Modules:
  0.0 43.3 jit_solution(12445984047714262124)
XLA Ops:
  0.6 0.9 %pad_select_fusion = bf16[64,1024]{1,0:T(8,128)(2,1)S(1)} fusion(bf16[64,512]{1,0:T(8,128)(2,1)} %param.11, bf16[64,512]{1,0:T(8,128)(2,1)} %param.10, pred[1024]{0:T(1024)(128)(4,1)S(1)} %iota_compare_fusion), kind=kLoop, calls=%fused_computation.5 | loop fusion | flops 65536 | bytes 263168 | tf_op jit(solution)/shard_map/jit(_where)/select_n | solution.py:393
  1.5 0.5 %collective-permute-start = (bf16[128,512]{1,0:T(8,128)(2,1)}, bf16[128,512]{1,0:T(8,128)(2,1)S(1)}, u32[]{:S(2)}, u32[]{:S(2)}) collective-permute-start(bf16[128,512]{1,0:T(8,128)(2,1)} %key_hbm.3), channel_id=1, source_target_pairs={{0,1},{1,0},{2,3},{3,2},{4,5},{5,4},{6,7},{7,6},{8,9},{9,8},{10,11... | collective-permute-start | bytes 393224 | tf_op jit(solution)/shard_map/ppermute | solution.py:396
  2.1 0.1 collective-permute-start.1
  2.1 4.0 %collective-permute-start.2 = (bf16[64,1024]{1,0:T(8,128)(2,1)S(1)}, bf16[64,1024]{1,0:T(8,128)(2,1)S(1)}, u32[]{:S(2)}, u32[]{:S(2)}) collective-permute-start(bf16[64,1024]{1,0:T(8,128)(2,1)S(1)} %pad_select_fusion), channel_id=1, source_target_pairs={{0,8},{4,12},{8,0},{12,4},{1,9},{5,13},{9,1},{13,5},{2,10},{6,14},... | collective-permute-start | bytes 393224 | tf_op jit(solution)/shard_map/ppermute | solution.py:395
  6.2 1.3 %collective-permute-start.6 = (bf16[64,1024]{1,0:T(8,128)(2,1)S(1)}, bf16[64,1024]{1,0:T(8,128)(2,1)S(1)}, u32[]{:S(2)}, u32[]{:S(2)}) collective-permute-start(bf16[64,1024]{1,0:T(8,128)(2,1)S(1)} %pad_select_fusion), channel_id=1, source_target_pairs={{0,12},{4,0},{8,4},{12,8},{1,13},{5,1},{9,5},{13,9},{2,14},{6,2},{... | collective-permute-start | bytes 393224 | tf_op jit(solution)/shard_map/ppermute | solution.py:395
  7.5 0.7 %collective-permute-start.3 = (bf16[64,1024]{1,0:T(8,128)(2,1)S(1)}, bf16[64,1024]{1,0:T(8,128)(2,1)S(1)}, u32[]{:S(2)}, u32[]{:S(2)}) collective-permute-start(bf16[64,1024]{1,0:T(8,128)(2,1)S(1)} %pad_select_fusion), channel_id=1, source_target_pairs={{0,4},{4,8},{8,12},{12,0},{1,5},{5,9},{9,13},{13,1},{2,6},{6,10},{... | collective-permute-start | bytes 393224 | tf_op jit(solution)/shard_map/ppermute | solution.py:395
  8.2 0.0 collective-permute-done.other_key
  8.2 0.0 collective-permute-done.1.other_value
  8.2 0.0 copy-start
  8.2 0.7 %copy-done = s32[4]{0:T(128)S(1)} copy-done((s32[4]{0:T(128)S(1)}, s32[4]{0:T(128)}, u32[]{:S(2)}) %copy-start) | copy-done | bytes 40
  8.8 4.3 %shard_map.110 = (bf16[128,4096]{1,0:T(8,128)(2,1)S(1)}, bf16[128,4096]{1,0:T(8,128)(2,1)S(1)}, bf16[384,128]{1,0:T(8,128)(2,1)S(1)}, f32[8,256,512]{2,1,0:T(8,1...) custom-call(s32[4]{0:T(128)S(1)} %copy-done, bf16[128,4096]{1,0:T(8,128)(2,1)} %q_hbm.1, ...), custom_call_target="tpu_custom_call" | custom-call | flops 536870912 | bytes 2097152 | tf_op jit(solution)/shard_map/pallas_call | solution.py:363
  13.1 0.4 %collective-permute-done.2.refs_2_ = bf16[64,1024]{1,0:T(8,128)(2,1)S(1)} collective-permute-done((bf16[64,1024]{1,0:T(8,128)(2,1)S(1)}, bf16[64,1024]{1,0:T(8,128)(2,1)S(1)}, u32[]{:S(2)}, u32[]{:S(2)}) %collective-permute-start.2) | collective-permute-done | bytes 131104 | tf_op jit(solution)/shard_map/ppermute | solution.py:395
  13.6 0.0 collective-permute-done.6.refs_4_
  13.6 0.0 collective-permute-start.7
  13.6 3.2 %collective-permute-done.3.refs_0_ = bf16[64,1024]{1,0:T(8,128)(2,1)S(1)} collective-permute-done((bf16[64,1024]{1,0:T(8,128)(2,1)S(1)}, bf16[64,1024]{1,0:T(8,128)(2,1)S(1)}, u32[]{:S(2)}, u32[]{:S(2)}) %collective-permute-start.3) | collective-permute-done | bytes 131104 | tf_op jit(solution)/shard_map/ppermute | solution.py:395
  16.7 0.0 collective-permute-start.4
  16.7 0.5 %collective-permute-start.5 = (bf16[64,1024]{1,0:T(8,128)(2,1)S(1)}, bf16[64,1024]{1,0:T(8,128)(2,1)S(1)}, u32[]{:S(2)}, u32[]{:S(2)}) collective-permute-start(bf16[64,1024]{1,0:T(8,128)(2,1)S(1)} %collective-permute-done.2.refs_2_), channel_id=1, source_target_pairs={{0,1},{1,0},{2,3},{3,2},{4,5},{5,4},{6,7},{7,6},{8,9},{9,8},{10,11... | collective-permute-start | bytes 393224 | tf_op jit(solution)/shard_map/ppermute | solution.py:417
  17.2 0.0 collective-permute-done.7.refs_5_
  17.2 0.8 %collective-permute-done.4.refs_1_ = bf16[64,1024]{1,0:T(8,128)(2,1)S(1)} collective-permute-done((bf16[64,1024]{1,0:T(8,128)(2,1)S(1)}, bf16[64,1024]{1,0:T(8,128)(2,1)S(1)}, u32[]{:S(2)}, u32[]{:S(2)}) %collective-permute-start.4) | collective-permute-done | bytes 131104 | tf_op jit(solution)/shard_map/ppermute | solution.py:417
  18.1 0.2 collective-permute-done.5.refs_3_
  18.3 6.5 %shard_map.111 = (f32[8,8,512]{2,1,0:T(8,128)S(1)}, f32[8,8,512]{2,1,0:T(8,128)S(1)}, bf16[8,384,512]{2,1,0:T(8,128)(2,1)S(1)}, f32[64,1024]{1,0:T(8,128)S(1)}, ...) custom-call(bf16[128,4096]{1,0:T(8,128)(2,1)S(1)} %get-tuple-element.37.q_buf, ...), custom_call_target="tpu_custom_call" | custom-call | flops 1610612736 | bytes 6291456 | tf_op jit(solution)/shard_map/pallas_call | solution.py:363
  24.8 0.4 collective-permute-start.8
  25.1 1.4 %collective-permute-done.8 = bf16[192,1024]{1,0:T(8,128)(2,1)S(1)} collective-permute-done((bf16[192,1024]{1,0:T(8,128)(2,1)S(1)}, bf16[192,1024]{1,0:T(8,128)(2,1)S(1)}, u32[]{:S(2)}, u32[]{:S(2)}) %collective-permute-start.8) | collective-permute-done | bytes 393248 | tf_op jit(solution)/shard_map/ppermute | solution.py:435
  26.5 0.1 add_convert_fusion.2
  26.6 4.3 %collective-permute-start.9 = (bf16[64,1024]{1,0:T(8,128)(2,1)S(1)}, bf16[64,1024]{1,0:T(8,128)(2,1)S(1)}, u32[]{:S(2)}, u32[]{:S(2)}) collective-permute-start(bf16[64,1024]{1,0:T(8,128)(2,1)S(1)} %get-tuple-element.52), channel_id=1, source_target_pairs={{0,8},{4,12},{8,0},{12,4},{1,9},{5,13},{9,1},{13,5},{2,10},{6,14},... | collective-permute-start | bytes 393224 | tf_op jit(solution)/shard_map/ppermute | solution.py:439
  31.0 0.6 %collective-permute-start.10 = (bf16[64,1024]{1,0:T(8,128)(2,1)S(1)}, bf16[64,1024]{1,0:T(8,128)(2,1)S(1)}, u32[]{:S(2)}, u32[]{:S(2)}) collective-permute-start(bf16[64,1024]{1,0:T(8,128)(2,1)S(1)} %get-tuple-element.53), channel_id=1, source_target_pairs={{0,12},{4,0},{8,4},{12,8},{1,13},{5,1},{9,5},{13,9},{2,14},{6,2},{... | collective-permute-start | bytes 393224 | tf_op jit(solution)/shard_map/ppermute | solution.py:439
  31.5 1.5 %collective-permute-start.11 = (bf16[64,1024]{1,0:T(8,128)(2,1)S(1)}, bf16[64,1024]{1,0:T(8,128)(2,1)S(1)}, u32[]{:S(2)}, u32[]{:S(2)}) collective-permute-start(bf16[64,1024]{1,0:T(8,128)(2,1)S(1)} %get-tuple-element.54), channel_id=1, source_target_pairs={{0,4},{4,8},{8,12},{12,0},{1,5},{5,9},{9,13},{13,1},{2,6},{6,10},{... | collective-permute-start | bytes 393224 | tf_op jit(solution)/shard_map/ppermute | solution.py:439
  33.0 1.5 %shard_map.112 = (bf16[8,256,512]{2,1,0:T(8,128)(2,1)S(1)}, f32[128,1024]{1,0:T(8,128)S(1)}, bf16[128,1024]{1,0:T(8,128)(2,1)S(1)}) custom-call(bf16[128,4096]{1,0:T(8,128)(2,1)S(1)} %get-tuple-element.37.q_buf, bf16[128,4096]{1,0:T(8,128)(2,1)S(1)} %get-tuple-element.38.g_buf, f32[8,256,512]{2,1,0:T(8,128)S(1)} %get-tuple-element.40.near_grown.grown, ...), custom_call_target="tpu_custom_call" | custom-call | flops 1048576 | bytes 4096 | tf_op jit(solution)/shard_map/pallas_call | solution.py:363
  34.5 0.1 collective-permute-start.12
  34.6 2.8 %shard_map.113 = bf16[128,4096]{1,0:T(8,128)(2,1)} custom-call(bf16[8,256,512]{2,1,0:T(8,128)(2,1)S(1)} %get-tuple-element.57.near_slopes, bf16[8,384,512]{2,1,0:T(8,128)(2,1)S(1)} %get-tuple-element.58.far_slopes, bf16[128,512]{1,0:T(8,128)(2,1)} %key_hbm.3, bf16[128,512]{1,0:T(8,128)(2,1)S(1)} %collective-permute-done.other_key, ...), custom_call_target="tpu_custom_call" | custom-call | flops 1048576 | bytes 4096 | tf_op jit(solution)/shard_map/pallas_call | solution.py:363
  37.5 1.3 %collective-permute-done.9 = bf16[64,1024]{1,0:T(8,128)(2,1)S(1)} collective-permute-done((bf16[64,1024]{1,0:T(8,128)(2,1)S(1)}, bf16[64,1024]{1,0:T(8,128)(2,1)S(1)}, u32[]{:S(2)}, u32[]{:S(2)}) %collective-permute-start.9) | collective-permute-done | bytes 131104 | tf_op jit(solution)/shard_map/ppermute | solution.py:439
  38.8 3.0 %collective-permute-done.10 = bf16[64,1024]{1,0:T(8,128)(2,1)S(1)} collective-permute-done((bf16[64,1024]{1,0:T(8,128)(2,1)S(1)}, bf16[64,1024]{1,0:T(8,128)(2,1)S(1)}, u32[]{:S(2)}, u32[]{:S(2)}) %collective-permute-start.10) | collective-permute-done | bytes 131104 | tf_op jit(solution)/shard_map/ppermute | solution.py:439
  41.8 0.0 collective-permute-done.11
  41.8 0.1 add_convert_fusion.1
  41.8 0.7 %fusion.1 = (bf16[64,512]{1,0:T(8,128)(2,1)}, bf16[64,512]{1,0:T(8,128)(2,1)}) fusion(bf16[64,1024]{1,0:T(8,128)(2,1)S(1)} %add_convert_fusion.1), kind=kLoop, calls=%fused_computation.8 | loop fusion | bytes 262144 | tf_op jit(solution)/shard_map/slice | solution.py:471
  42.5 0.0 collective-permute-done.12
  42.5 0.1 add_convert_fusion
  42.6 0.7 %fusion = (bf16[128,512]{1,0:T(8,128)(2,1)}, bf16[128,512]{1,0:T(8,128)(2,1)}) fusion(bf16[128,1024]{1,0:T(8,128)(2,1)S(1)} %add_convert_fusion), kind=kLoop, calls=%fused_computation.7 | loop fusion | bytes 524288 | tf_op jit(solution)/shard_map/slice | solution.py:468
  (1 shorter events, 0.0 us)
Async XLA Ops:
  1.5 6.6 %collective-permute-start = (bf16[128,512]{1,0:T(8,128)(2,1)}, bf16[128,512]{1,0:T(8,128)(2,1)S(1)}, u32[]{:S(2)}, u32[]{:S(2)}) collective-permute-start(bf16[128,512]{1,0:T(8,128)(2,1)} %key_hbm.3), channel_id=1, source_target_pairs={{0,1},{1,0},{2,3},{3,2},{4,5},{5,4},{6,7},{7,6},{8,9},{9,8},{10,11... | collective-permute-start | bytes 393224 | tf_op jit(solution)/shard_map/ppermute | solution.py:396
  2.1 6.1 %collective-permute-start.1 = (bf16[128,512]{1,0:T(8,128)(2,1)}, bf16[128,512]{1,0:T(8,128)(2,1)S(1)}, u32[]{:S(2)}, u32[]{:S(2)}) collective-permute-start(bf16[128,512]{1,0:T(8,128)(2,1)} %value_hbm.1), channel_id=1, source_target_pairs={{0,1},{1,0},{2,3},{3,2},{4,5},{5,4},{6,7},{7,6},{8,9},{9,8},{10,11... | collective-permute-start | bytes 393224 | tf_op jit(solution)/shard_map/ppermute | solution.py:396
  2.1 11.4 %collective-permute-start.2 = (bf16[64,1024]{1,0:T(8,128)(2,1)S(1)}, bf16[64,1024]{1,0:T(8,128)(2,1)S(1)}, u32[]{:S(2)}, u32[]{:S(2)}) collective-permute-start(bf16[64,1024]{1,0:T(8,128)(2,1)S(1)} %pad_select_fusion), channel_id=1, source_target_pairs={{0,8},{4,12},{8,0},{12,4},{1,9},{5,13},{9,1},{13,5},{2,10},{6,14},... | collective-permute-start | bytes 393224 | tf_op jit(solution)/shard_map/ppermute | solution.py:395
  6.2 7.4 %collective-permute-start.6 = (bf16[64,1024]{1,0:T(8,128)(2,1)S(1)}, bf16[64,1024]{1,0:T(8,128)(2,1)S(1)}, u32[]{:S(2)}, u32[]{:S(2)}) collective-permute-start(bf16[64,1024]{1,0:T(8,128)(2,1)S(1)} %pad_select_fusion), channel_id=1, source_target_pairs={{0,12},{4,0},{8,4},{12,8},{1,13},{5,1},{9,5},{13,9},{2,14},{6,2},{... | collective-permute-start | bytes 393224 | tf_op jit(solution)/shard_map/ppermute | solution.py:395
  7.5 9.2 %collective-permute-start.3 = (bf16[64,1024]{1,0:T(8,128)(2,1)S(1)}, bf16[64,1024]{1,0:T(8,128)(2,1)S(1)}, u32[]{:S(2)}, u32[]{:S(2)}) collective-permute-start(bf16[64,1024]{1,0:T(8,128)(2,1)S(1)} %pad_select_fusion), channel_id=1, source_target_pairs={{0,4},{4,8},{8,12},{12,0},{1,5},{5,9},{9,13},{13,1},{2,6},{6,10},{... | collective-permute-start | bytes 393224 | tf_op jit(solution)/shard_map/ppermute | solution.py:395
  8.2 0.7 %copy-start = (s32[4]{0:T(128)S(1)}, s32[4]{0:T(128)}, u32[]{:S(2)}) copy-start(s32[4]{0:T(128)} %ratios.1) | copy-start | bytes 52
  13.6 3.7 %collective-permute-start.7 = (bf16[64,1024]{1,0:T(8,128)(2,1)S(1)}, bf16[64,1024]{1,0:T(8,128)(2,1)S(1)}, u32[]{:S(2)}, u32[]{:S(2)}) collective-permute-start(bf16[64,1024]{1,0:T(8,128)(2,1)S(1)} %collective-permute-done.6.refs_4_), channel_id=1, source_target_pairs={{0,1},{1,0},{2,3},{3,2},{4,5},{5,4},{6,7},{7,6},{8,9},{9,8},{10,11... | collective-permute-start | bytes 393224 | tf_op jit(solution)/shard_map/ppermute | solution.py:417
  16.7 1.3 %collective-permute-start.4 = (bf16[64,1024]{1,0:T(8,128)(2,1)S(1)}, bf16[64,1024]{1,0:T(8,128)(2,1)S(1)}, u32[]{:S(2)}, u32[]{:S(2)}) collective-permute-start(bf16[64,1024]{1,0:T(8,128)(2,1)S(1)} %collective-permute-done.3.refs_0_), channel_id=1, source_target_pairs={{0,1},{1,0},{2,3},{3,2},{4,5},{5,4},{6,7},{7,6},{8,9},{9,8},{10,11... | collective-permute-start | bytes 393224 | tf_op jit(solution)/shard_map/ppermute | solution.py:417
  16.7 1.5 %collective-permute-start.5 = (bf16[64,1024]{1,0:T(8,128)(2,1)S(1)}, bf16[64,1024]{1,0:T(8,128)(2,1)S(1)}, u32[]{:S(2)}, u32[]{:S(2)}) collective-permute-start(bf16[64,1024]{1,0:T(8,128)(2,1)S(1)} %collective-permute-done.2.refs_2_), channel_id=1, source_target_pairs={{0,1},{1,0},{2,3},{3,2},{4,5},{5,4},{6,7},{7,6},{8,9},{9,8},{10,11... | collective-permute-start | bytes 393224 | tf_op jit(solution)/shard_map/ppermute | solution.py:417
  24.8 1.8 %collective-permute-start.8 = (bf16[192,1024]{1,0:T(8,128)(2,1)S(1)}, bf16[192,1024]{1,0:T(8,128)(2,1)S(1)}, u32[]{:S(2)}, u32[]{:S(2)}) collective-permute-start(bf16[192,1024]{1,0:T(8,128)(2,1)S(1)} %get-tuple-element.48), channel_id=1, source_target_pairs={{0,1},{1,0},{2,3},{3,2},{4,5},{5,4},{6,7},{7,6},{8,9},{9,8},{10,11... | collective-permute-start | bytes 1179656 | tf_op jit(solution)/shard_map/ppermute | solution.py:435
  26.6 12.2 %collective-permute-start.9 = (bf16[64,1024]{1,0:T(8,128)(2,1)S(1)}, bf16[64,1024]{1,0:T(8,128)(2,1)S(1)}, u32[]{:S(2)}, u32[]{:S(2)}) collective-permute-start(bf16[64,1024]{1,0:T(8,128)(2,1)S(1)} %get-tuple-element.52), channel_id=1, source_target_pairs={{0,8},{4,12},{8,0},{12,4},{1,9},{5,13},{9,1},{13,5},{2,10},{6,14},... | collective-permute-start | bytes 393224 | tf_op jit(solution)/shard_map/ppermute | solution.py:439
  31.0 10.8 %collective-permute-start.10 = (bf16[64,1024]{1,0:T(8,128)(2,1)S(1)}, bf16[64,1024]{1,0:T(8,128)(2,1)S(1)}, u32[]{:S(2)}, u32[]{:S(2)}) collective-permute-start(bf16[64,1024]{1,0:T(8,128)(2,1)S(1)} %get-tuple-element.53), channel_id=1, source_target_pairs={{0,12},{4,0},{8,4},{12,8},{1,13},{5,1},{9,5},{13,9},{2,14},{6,2},{... | collective-permute-start | bytes 393224 | tf_op jit(solution)/shard_map/ppermute | solution.py:439
  31.5 10.2 %collective-permute-start.11 = (bf16[64,1024]{1,0:T(8,128)(2,1)S(1)}, bf16[64,1024]{1,0:T(8,128)(2,1)S(1)}, u32[]{:S(2)}, u32[]{:S(2)}) collective-permute-start(bf16[64,1024]{1,0:T(8,128)(2,1)S(1)} %get-tuple-element.54), channel_id=1, source_target_pairs={{0,4},{4,8},{8,12},{12,0},{1,5},{5,9},{9,13},{13,1},{2,6},{6,10},{... | collective-permute-start | bytes 393224 | tf_op jit(solution)/shard_map/ppermute | solution.py:439
  34.5 8.0 %collective-permute-start.12 = (bf16[128,1024]{1,0:T(8,128)(2,1)S(1)}, bf16[128,1024]{1,0:T(8,128)(2,1)S(1)}, u32[]{:S(2)}, u32[]{:S(2)}) collective-permute-start(bf16[128,1024]{1,0:T(8,128)(2,1)S(1)} %get-tuple-element.61), channel_id=1, source_target_pairs={{0,1},{1,0},{2,3},{3,2},{4,5},{5,4},{6,7},{7,6},{8,9},{9,8},{10,11... | collective-permute-start | bytes 786440 | tf_op jit(solution)/shard_map/ppermute | solution.py:467
where the time goes:
time: 43.5 us; the launch traced here: 43.3 us
  Pallas kernels  15.1 us (35%)
  starting transfers between devices  14 us (32%)
  waiting for transfers between devices  10.3 us (24%)
  local copies, waits for them, and re-layouts  2.03 us (5%)
  other arithmetic  1.1 us (3%)
  between operations  0.71 us (2%)
    pallas_call x4, Pallas kernels, call(): pl.pallas_call(kernel, out_shape=[jax.ShapeDtypeStruct(*x) for x in outs]...  15.1 us
    ppermute x3, starting transfers between devices, local(): sums = [lax.ppermute(pairs[k], 'ctx', up(-k)) for k in order]  6.37 us
    ppermute x3, starting transfers between devices, local(): own = {k: lax.ppermute(beacons, 'ctx', up(k)) for k in reversed(order)}  6.04 us
    ppermute x3, waiting for transfers between devices, local(): sums = [lax.ppermute(pairs[k], 'ctx', up(-k)) for k in order]  4.31 us
    ppermute x3, waiting for transfers between devices, local(): own = {k: lax.ppermute(beacons, 'ctx', up(k)) for k in reversed(order)}  3.6 us
    ppermute x1, waiting for transfers between devices, local(): got = lax.ppermute(sent, 'sub', swap)  1.4 us
    ppermute x3, waiting for transfers between devices, local(): other = {k: lax.ppermute(own[k], 'sub', swap) for k in order}  1.02 us
    select_n x1, other arithmetic, local(): jnp.where(left, jnp.pad(beacon_keys, ((0, 0), (0, wide))), jnp.pad(beacon...  0.9 us
  transfers between devices with their start and end apart: 13, of which 7 were waited for; matrix products, arithmetic and copies ran while one was open for 2% of the time, Pallas kernels for 20%

commit v1 on v0

--- a/solution.py
+++ b/solution.py
@@ -170,20 +170,35 @@
         place(key_buf, value_buf, at, source.at[:, :wide], source.at[:, wide:], mask[at : at + HALF, :])
 
 
-def far_kernel(shifts, group, q_buf, g_buf, far_mask, near_grown, near_signal, near_top, near_total, *refs):
+def far_kernel(shifts, group, *refs):
+    here = lax.axis_index("ctx")
+    levels = sorted({shifts * i // 3 for i in range(4)} | set(range(min(shifts, 4))))
+    for low, level in zip([-1, *levels], levels):
+        pl.when((here > low) & (here <= level))(functools.partial(far_part, shifts, level, group, *refs))
+
+
+def far_part(shifts, seen, group, q_buf, g_buf, far_mask, near_grown, near_signal, near_top, near_total, *refs):
     far, refs = refs[: 2 * shifts], refs[2 * shifts :]
-    share_out, delta_out, slopes_out, own_outs, sent_out = refs[0], refs[1], refs[2], refs[3 : 3 + shifts], refs[3 + shifts]
-    refs = refs[4 + shifts :]
+    share_out, delta_out, slopes_out, own_outs, sent_outs = refs[0], refs[1], refs[2], refs[3 : 3 + shifts], refs[3 + shifts : 3 + 2 * shifts]
+    refs = refs[3 + 2 * shifts :]
     (key_buf, value_buf, dk_buf, dv_buf), sets = refs[:4], (refs[4:7], refs[7:10])
     rows = q_buf.shape[0]
-    heads, columns = key_buf.shape[:2]
+    heads = key_buf.shape[0]
+    columns = seen * SLOTS
     wide = heads * DH
     per_head = group // JOIN
     chunks = heads * per_head
     width = JOIN * rows
-    place_far(key_buf, value_buf, far, far_mask)
+    if seen:
+        place_far(key_buf, value_buf, far[: 2 * seen], far_mask)
+    for out in (*own_outs[seen:], *sent_outs[seen:]):
+        out[...] = jnp.zeros_like(out)
+    key_buf, value_buf = key_buf.at[:, :columns, :], value_buf.at[:, :columns, :]
+    sets = [[ref.at[:columns, :] for ref in refs] for refs in sets]
 
     def products(chunk):
+        if not seen:
+            return []
         score_ref, signal_ref, _ = sets[chunk % 2]
         return pair_products(key_buf, value_buf, q_buf, g_buf, chunk, chunk // per_head, score_ref, signal_ref)
 
@@ -236,13 +251,20 @@
 
         grown, signal = near_grown.at[chunk], near_signal.at[chunk]
         blocks = range(0, columns, BLOCK)
-        steps = [functools.partial(top, at) for at in blocks] + [end_top]
+
+        def clear():
+            if seen < shifts:
+                slope_ref[columns:, :] = jnp.zeros((SLOTS * (shifts - seen), width), jnp.bfloat16)
+
+        steps = [clear] + [functools.partial(top, at) for at in blocks] + [end_top]
         steps += [functools.partial(grow, at) for at in blocks] + [end_grow]
         steps += [functools.partial(weigh, score_ref, signal_ref, "far", at) for at in blocks]
         steps += [functools.partial(weigh, grown, signal, "near", at) for at in range(0, 2 * rows, BLOCK)] + [end_weigh]
         return steps + [functools.partial(slope, at) for at in blocks]
 
     def gradients(chunk):
+        if not seen:
+            return []
         weight_ref = sets[chunk % 2][2]
         head = chunk // per_head
         last = chunk % per_head == per_head - 1
@@ -254,19 +276,18 @@
                 part = jnp.dot(left(cols), joined(buf, chunk, start, 2), preferred_element_type=jnp.float32)
                 total = part if total is None else total + part
             if chunk % per_head:
-                total = total + total_ref[...]
+                total = total + total_ref[:columns, :]
             if not last:
-                total_ref[...] = total
+                total_ref[:columns, :] = total
                 return
             cols = slice(side * wide + head * DH, side * wide + (head + 1) * DH)
-            for shift, out in enumerate(own_outs):
+            for shift in range(seen):
                 at = shift * SLOTS
-                out[:, cols] = total[at : at + HALF] * factor
-                sent = total[at + HALF : at + SLOTS] * factor
-                sent_out[shift * HALF : (shift + 1) * HALF, cols] = sent.astype(sent_out.dtype)
+                own_outs[shift][:, cols] = total[at : at + HALF] * factor
+                sent_outs[shift][:, cols] = (total[at + HALF : at + SLOTS] * factor).astype(jnp.bfloat16)
 
         return [
-            functools.partial(collect, dk_buf, q_buf, lambda cols: slopes_out[chunk, :, cols], 0, SCALE),
+            functools.partial(collect, dk_buf, q_buf, lambda cols: slopes_out[chunk, :columns, cols], 0, SCALE),
             functools.partial(collect, dv_buf, g_buf, lambda cols: weight_ref[:, cols], 1, 1.0),
         ]
 
@@ -417,25 +438,28 @@
     other = {k: lax.ppermute(own[k], "sub", swap) for k in order}
     far = [x[k] for k in shifts for x in (own, other)]
     sets = [vmem((columns, width), f32)] * 2 + [vmem((columns, width), bf16)]
-    share, delta, far_slopes, *grads, sent = call(
+    share, delta, far_slopes, *grads = call(
         functools.partial(far_kernel, last, group),
         [q_in, g_in, far_mask, *near_stats, *far],
         [vmem] * (7 + len(far)),
         [((chunks, 8, width), f32)] * 2
         + [((chunks, columns, width), bf16)]
         + [((HALF, 2 * wide), f32)] * last
-        + [((HALF * last, 2 * wide), bf16)],
-        [vmem] * (4 + last),
+        + [((HALF, 2 * wide), bf16)] * last,
+        [vmem] * (3 + 2 * last),
         [vmem((heads, columns, 2 * DH), bf16), vmem((heads, columns, DH), bf16)]
         + [vmem((columns, DH), f32)] * 2
         + sets * 2,
-        16,
+        12 + 30 * columns * width // 2**20,
         4 * product * columns,
     )
-    got = lax.ppermute(sent, "sub", swap)
-    pairs = {k: grads[k - 1] + got[HALF * (k - 1) : HALF * k].astype(f32) for k in range(1, spans)}
-    pairs = {k: x.astype(bf16) for k, x in pairs.items()}
-    pairs, delta = lax.optimization_barrier((pairs, delta))
+    sent = dict(zip(shifts, grads[last:]))
+
+    def pair(k):
+        return (grads[k - 1] + lax.ppermute(sent[k], "sub", swap).astype(f32)).astype(bf16)
+
+    pairs = {k: pair(k) for k in order}
+    pairs[order[-1]], delta = lax.optimization_barrier((pairs[order[-1]], delta))
     sums = [lax.ppermute(pairs[k], "ctx", up(-k)) for k in order]
     near_slopes, near_grad, near_sent = call(
         functools.partial(near_gradients_kernel, group),
@@ -465,10 +489,10 @@
         product,
     )
     near_total = (near_grad + lax.ppermute(near_sent, "sub", swap).astype(f32)).astype(bf16)
-    near_outs = near_total[:, :wide], near_total[:, wide:]
     sums, grad_queries = lax.optimization_barrier((sums, grad_queries))
     beacon_total = functools.reduce(jnp.add, [x.astype(f32) for x in sums]).astype(bf16)
-    return grad_queries, *near_outs, beacon_total[:, :wide], beacon_total[:, wide:]
+    outs = [x for y in (near_total, beacon_total) for x in (y[:, :wide], y[:, wide:])]
+    return (grad_queries, *outs)
 
 
 def solution(mesh):

time: 43.5 us -> 42.1 us (0.968)
  Pallas kernels: 15.1 us -> 9.87 us
  starting transfers between devices: 14 us -> 18.8 us
  waiting for transfers between devices: 10.3 us -> 9.32 us
    pallas_call x4, Pallas kernels: 15.1 us -> 9.87 us  [call(): pl.pallas_call(kernel, out_shape=[jax.ShapeDtypeStruct(*x) for x in outs]...]
    ppermute x3, starting transfers between devices: 6.37 us -> 10.7 us  [local(): sums = [lax.ppermute(pairs[k], 'ctx', up(-k)) for k in order]]
    ppermute x1 -> x3, waiting for transfers between devices: 1.4 us -> 0.52 us  [pair(): lax.ppermute(sent[k], 'sub', swap).astype(f32)]
    ppermute x1 -> x3, starting transfers between devices: 0.39 us -> 0.9 us  [pair(): lax.ppermute(sent[k], 'sub', swap).astype(f32)]
  transfers between devices with their start and end apart: 13 -> 15, of which waited for: 7 -> 7; matrix products, arithmetic and copies ran while one was open for 2% -> 2% of each run, Pallas kernels for 20% -> 21%
where the time goes in v1:
time: 42.1 us; the launch traced here: 41.9 us
  starting transfers between devices  18.8 us (45%)
  Pallas kernels  9.87 us (23%)
  waiting for transfers between devices  9.32 us (22%)
  local copies, waits for them, and re-layouts  2.03 us (5%)
  other arithmetic  1.09 us (3%)
  between operations  0.72 us (2%)
    ppermute x3, starting transfers between devices, local(): sums = [lax.ppermute(pairs[k], 'ctx', up(-k)) for k in order]  10.7 us
    pallas_call x4, Pallas kernels, call(): pl.pallas_call(kernel, out_shape=[jax.ShapeDtypeStruct(*x) for x in outs]...  9.87 us
    ppermute x3, starting transfers between devices, local(): own = {k: lax.ppermute(beacons, 'ctx', up(k)) for k in reversed(order)}  6.04 us
    ppermute x3, waiting for transfers between devices, local(): sums = [lax.ppermute(pairs[k], 'ctx', up(-k)) for k in order]  4.17 us
    ppermute x3, waiting for transfers between devices, local(): own = {k: lax.ppermute(beacons, 'ctx', up(k)) for k in reversed(order)}  3.6 us
    slice x2, local copies, waits for them, and re-layouts, local(): y[:, wide:]  1.38 us
    ppermute x3, waiting for transfers between devices, local(): other = {k: lax.ppermute(own[k], 'sub', swap) for k in order}  1.02 us
    select_n x1, other arithmetic, local(): jnp.where(left, jnp.pad(beacon_keys, ((0, 0), (0, wide))), jnp.pad(beacon...  0.9 us
  transfers between devices with their start and end apart: 15, of which 7 were waited for; matrix products, arithmetic and copies ran while one was open for 2% of the time, Pallas kernels for 21%

profile of v1, /device:TPU:0, one launch (start us, length us, event | category | flops | bytes accessed | tf_op | source)
XLA Modules:
  0.0 41.9 jit_solution(11149296384250175986)
XLA Ops:
  0.6 0.9 %pad_select_fusion = bf16[64,1024]{1,0:T(8,128)(2,1)S(1)} fusion(bf16[64,512]{1,0:T(8,128)(2,1)} %param.11, bf16[64,512]{1,0:T(8,128)(2,1)} %param.10, pred[1024]{0:T(1024)(128)(4,1)S(1)} %iota_compare_fusion), kind=kLoop, calls=%fused_computation.5 | loop fusion | flops 65536 | bytes 263168 | tf_op jit(solution)/shard_map/jit(_where)/select_n | solution.py:414
  1.5 0.5 %collective-permute-start = (bf16[128,512]{1,0:T(8,128)(2,1)}, bf16[128,512]{1,0:T(8,128)(2,1)S(1)}, u32[]{:S(2)}, u32[]{:S(2)}) collective-permute-start(bf16[128,512]{1,0:T(8,128)(2,1)} %key_hbm.3), channel_id=1, source_target_pairs={{0,1},{1,0},{2,3},{3,2},{4,5},{5,4},{6,7},{7,6},{8,9},{9,8},{10,11... | collective-permute-start | bytes 393224 | tf_op jit(solution)/shard_map/ppermute | solution.py:417
  2.1 0.1 collective-permute-start.1
  2.1 4.0 %collective-permute-start.2 = (bf16[64,1024]{1,0:T(8,128)(2,1)S(1)}, bf16[64,1024]{1,0:T(8,128)(2,1)S(1)}, u32[]{:S(2)}, u32[]{:S(2)}) collective-permute-start(bf16[64,1024]{1,0:T(8,128)(2,1)S(1)} %pad_select_fusion), channel_id=1, source_target_pairs={{0,8},{4,12},{8,0},{12,4},{1,9},{5,13},{9,1},{13,5},{2,10},{6,14},... | collective-permute-start | bytes 393224 | tf_op jit(solution)/shard_map/ppermute | solution.py:416
  6.2 1.3 %collective-permute-start.6 = (bf16[64,1024]{1,0:T(8,128)(2,1)S(1)}, bf16[64,1024]{1,0:T(8,128)(2,1)S(1)}, u32[]{:S(2)}, u32[]{:S(2)}) collective-permute-start(bf16[64,1024]{1,0:T(8,128)(2,1)S(1)} %pad_select_fusion), channel_id=1, source_target_pairs={{0,12},{4,0},{8,4},{12,8},{1,13},{5,1},{9,5},{13,9},{2,14},{6,2},{... | collective-permute-start | bytes 393224 | tf_op jit(solution)/shard_map/ppermute | solution.py:416
  7.5 0.7 %collective-permute-start.3 = (bf16[64,1024]{1,0:T(8,128)(2,1)S(1)}, bf16[64,1024]{1,0:T(8,128)(2,1)S(1)}, u32[]{:S(2)}, u32[]{:S(2)}) collective-permute-start(bf16[64,1024]{1,0:T(8,128)(2,1)S(1)} %pad_select_fusion), channel_id=1, source_target_pairs={{0,4},{4,8},{8,12},{12,0},{1,5},{5,9},{9,13},{13,1},{2,6},{6,10},{... | collective-permute-start | bytes 393224 | tf_op jit(solution)/shard_map/ppermute | solution.py:416
  8.2 0.0 collective-permute-done.other_key
  8.2 0.0 collective-permute-done.1.other_value
  8.2 0.0 copy-start
  8.2 0.7 %copy-done = s32[4]{0:T(128)S(1)} copy-done((s32[4]{0:T(128)S(1)}, s32[4]{0:T(128)}, u32[]{:S(2)}) %copy-start) | copy-done | bytes 40
  8.8 4.3 %shard_map.110 = (bf16[128,4096]{1,0:T(8,128)(2,1)S(1)}, bf16[128,4096]{1,0:T(8,128)(2,1)S(1)}, bf16[384,128]{1,0:T(8,128)(2,1)S(1)}, f32[8,256,512]{2,1,0:T(8,1...) custom-call(s32[4]{0:T(128)S(1)} %copy-done, bf16[128,4096]{1,0:T(8,128)(2,1)} %q_hbm.1, ...), custom_call_target="tpu_custom_call" | custom-call | flops 536870912 | bytes 2097152 | tf_op jit(solution)/shard_map/pallas_call | solution.py:384
  13.1 0.4 %collective-permute-done.2.refs_9_.refs_2_ = bf16[64,1024]{1,0:T(8,128)(2,1)S(1)} collective-permute-done((bf16[64,1024]{1,0:T(8,128)(2,1)S(1)}, bf16[64,1024]{1,0:T(8,128)(2,1)S(1)}, u32[]{:S(2)}, u32[]{:S(2)}) %collective-permute-start.2) | collective-permute-done | bytes 131104 | tf_op jit(solution)/shard_map/ppermute | solution.py:416
  13.6 0.0 collective-permute-done.6.refs_11_.refs_4_
  13.6 0.0 collective-permute-start.7
  13.6 3.2 %collective-permute-done.3.refs_7_.refs_0_ = bf16[64,1024]{1,0:T(8,128)(2,1)S(1)} collective-permute-done((bf16[64,1024]{1,0:T(8,128)(2,1)S(1)}, bf16[64,1024]{1,0:T(8,128)(2,1)S(1)}, u32[]{:S(2)}, u32[]{:S(2)}) %collective-permute-start.3) | collective-permute-done | bytes 131104 | tf_op jit(solution)/shard_map/ppermute | solution.py:416
  16.7 0.0 collective-permute-start.4
  16.7 0.5 %collective-permute-start.5 = (bf16[64,1024]{1,0:T(8,128)(2,1)S(1)}, bf16[64,1024]{1,0:T(8,128)(2,1)S(1)}, u32[]{:S(2)}, u32[]{:S(2)}) collective-permute-start(bf16[64,1024]{1,0:T(8,128)(2,1)S(1)} %collective-permute-done.2.refs_9_.refs_2_), channel_id=1, source_target_pairs={{0,1},{1,0},{2,3},{3,2},{4,5},{5,4},{6,7},{7,6},{8,9},{9,8},{10,11... | collective-permute-start | bytes 393224 | tf_op jit(solution)/shard_map/ppermute | solution.py:438
  17.2 0.0 collective-permute-done.7.refs_12_.refs_5_
  17.2 0.8 %collective-permute-done.4.refs_8_.refs_1_ = bf16[64,1024]{1,0:T(8,128)(2,1)S(1)} collective-permute-done((bf16[64,1024]{1,0:T(8,128)(2,1)S(1)}, bf16[64,1024]{1,0:T(8,128)(2,1)S(1)}, u32[]{:S(2)}, u32[]{:S(2)}) %collective-permute-start.4) | collective-permute-done | bytes 131104 | tf_op jit(solution)/shard_map/ppermute | solution.py:438
  18.1 0.2 collective-permute-done.5.refs_10_.refs_3_
  18.3 1.2 %shard_map.111 = (f32[8,8,512]{2,1,0:T(8,128)S(1)}, f32[8,8,512]{2,1,0:T(8,128)S(1)}, bf16[8,384,512]{2,1,0:T(8,128)(2,1)S(1)}, f32[64,1024]{1,0:T(8,128)S(1)}, ...) custom-call(bf16[128,4096]{1,0:T(8,128)(2,1)S(1)} %get-tuple-element, ...), custom_call_target="tpu_custom_call" | custom-call | flops 1610612736 | bytes 6291456 | tf_op jit(solution)/shard_map/pallas_call | solution.py:384
  19.5 0.4 collective-permute-start.8
  19.9 0.2 collective-permute-start.10
  20.1 0.3 collective-permute-start.12
  20.4 0.5 %collective-permute-done.8 = bf16[64,1024]{1,0:T(8,128)(2,1)S(1)} collective-permute-done((bf16[64,1024]{1,0:T(8,128)(2,1)S(1)}, bf16[64,1024]{1,0:T(8,128)(2,1)S(1)}, u32[]{:S(2)}, u32[]{:S(2)}) %collective-permute-start.8) | collective-permute-done | bytes 131104 | tf_op jit(solution)/shard_map/ppermute | solution.py:459
  20.9 8.4 %collective-permute-start.9 = (bf16[64,1024]{1,0:T(8,128)(2,1)S(1)}, bf16[64,1024]{1,0:T(8,128)(2,1)S(1)}, u32[]{:S(2)}, u32[]{:S(2)}) collective-permute-start(bf16[64,1024]{1,0:T(8,128)(2,1)S(1)} %add_convert_fusion.4), channel_id=1, source_target_pairs={{0,8},{4,12},{8,0},{12,4},{1,9},{5,13},{9,1},{13,5},{2,10},{6,14},... | collective-permute-start | bytes 393224 | tf_op jit(solution)/shard_map/ppermute | solution.py:463
  29.3 0.0 collective-permute-done.10
  29.3 0.2 collective-permute-start.11
  29.5 0.0 collective-permute-done.12
  29.5 2.2 %collective-permute-start.13 = (bf16[64,1024]{1,0:T(8,128)(2,1)S(1)}, bf16[64,1024]{1,0:T(8,128)(2,1)S(1)}, u32[]{:S(2)}, u32[]{:S(2)}) collective-permute-start(bf16[64,1024]{1,0:T(8,128)(2,1)S(1)} %add_convert_fusion.2), channel_id=1, source_target_pairs={{0,4},{4,8},{8,12},{12,0},{1,5},{5,9},{9,13},{13,1},{2,6},{6,10},{... | collective-permute-start | bytes 393224 | tf_op jit(solution)/shard_map/ppermute | solution.py:463
  31.7 1.5 %shard_map.112 = (bf16[8,256,512]{2,1,0:T(8,128)(2,1)S(1)}, f32[128,1024]{1,0:T(8,128)S(1)}, bf16[128,1024]{1,0:T(8,128)(2,1)S(1)}) custom-call(bf16[128,4096]{1,0:T(8,128)(2,1)S(1)} %get-tuple-element.37.refs_0_.q_buf, bf16[128,4096]{1,0:T(8,128)(2,1)S(1)} %get-tuple-element.38.refs_1_.g_buf, f32[8,256,512]{2,1,0:T(8,128)S(1)} %get-tuple-element.40.refs_3_.grown, ...), custom_call_target="tpu_custom_call" | custom-call | flops 1048576 | bytes 4096 | tf_op jit(solution)/shard_map/pallas_call | solution.py:384
  33.3 0.1 collective-permute-start.14
  33.3 2.8 %shard_map.113 = bf16[128,4096]{1,0:T(8,128)(2,1)} custom-call(bf16[8,256,512]{2,1,0:T(8,128)(2,1)S(1)} %get-tuple-element.57.near_slopes, bf16[8,384,512]{2,1,0:T(8,128)(2,1)S(1)} %get-tuple-element.58.far_slopes, bf16[128,512]{1,0:T(8,128)(2,1)} %key_hbm.3, bf16[128,512]{1,0:T(8,128)(2,1)S(1)} %collective-permute-done.other_key, ...), custom_call_target="tpu_custom_call" | custom-call | flops 1048576 | bytes 4096 | tf_op jit(solution)/shard_map/pallas_call | solution.py:384
  36.2 0.3 collective-permute-done.9
  36.5 3.9 %collective-permute-done.11 = bf16[64,1024]{1,0:T(8,128)(2,1)S(1)} collective-permute-done((bf16[64,1024]{1,0:T(8,128)(2,1)S(1)}, bf16[64,1024]{1,0:T(8,128)(2,1)S(1)}, u32[]{:S(2)}, u32[]{:S(2)}) %collective-permute-start.11) | collective-permute-done | bytes 131104 | tf_op jit(solution)/shard_map/ppermute | solution.py:463
  40.4 0.0 collective-permute-done.13
  40.4 0.1 add_convert_fusion.1
  40.4 0.7 %fusion.1 = (bf16[64,512]{1,0:T(8,128)(2,1)}, bf16[64,512]{1,0:T(8,128)(2,1)}) fusion(bf16[64,1024]{1,0:T(8,128)(2,1)S(1)} %add_convert_fusion.1), kind=kLoop, calls=%fused_computation.8 | loop fusion | bytes 262144 | tf_op jit(solution)/shard_map/slice | solution.py:494
  41.1 0.0 collective-permute-done.14
  41.1 0.1 add_convert_fusion
  41.1 0.7 %fusion = (bf16[128,512]{1,0:T(8,128)(2,1)}, bf16[128,512]{1,0:T(8,128)(2,1)}) fusion(bf16[128,1024]{1,0:T(8,128)(2,1)S(1)} %add_convert_fusion), kind=kLoop, calls=%fused_computation.7 | loop fusion | bytes 524288 | tf_op jit(solution)/shard_map/slice | solution.py:494
  (4 shorter events, 0.1 us)
Async XLA Ops:
  1.5 6.6 %collective-permute-start = (bf16[128,512]{1,0:T(8,128)(2,1)}, bf16[128,512]{1,0:T(8,128)(2,1)S(1)}, u32[]{:S(2)}, u32[]{:S(2)}) collective-permute-start(bf16[128,512]{1,0:T(8,128)(2,1)} %key_hbm.3), channel_id=1, source_target_pairs={{0,1},{1,0},{2,3},{3,2},{4,5},{5,4},{6,7},{7,6},{8,9},{9,8},{10,11... | collective-permute-start | bytes 393224 | tf_op jit(solution)/shard_map/ppermute | solution.py:417
  2.1 6.1 %collective-permute-start.1 = (bf16[128,512]{1,0:T(8,128)(2,1)}, bf16[128,512]{1,0:T(8,128)(2,1)S(1)}, u32[]{:S(2)}, u32[]{:S(2)}) collective-permute-start(bf16[128,512]{1,0:T(8,128)(2,1)} %value_hbm.1), channel_id=1, source_target_pairs={{0,1},{1,0},{2,3},{3,2},{4,5},{5,4},{6,7},{7,6},{8,9},{9,8},{10,11... | collective-permute-start | bytes 393224 | tf_op jit(solution)/shard_map/ppermute | solution.py:417
  2.1 11.4 %collective-permute-start.2 = (bf16[64,1024]{1,0:T(8,128)(2,1)S(1)}, bf16[64,1024]{1,0:T(8,128)(2,1)S(1)}, u32[]{:S(2)}, u32[]{:S(2)}) collective-permute-start(bf16[64,1024]{1,0:T(8,128)(2,1)S(1)} %pad_select_fusion), channel_id=1, source_target_pairs={{0,8},{4,12},{8,0},{12,4},{1,9},{5,13},{9,1},{13,5},{2,10},{6,14},... | collective-permute-start | bytes 393224 | tf_op jit(solution)/shard_map/ppermute | solution.py:416
  6.2 7.4 %collective-permute-start.6 = (bf16[64,1024]{1,0:T(8,128)(2,1)S(1)}, bf16[64,1024]{1,0:T(8,128)(2,1)S(1)}, u32[]{:S(2)}, u32[]{:S(2)}) collective-permute-start(bf16[64,1024]{1,0:T(8,128)(2,1)S(1)} %pad_select_fusion), channel_id=1, source_target_pairs={{0,12},{4,0},{8,4},{12,8},{1,13},{5,1},{9,5},{13,9},{2,14},{6,2},{... | collective-permute-start | bytes 393224 | tf_op jit(solution)/shard_map/ppermute | solution.py:416
  7.5 9.2 %collective-permute-start.3 = (bf16[64,1024]{1,0:T(8,128)(2,1)S(1)}, bf16[64,1024]{1,0:T(8,128)(2,1)S(1)}, u32[]{:S(2)}, u32[]{:S(2)}) collective-permute-start(bf16[64,1024]{1,0:T(8,128)(2,1)S(1)} %pad_select_fusion), channel_id=1, source_target_pairs={{0,4},{4,8},{8,12},{12,0},{1,5},{5,9},{9,13},{13,1},{2,6},{6,10},{... | collective-permute-start | bytes 393224 | tf_op jit(solution)/shard_map/ppermute | solution.py:416
  8.2 0.7 %copy-start = (s32[4]{0:T(128)S(1)}, s32[4]{0:T(128)}, u32[]{:S(2)}) copy-start(s32[4]{0:T(128)} %ratios.1) | copy-start | bytes 52
  13.6 3.7 %collective-permute-start.7 = (bf16[64,1024]{1,0:T(8,128)(2,1)S(1)}, bf16[64,1024]{1,0:T(8,128)(2,1)S(1)}, u32[]{:S(2)}, u32[]{:S(2)}) collective-permute-start(bf16[64,1024]{1,0:T(8,128)(2,1)S(1)} %collective-permute-done.6.refs_11_.refs_4_), channel_id=1, source_target_pairs={{0,1},{1,0},{2,3},{3,2},{4,5},{5,4},{6,7},{7,6},{8,9},{9,8},{10,11... | collective-permute-start | bytes 393224 | tf_op jit(solution)/shard_map/ppermute | solution.py:438
  16.7 1.3 %collective-permute-start.4 = (bf16[64,1024]{1,0:T(8,128)(2,1)S(1)}, bf16[64,1024]{1,0:T(8,128)(2,1)S(1)}, u32[]{:S(2)}, u32[]{:S(2)}) collective-permute-start(bf16[64,1024]{1,0:T(8,128)(2,1)S(1)} %collective-permute-done.3.refs_7_.refs_0_), channel_id=1, source_target_pairs={{0,1},{1,0},{2,3},{3,2},{4,5},{5,4},{6,7},{7,6},{8,9},{9,8},{10,11... | collective-permute-start | bytes 393224 | tf_op jit(solution)/shard_map/ppermute | solution.py:438
  16.7 1.5 %collective-permute-start.5 = (bf16[64,1024]{1,0:T(8,128)(2,1)S(1)}, bf16[64,1024]{1,0:T(8,128)(2,1)S(1)}, u32[]{:S(2)}, u32[]{:S(2)}) collective-permute-start(bf16[64,1024]{1,0:T(8,128)(2,1)S(1)} %collective-permute-done.2.refs_9_.refs_2_), channel_id=1, source_target_pairs={{0,1},{1,0},{2,3},{3,2},{4,5},{5,4},{6,7},{7,6},{8,9},{9,8},{10,11... | collective-permute-start | bytes 393224 | tf_op jit(solution)/shard_map/ppermute | solution.py:438
  19.5 1.4 %collective-permute-start.8 = (bf16[64,1024]{1,0:T(8,128)(2,1)S(1)}, bf16[64,1024]{1,0:T(8,128)(2,1)S(1)}, u32[]{:S(2)}, u32[]{:S(2)}) collective-permute-start(bf16[64,1024]{1,0:T(8,128)(2,1)S(1)} %get-tuple-element.48), channel_id=1, source_target_pairs={{0,1},{1,0},{2,3},{3,2},{4,5},{5,4},{6,7},{7,6},{8,9},{9,8},{10,11... | collective-permute-start | bytes 393224 | tf_op jit(solution)/shard_map/ppermute | solution.py:459
  19.9 9.4 %collective-permute-start.10 = (bf16[64,1024]{1,0:T(8,128)(2,1)S(1)}, bf16[64,1024]{1,0:T(8,128)(2,1)S(1)}, u32[]{:S(2)}, u32[]{:S(2)}) collective-permute-start(bf16[64,1024]{1,0:T(8,128)(2,1)S(1)} %get-tuple-element.50), channel_id=1, source_target_pairs={{0,1},{1,0},{2,3},{3,2},{4,5},{5,4},{6,7},{7,6},{8,9},{9,8},{10,11... | collective-permute-start | bytes 393224 | tf_op jit(solution)/shard_map/ppermute | solution.py:459
  20.1 9.4 %collective-permute-start.12 = (bf16[64,1024]{1,0:T(8,128)(2,1)S(1)}, bf16[64,1024]{1,0:T(8,128)(2,1)S(1)}, u32[]{:S(2)}, u32[]{:S(2)}) collective-permute-start(bf16[64,1024]{1,0:T(8,128)(2,1)S(1)} %get-tuple-element.52), channel_id=1, source_target_pairs={{0,1},{1,0},{2,3},{3,2},{4,5},{5,4},{6,7},{7,6},{8,9},{9,8},{10,11... | collective-permute-start | bytes 393224 | tf_op jit(solution)/shard_map/ppermute | solution.py:459
  20.9 15.5 %collective-permute-start.9 = (bf16[64,1024]{1,0:T(8,128)(2,1)S(1)}, bf16[64,1024]{1,0:T(8,128)(2,1)S(1)}, u32[]{:S(2)}, u32[]{:S(2)}) collective-permute-start(bf16[64,1024]{1,0:T(8,128)(2,1)S(1)} %add_convert_fusion.4), channel_id=1, source_target_pairs={{0,8},{4,12},{8,0},{12,4},{1,9},{5,13},{9,1},{13,5},{2,10},{6,14},... | collective-permute-start | bytes 393224 | tf_op jit(solution)/shard_map/ppermute | solution.py:463
  29.3 11.0 %collective-permute-start.11 = (bf16[64,1024]{1,0:T(8,128)(2,1)S(1)}, bf16[64,1024]{1,0:T(8,128)(2,1)S(1)}, u32[]{:S(2)}, u32[]{:S(2)}) collective-permute-start(bf16[64,1024]{1,0:T(8,128)(2,1)S(1)} %add_convert_fusion.3), channel_id=1, source_target_pairs={{0,12},{4,0},{8,4},{12,8},{1,13},{5,1},{9,5},{13,9},{2,14},{6,2},{... | collective-permute-start | bytes 393224 | tf_op jit(solution)/shard_map/ppermute | solution.py:463
  29.5 10.8 %collective-permute-start.13 = (bf16[64,1024]{1,0:T(8,128)(2,1)S(1)}, bf16[64,1024]{1,0:T(8,128)(2,1)S(1)}, u32[]{:S(2)}, u32[]{:S(2)}) collective-permute-start(bf16[64,1024]{1,0:T(8,128)(2,1)S(1)} %add_convert_fusion.2), channel_id=1, source_target_pairs={{0,4},{4,8},{8,12},{12,0},{1,5},{5,9},{9,13},{13,1},{2,6},{6,10},{... | collective-permute-start | bytes 393224 | tf_op jit(solution)/shard_map/ppermute | solution.py:463
  33.3 7.8 %collective-permute-start.14 = (bf16[128,1024]{1,0:T(8,128)(2,1)S(1)}, bf16[128,1024]{1,0:T(8,128)(2,1)S(1)}, u32[]{:S(2)}, u32[]{:S(2)}) collective-permute-start(bf16[128,1024]{1,0:T(8,128)(2,1)S(1)} %get-tuple-element.61), channel_id=1, source_target_pairs={{0,1},{1,0},{2,3},{3,2},{4,5},{5,4},{6,7},{7,6},{8,9},{9,8},{10,11... | collective-permute-start | bytes 786440 | tf_op jit(solution)/shard_map/ppermute | solution.py:491

commit v2 on v1

--- a/solution.py
+++ b/solution.py
@@ -114,6 +114,10 @@
 
     blocks = range(0, columns, BLOCK)
     return [functools.partial(top, at) for at in blocks] + [end_top] + [functools.partial(grow, at) for at in blocks] + [end_grow]
+
+
+def piece_of(shifts, shift, side):
+    return side * (shifts - 1) + shift if shift < shifts - 1 else 2 * (shifts - 1) + side
 
 
 def near_kernel(
@@ -140,7 +144,7 @@
         owner = jnp.maximum(here - 1 - shift, 0)
         live = jnp.where(here > shift, SPAN // ratios[owner], 0)
         for side, first in enumerate((sub * HALF, (1 - sub) * HALF)):
-            at = (2 * shift + side) * HALF
+            at = piece_of(shifts, shift, side) * HALF
             mask_out[at : at + HALF, :] = mask_of(slot_at < live - first)
     loads[0].wait()
     loads[1].wait()
@@ -170,34 +174,58 @@
         place(key_buf, value_buf, at, source.at[:, :wide], source.at[:, wide:], mask[at : at + HALF, :])
 
 
+def middle_kernel(group, q_buf, g_buf, far_mask, *refs):
+    far, (grown_out, signal_out, top_out, total_out, key_buf, value_buf) = refs[:-6], refs[-6:]
+    heads = key_buf.shape[0]
+    per_head = group // JOIN
+    place_far(key_buf, value_buf, far, far_mask)
+
+    def products(chunk):
+        return pair_products(
+            key_buf, value_buf, q_buf, g_buf, chunk, chunk // per_head, grown_out.at[chunk], signal_out.at[chunk]
+        )
+
+    pipeline(
+        heads * per_head,
+        products,
+        lambda chunk: exponentials(chunk, grown_out, top_out, total_out),
+        lambda chunk: [],
+    )
+
+
 def far_kernel(shifts, group, *refs):
     here = lax.axis_index("ctx")
-    levels = sorted({shifts * i // 3 for i in range(4)} | set(range(min(shifts, 4))))
+    levels = sorted({0, shifts - 1, shifts})
     for low, level in zip([-1, *levels], levels):
         pl.when((here > low) & (here <= level))(functools.partial(far_part, shifts, level, group, *refs))
 
 
-def far_part(shifts, seen, group, q_buf, g_buf, far_mask, near_grown, near_signal, near_top, near_total, *refs):
-    far, refs = refs[: 2 * shifts], refs[2 * shifts :]
+def far_part(shifts, seen, group, q_buf, g_buf, far_mask, *refs):
+    groups, refs = [refs[4 * i : 4 * i + 4] for i in range(min(shifts, 2))], refs[4 * min(shifts, 2) :]
+    far, refs = refs[: shifts + 1], refs[shifts + 1 :]
     share_out, delta_out, slopes_out, own_outs, sent_outs = refs[0], refs[1], refs[2], refs[3 : 3 + shifts], refs[3 + shifts : 3 + 2 * shifts]
     refs = refs[3 + 2 * shifts :]
     (key_buf, value_buf, dk_buf, dv_buf), sets = refs[:4], (refs[4:7], refs[7:10])
     rows = q_buf.shape[0]
     heads = key_buf.shape[0]
-    columns = seen * SLOTS
+    middle = (shifts - 1) * HALF if seen else 0
+    fresh = middle + (SLOTS if seen == shifts else 0)
+    columns = middle + fresh
     wide = heads * DH
     per_head = group // JOIN
     chunks = heads * per_head
     width = JOIN * rows
-    if seen:
-        place_far(key_buf, value_buf, far[: 2 * seen], far_mask)
+    if not middle:
+        groups = groups[:1]
+    if fresh:
+        place_far(key_buf, value_buf, far[: fresh // HALF], far_mask.at[middle:, :])
+    key_buf, value_buf = key_buf.at[:, :fresh, :], value_buf.at[:, :fresh, :]
+    sets = [(score.at[:fresh, :], signal.at[:fresh, :], weight) for score, signal, weight in sets]
     for out in (*own_outs[seen:], *sent_outs[seen:]):
         out[...] = jnp.zeros_like(out)
-    key_buf, value_buf = key_buf.at[:, :columns, :], value_buf.at[:, :columns, :]
-    sets = [[ref.at[:columns, :] for ref in refs] for refs in sets]
 
     def products(chunk):
-        if not seen:
+        if not fresh:
             return []
         score_ref, signal_ref, _ = sets[chunk % 2]
         return pair_products(key_buf, value_buf, q_buf, g_buf, chunk, chunk // per_head, score_ref, signal_ref)
@@ -205,7 +233,11 @@
     def softmax(chunk):
         score_ref, signal_ref, weight_ref = sets[chunk % 2]
         slope_ref = slopes_out.at[chunk]
-        state = {"top": near_top[chunk]}
+        state = {"top": functools.reduce(jnp.maximum, [group[2][chunk] for group in groups])}
+
+        def clear():
+            if seen < shifts:
+                slope_ref[columns:, :] = jnp.zeros((SLOTS * shifts - columns, width), jnp.bfloat16)
 
         def top(at):
             for i in range(at, at + BLOCK, 8):
@@ -222,18 +254,20 @@
                 state["total"] = state["total"] + grown
 
         def end_grow():
-            total = spread(jnp.sum(state["total"], axis=0, keepdims=True))
-            shrink = jnp.exp2((near_top[chunk] - state["top"]) * LOG_SCALE)
-            state["far"] = 1.0 / (near_total[chunk] * shrink + total)
-            state["near"] = shrink * state["far"]
-            share_out[chunk] = state["near"]
+            shrinks = [jnp.exp2((group[2][chunk] - state["top"]) * LOG_SCALE) for group in groups]
+            totals = [group[3][chunk] * shrink for group, shrink in zip(groups, shrinks)]
+            if fresh:
+                totals.append(spread(jnp.sum(state["total"], axis=0, keepdims=True)))
+            share = 1.0 / functools.reduce(jnp.add, totals)
+            state["shares"] = [shrink * share for shrink in shrinks] + [share]
+            share_out[chunk] = state["shares"][0]
             state["delta"] = jnp.zeros((8, width), jnp.float32)
 
-        def weigh(grown, signal, share, at):
-            probs = [grown[i : i + 8, :] * state[share] for i in range(at, at + BLOCK, 8)]
+        def weigh(grown, signal, index, offset, at):
+            probs = [grown[i : i + 8, :] * state["shares"][index] for i in range(at, at + BLOCK, 8)]
             weights = jnp.concatenate(probs, axis=0).astype(jnp.bfloat16)
-            if share == "far":
-                weight_ref[at : at + BLOCK, :] = weights
+            if index:
+                weight_ref[offset + at : offset + at + BLOCK, :] = weights
             terms = weights.astype(jnp.float32) * signal[at : at + BLOCK, :]
             for i in range(0, BLOCK, 8):
                 state["delta"] = state["delta"] + terms[i : i + 8]
@@ -242,25 +276,27 @@
             state["delta"] = spread(jnp.sum(state["delta"], axis=0, keepdims=True))
             delta_out[chunk] = state["delta"]
 
-        def slope(at):
+        def slope(grown, signal, index, offset, at):
             slopes = []
             for i in range(at, at + BLOCK, 8):
-                probs = score_ref[i : i + 8, :] * state["far"]
-                slopes.append(probs * (signal_ref[i : i + 8, :] - state["delta"]))
-            slope_ref[at : at + BLOCK, :] = jnp.concatenate(slopes, axis=0).astype(jnp.bfloat16)
-
-        grown, signal = near_grown.at[chunk], near_signal.at[chunk]
-        blocks = range(0, columns, BLOCK)
-
-        def clear():
-            if seen < shifts:
-                slope_ref[columns:, :] = jnp.zeros((SLOTS * (shifts - seen), width), jnp.bfloat16)
-
-        steps = [clear] + [functools.partial(top, at) for at in blocks] + [end_top]
-        steps += [functools.partial(grow, at) for at in blocks] + [end_grow]
-        steps += [functools.partial(weigh, score_ref, signal_ref, "far", at) for at in blocks]
-        steps += [functools.partial(weigh, grown, signal, "near", at) for at in range(0, 2 * rows, BLOCK)] + [end_weigh]
-        return steps + [functools.partial(slope, at) for at in blocks]
+                probs = grown[i : i + 8, :] * state["shares"][index]
+                slopes.append(probs * (signal[i : i + 8, :] - state["delta"]))
+            slope_ref[offset + at : offset + at + BLOCK, :] = jnp.concatenate(slopes, axis=0).astype(jnp.bfloat16)
+
+        parts = [(group[0].at[chunk], group[1].at[chunk], index, 0) for index, group in enumerate(groups)]
+        sizes = [2 * rows, middle][: len(groups)]
+        steps = [clear]
+        if fresh:
+            parts.append((score_ref, signal_ref, len(groups), middle))
+            sizes.append(fresh)
+            steps += [functools.partial(top, at) for at in range(0, fresh, BLOCK)] + [end_top]
+            steps += [functools.partial(grow, at) for at in range(0, fresh, BLOCK)]
+        steps.append(end_grow)
+        for work, first, end in ((weigh, 0, end_weigh), (slope, 1, None)):
+            for part, size in list(zip(parts, sizes))[first:]:
+                steps += [functools.partial(work, *part, at) for at in range(0, size, BLOCK)]
+            steps += [end] if end else []
+        return steps
 
     def gradients(chunk):
         if not seen:
@@ -282,21 +318,22 @@
                 return
             cols = slice(side * wide + head * DH, side * wide + (head + 1) * DH)
             for shift in range(seen):
-                at = shift * SLOTS
-                own_outs[shift][:, cols] = total[at : at + HALF] * factor
-                sent_outs[shift][:, cols] = (total[at + HALF : at + SLOTS] * factor).astype(jnp.bfloat16)
+                at = [piece_of(shifts, shift, side) * HALF for side in range(2)]
+                own_outs[shift][:, cols] = total[at[0] : at[0] + HALF] * factor
+                sent_outs[shift][:, cols] = (total[at[1] : at[1] + HALF] * factor).astype(jnp.bfloat16)
 
         return [
             functools.partial(collect, dk_buf, q_buf, lambda cols: slopes_out[chunk, :columns, cols], 0, SCALE),
-            functools.partial(collect, dv_buf, g_buf, lambda cols: weight_ref[:, cols], 1, 1.0),
+            functools.partial(collect, dv_buf, g_buf, lambda cols: weight_ref[:columns, cols], 1, 1.0),
         ]
 
     pipeline(chunks, products, softmax, gradients)
 
 
-def near_gradients_kernel(group, q_buf, g_buf, grown, signal, share, delta, slopes_out, own_out, sent_out, *sets):
+def near_gradients_kernel(group, q_buf, g_buf, grown, signal, share, delta, slopes_out, *refs):
+    own_outs, sent_outs, sets = refs[:2], refs[2:4], refs[4:]
     rows = q_buf.shape[0]
-    wide = own_out.shape[1] // 2
+    wide = own_outs[0].shape[1]
     per_head = group // JOIN
     chunks = wide // DH * per_head
     near = 2 * rows
@@ -329,9 +366,8 @@
             if chunk % per_head < per_head - 1:
                 totals[side] = total
                 return
-            cols = slice(side * wide + head * DH, side * wide + (head + 1) * DH)
-            own_out[:, cols] = total[:rows] * factor
-            sent_out[:, cols] = (total[rows:] * factor).astype(sent_out.dtype)
+            own_outs[side][:, head_cols(head)] = total[:rows] * factor
+            sent_outs[side][:, head_cols(head)] = (total[rows:] * factor).astype(jnp.bfloat16)
 
         return [
             functools.partial(collect, lambda cols: slopes_out[chunk, :, cols], q_buf, 0, SCALE),
@@ -376,6 +412,20 @@
         store.wait()
 
 
+def total_kernel(own_key, own_value, got_key, got_value, *refs):
+    terms, (outs, bufs, sem) = refs[:-9], (refs[-9:-5], refs[-5:-1], refs[-1])
+    wide = bufs[0].shape[1]
+    near = [own[...] + got[...].astype(jnp.float32) for own, got in ((own_key, got_key), (own_value, got_value))]
+    beacon = functools.reduce(jnp.add, [x[...].astype(jnp.float32) for x in terms])
+    stores = []
+    for at, total in enumerate((*near, beacon[:, :wide], beacon[:, wide:])):
+        bufs[at][...] = total.astype(jnp.bfloat16)
+        stores.append(pltpu.make_async_copy(bufs[at], outs[at], sem.at[at]))
+        stores[-1].start()
+    for store in stores:
+        store.wait()
+
+
 def in_hbm(x):
     return pltpu.with_memory_space_constraint(x, pltpu.HBM)
 
@@ -402,10 +452,11 @@
     chunks = heads * group // JOIN
     width = JOIN * rows
     last = spans - 1
-    near, columns = 2 * rows, SLOTS * last
+    near, middle, columns = 2 * rows, HALF * (last - 1), SLOTS * last
     swap = [(0, 1), (1, 0)]
     shifts = range(1, spans)
     order = sorted(shifts, key=lambda k: abs(2 * k - spans))
+    starts = [*sorted(range(1, last), key=lambda k: abs(2 * k - spans)), last]
 
     def up(k):
         return [(i, (i + k) % spans) for i in range(spans)]
@@ -413,7 +464,7 @@
     left = lax.broadcasted_iota(jnp.int32, (beacon_keys.shape[0], 2 * wide), 1) < wide
     beacons = jnp.where(left, jnp.pad(beacon_keys, ((0, 0), (0, wide))), jnp.pad(beacon_values, ((0, 0), (wide, 0))))
     near_keys, near_values, beacons = lax.optimization_barrier((keys, values, beacons))
-    own = {k: lax.ppermute(beacons, "ctx", up(k)) for k in reversed(order)}
+    own = {k: lax.ppermute(beacons, "ctx", up(k)) for k in starts}
     other_key, other_value = (lax.ppermute(x, "sub", swap) for x in (near_keys, near_values))
 
     product = queries.shape[1] * rows * 2
@@ -433,24 +484,40 @@
         8,
         2 * product * near,
     )
-    first = order[0]
-    own[first], near_stats[2] = lax.optimization_barrier((own[first], near_stats[2]))
-    other = {k: lax.ppermute(own[k], "sub", swap) for k in order}
-    far = [x[k] for k in shifts for x in (own, other)]
-    sets = [vmem((columns, width), f32)] * 2 + [vmem((columns, width), bf16)]
+    groups = [near_stats]
+    if middle:
+        first = starts[0]
+        own[first], near_stats[2] = lax.optimization_barrier((own[first], near_stats[2]))
+        groups.append(
+            call(
+                functools.partial(middle_kernel, group),
+                [q_in, g_in, far_mask, *[own[k] for k in range(1, last)]],
+                [vmem] * (2 + last),
+                stats_of(middle),
+                [vmem] * 4,
+                [vmem((heads, middle, 2 * DH), bf16), vmem((heads, middle, DH), bf16)],
+                8,
+                product,
+            )
+        )
+        own[last], groups[1][2] = lax.optimization_barrier((own[last], groups[1][2]))
+    other = {k: lax.ppermute(own[k], "sub", swap) for k in starts}
+    far = [own[k] for k in range(1, last)] + [other[k] for k in range(1, last)] + [own[last], other[last]]
+    fresh = columns - middle
+    sets = [vmem((fresh, width), f32)] * 2 + [vmem((columns, width), bf16)]
     share, delta, far_slopes, *grads = call(
         functools.partial(far_kernel, last, group),
-        [q_in, g_in, far_mask, *near_stats, *far],
-        [vmem] * (7 + len(far)),
+        [q_in, g_in, far_mask, *[x for stats in groups for x in stats], *far[last - 1 :]],
+        [vmem] * (3 + 4 * len(groups) + last + 1),
         [((chunks, 8, width), f32)] * 2
         + [((chunks, columns, width), bf16)]
         + [((HALF, 2 * wide), f32)] * last
         + [((HALF, 2 * wide), bf16)] * last,
         [vmem] * (3 + 2 * last),
-        [vmem((heads, columns, 2 * DH), bf16), vmem((heads, columns, DH), bf16)]
+        [vmem((heads, fresh, 2 * DH), bf16), vmem((heads, fresh, DH), bf16)]
         + [vmem((columns, DH), f32)] * 2
         + sets * 2,
-        12 + 30 * columns * width // 2**20,
+        12 + 25 * columns * width // 2**20,
         4 * product * columns,
     )
     sent = dict(zip(shifts, grads[last:]))
@@ -459,14 +526,14 @@
         return (grads[k - 1] + lax.ppermute(sent[k], "sub", swap).astype(f32)).astype(bf16)
 
     pairs = {k: pair(k) for k in order}
-    pairs[order[-1]], delta = lax.optimization_barrier((pairs[order[-1]], delta))
+    pairs, delta = lax.optimization_barrier((pairs, delta))
     sums = [lax.ppermute(pairs[k], "ctx", up(-k)) for k in order]
-    near_slopes, near_grad, near_sent = call(
+    near_slopes, *near_grads = call(
         functools.partial(near_gradients_kernel, group),
         [q_in, g_in, near_stats[0], near_stats[1], share, delta],
         [vmem] * 6,
-        [((chunks, near, width), bf16), ((rows, 2 * wide), f32), ((rows, 2 * wide), bf16)],
-        [vmem] * 3,
+        [((chunks, near, width), bf16)] + [(keys.shape, f32)] * 2 + [(keys.shape, bf16)] * 2,
+        [vmem] * 5,
         [vmem((near, width), bf16)] * 2,
         8,
         product,
@@ -488,10 +555,19 @@
         12,
         product,
     )
-    near_total = (near_grad + lax.ppermute(near_sent, "sub", swap).astype(f32)).astype(bf16)
+    near_got = [lax.ppermute(x, "sub", swap) for x in near_grads[2:]]
     sums, grad_queries = lax.optimization_barrier((sums, grad_queries))
-    beacon_total = functools.reduce(jnp.add, [x.astype(f32) for x in sums]).astype(bf16)
-    outs = [x for y in (near_total, beacon_total) for x in (y[:, :wide], y[:, wide:])]
+    out_shapes = [(x.shape, bf16) for x in (keys, values, beacon_keys, beacon_values)]
+    outs = call(
+        total_kernel,
+        [*near_grads[:2], *near_got, *sums],
+        [vmem] * (4 + len(sums)),
+        out_shapes,
+        [hbm] * 4,
+        [vmem(*x) for x in out_shapes] + [pltpu.SemaphoreType.DMA((4,))],
+        4,
+        product,
+    )
     return (grad_queries, *outs)
 
 

time: 42.1 us -> 42.8 us (1.017)
  starting transfers between devices: 18.8 us -> 20.9 us
  waiting for transfers between devices: 9.32 us -> 7.38 us
  Pallas kernels: 9.87 us -> 11.8 us
  local copies, waits for them, and re-layouts: 2.03 us -> 0.65 us
    ppermute x7 -> x8, starting transfers between devices: 6.62 us -> 9.06 us  [the longest x3 7.84 us: local(): own = {k: lax.ppermute(beacons, 'ctx', up(k)) for k in starts}]
    ppermute x7 -> x8, waiting for transfers between devices: 4.62 us -> 2.46 us  [the longest x3 1.27 us: local(): other = {k: lax.ppermute(own[k], 'sub', swap) for k in starts}]
    pallas_call x4 -> x6, Pallas kernels: 9.87 us -> 11.8 us  [call(): pl.pallas_call(kernel, out_shape=[jax.ShapeDtypeStruct(*x) for x in outs]...]
    slice x2 -> x0, local copies, waits for them, and re-layouts: 1.38 us -> none  [local(): y[:, wide:]]
    ppermute x3, waiting for transfers between devices: 0.52 us -> 1.1 us  [pair(): lax.ppermute(sent[k], 'sub', swap).astype(f32)]
  transfers between devices with their start and end apart: 15 -> 16, of which waited for: 7 -> 8; matrix products, arithmetic and copies ran while one was open for 2% -> 0% of each run, Pallas kernels for 21% -> 23%
where the time goes in v2:
time: 42.8 us; the launch traced here: 42.6 us
  starting transfers between devices  20.9 us (49%)
  Pallas kernels  11.8 us (28%)
  waiting for transfers between devices  7.38 us (17%)
  other arithmetic  0.99 us (2%)
  between operations  0.88 us (2%)
  local copies, waits for them, and re-layouts  0.65 us (2%)
    pallas_call x6, Pallas kernels, call(): pl.pallas_call(kernel, out_shape=[jax.ShapeDtypeStruct(*x) for x in outs]...  11.8 us
    ppermute x3, starting transfers between devices, local(): sums = [lax.ppermute(pairs[k], 'ctx', up(-k)) for k in order]  10.4 us
    ppermute x3, starting transfers between devices, local(): own = {k: lax.ppermute(beacons, 'ctx', up(k)) for k in starts}  7.84 us
    ppermute x3, waiting for transfers between devices, local(): sums = [lax.ppermute(pairs[k], 'ctx', up(-k)) for k in order]  3.82 us
    ppermute x3, waiting for transfers between devices, local(): other = {k: lax.ppermute(own[k], 'sub', swap) for k in starts}  1.27 us
    ppermute x3, waiting for transfers between devices, local(): own = {k: lax.ppermute(beacons, 'ctx', up(k)) for k in starts}  1.19 us
    ppermute x3, waiting for transfers between devices, pair(): lax.ppermute(sent[k], 'sub', swap).astype(f32)  1.1 us
    select_n x1, other arithmetic, local(): jnp.where(left, jnp.pad(beacon_keys, ((0, 0), (0, wide))), jnp.pad(beacon...  0.9 us
  transfers between devices with their start and end apart: 16, of which 8 were waited for; matrix products, arithmetic and copies ran while one was open for 0% of the time, Pallas kernels for 23%

profile of v2, /device:TPU:0, one launch (start us, length us, event | category | flops | bytes accessed | tf_op | source)
XLA Modules:
  0.0 42.6 jit_solution(2339163094958212008)
XLA Ops:
  0.6 0.9 %pad_select_fusion = bf16[64,1024]{1,0:T(8,128)(2,1)S(1)} fusion(bf16[64,512]{1,0:T(8,128)(2,1)} %param.11, bf16[64,512]{1,0:T(8,128)(2,1)} %param.10, pred[1024]{0:T(1024)(128)(4,1)S(1)} %iota_compare_fusion), kind=kLoop, calls=%fused_computation.3 | loop fusion | flops 65536 | bytes 263168 | tf_op jit(solution)/shard_map/jit(_where)/select_n | solution.py:465
  1.5 0.5 %collective-permute-start = (bf16[128,512]{1,0:T(8,128)(2,1)}, bf16[128,512]{1,0:T(8,128)(2,1)S(1)}, u32[]{:S(2)}, u32[]{:S(2)}) collective-permute-start(bf16[128,512]{1,0:T(8,128)(2,1)} %key_hbm.3), channel_id=1, source_target_pairs={{0,1},{1,0},{2,3},{3,2},{4,5},{5,4},{6,7},{7,6},{8,9},{9,8},{10,11... | collective-permute-start | bytes 393224 | tf_op jit(solution)/shard_map/ppermute | solution.py:468
  2.1 0.1 collective-permute-start.1
  2.1 4.0 %collective-permute-start.2 = (bf16[64,1024]{1,0:T(8,128)(2,1)S(1)}, bf16[64,1024]{1,0:T(8,128)(2,1)S(1)}, u32[]{:S(2)}, u32[]{:S(2)}) collective-permute-start(bf16[64,1024]{1,0:T(8,128)(2,1)S(1)} %pad_select_fusion), channel_id=1, source_target_pairs={{0,8},{4,12},{8,0},{12,4},{1,9},{5,13},{9,1},{13,5},{2,10},{6,14},... | collective-permute-start | bytes 393224 | tf_op jit(solution)/shard_map/ppermute | solution.py:467
  6.2 1.6 %collective-permute-start.3 = (bf16[64,1024]{1,0:T(8,128)(2,1)S(1)}, bf16[64,1024]{1,0:T(8,128)(2,1)S(1)}, u32[]{:S(2)}, u32[]{:S(2)}) collective-permute-start(bf16[64,1024]{1,0:T(8,128)(2,1)S(1)} %pad_select_fusion), channel_id=1, source_target_pairs={{0,4},{4,8},{8,12},{12,0},{1,5},{5,9},{9,13},{13,1},{2,6},{6,10},{... | collective-permute-start | bytes 393224 | tf_op jit(solution)/shard_map/ppermute | solution.py:467
  7.7 2.2 %collective-permute-start.4 = (bf16[64,1024]{1,0:T(8,128)(2,1)S(1)}, bf16[64,1024]{1,0:T(8,128)(2,1)S(1)}, u32[]{:S(2)}, u32[]{:S(2)}) collective-permute-start(bf16[64,1024]{1,0:T(8,128)(2,1)S(1)} %pad_select_fusion), channel_id=1, source_target_pairs={{0,12},{4,0},{8,4},{12,8},{1,13},{5,1},{9,5},{13,9},{2,14},{6,2},{... | collective-permute-start | bytes 393224 | tf_op jit(solution)/shard_map/ppermute | solution.py:467
  10.0 0.0 collective-permute-done.other_key
  10.0 0.0 collective-permute-done.1.other_value
  10.0 0.0 copy-start
  10.0 0.7 %copy-done = s32[4]{0:T(128)S(1)} copy-done((s32[4]{0:T(128)S(1)}, s32[4]{0:T(128)}, u32[]{:S(2)}) %copy-start) | copy-done | bytes 40
  10.6 4.3 %shard_map.110 = (bf16[128,4096]{1,0:T(8,128)(2,1)S(1)}, bf16[128,4096]{1,0:T(8,128)(2,1)S(1)}, bf16[384,128]{1,0:T(8,128)(2,1)S(1)}, f32[8,256,512]{2,1,0:T(8,1...) custom-call(s32[4]{0:T(128)S(1)} %copy-done, bf16[128,4096]{1,0:T(8,128)(2,1)} %q_hbm.1, ...), custom_call_target="tpu_custom_call" | custom-call | flops 536870912 | bytes 2097152 | tf_op jit(solution)/shard_map/pallas_call | solution.py:434
  14.9 1.2 %collective-permute-done.2.refs_1_ = bf16[64,1024]{1,0:T(8,128)(2,1)S(1)} collective-permute-done((bf16[64,1024]{1,0:T(8,128)(2,1)S(1)}, bf16[64,1024]{1,0:T(8,128)(2,1)S(1)}, u32[]{:S(2)}, u32[]{:S(2)}) %collective-permute-start.2) | collective-permute-done | bytes 131104 | tf_op jit(solution)/shard_map/ppermute | solution.py:467
  16.1 0.0 collective-permute-start.6
  16.1 0.0 collective-permute-done.3.refs_0_
  16.1 1.2 %shard_map.111 = (f32[8,128,512]{2,1,0:T(8,128)S(1)}, f32[8,128,512]{2,1,0:T(8,128)S(1)}, f32[8,8,512]{2,1,0:T(8,128)S(1)}, f32[8,8,512]{2,1,0:T(8,128)S(1)}) custom-call(bf16[128,4096]{1,0:T(8,128)(2,1)S(1)} %get-tuple-element.51.q_buf.refs_0_, bf16[128,4096]{1,0:T(8,128)(2,1)S(1)} %get-tuple-element.52.g_buf.refs_1_, ...), custom_call_target="tpu_custom_call" | custom-call | flops 1048576 | bytes 4096 | tf_op jit(solution)/shard_map/pallas_call | solution.py:434
  17.4 0.0 collective-permute-done.4.refs_13_.refs_4_
  17.4 0.6 %collective-permute-start.5 = (bf16[64,1024]{1,0:T(8,128)(2,1)S(1)}, bf16[64,1024]{1,0:T(8,128)(2,1)S(1)}, u32[]{:S(2)}, u32[]{:S(2)}) collective-permute-start(bf16[64,1024]{1,0:T(8,128)(2,1)S(1)} %collective-permute-done.3.refs_0_), channel_id=1, source_target_pairs={{0,1},{1,0},{2,3},{3,2},{4,5},{5,4},{6,7},{7,6},{8,9},{9,8},{10,11... | collective-permute-start | bytes 393224 | tf_op jit(solution)/shard_map/ppermute | solution.py:504
  17.9 0.1 collective-permute-start.7
  18.0 0.9 %collective-permute-done.5.refs_11_.refs_2_ = bf16[64,1024]{1,0:T(8,128)(2,1)S(1)} collective-permute-done((bf16[64,1024]{1,0:T(8,128)(2,1)S(1)}, bf16[64,1024]{1,0:T(8,128)(2,1)S(1)}, u32[]{:S(2)}, u32[]{:S(2)}) %collective-permute-start.5) | collective-permute-done | bytes 131104 | tf_op jit(solution)/shard_map/ppermute | solution.py:504
  18.9 0.0 collective-permute-done.6.refs_12_.refs_3_
  18.9 0.4 collective-permute-done.7.refs_14_.refs_5_
  19.3 1.2 %shard_map.112 = (f32[8,8,512]{2,1,0:T(8,128)S(1)}, f32[8,8,512]{2,1,0:T(8,128)S(1)}, bf16[8,384,512]{2,1,0:T(8,128)(2,1)S(1)}, f32[64,1024]{1,0:T(8,128)S(1)}, ...) custom-call(bf16[128,4096]{1,0:T(8,128)(2,1)S(1)} %get-tuple-element, ...), custom_call_target="tpu_custom_call" | custom-call | flops 1610612736 | bytes 6291456 | tf_op jit(solution)/shard_map/pallas_call | solution.py:434
  20.5 0.3 collective-permute-start.8
  20.7 0.3 collective-permute-start.9
  21.0 0.2 collective-permute-start.10
  21.2 0.7 %collective-permute-done.8 = bf16[64,1024]{1,0:T(8,128)(2,1)S(1)} collective-permute-done((bf16[64,1024]{1,0:T(8,128)(2,1)S(1)}, bf16[64,1024]{1,0:T(8,128)(2,1)S(1)}, u32[]{:S(2)}, u32[]{:S(2)}) %collective-permute-start.8) | collective-permute-done | bytes 131104 | tf_op jit(solution)/shard_map/ppermute | solution.py:526
  21.9 0.2 collective-permute-done.9
  22.1 0.3 collective-permute-done.10
  22.4 8.4 %collective-permute-start.11 = (bf16[64,1024]{1,0:T(8,128)(2,1)S(1)}, bf16[64,1024]{1,0:T(8,128)(2,1)S(1)}, u32[]{:S(2)}, u32[]{:S(2)}) collective-permute-start(bf16[64,1024]{1,0:T(8,128)(2,1)S(1)} %add_convert_fusion.1), channel_id=1, source_target_pairs={{0,8},{4,12},{8,0},{12,4},{1,9},{5,13},{9,1},{13,5},{2,10},{6,14},... | collective-permute-start | bytes 393224 | tf_op jit(solution)/shard_map/ppermute | solution.py:530
  30.8 0.4 %collective-permute-start.12 = (bf16[64,1024]{1,0:T(8,128)(2,1)S(1)}, bf16[64,1024]{1,0:T(8,128)(2,1)S(1)}, u32[]{:S(2)}, u32[]{:S(2)}) collective-permute-start(bf16[64,1024]{1,0:T(8,128)(2,1)S(1)} %add_convert_fusion.2), channel_id=1, source_target_pairs={{0,12},{4,0},{8,4},{12,8},{1,13},{5,1},{9,5},{13,9},{2,14},{6,2},{... | collective-permute-start | bytes 393224 | tf_op jit(solution)/shard_map/ppermute | solution.py:530
  31.3 1.6 %collective-permute-start.13 = (bf16[64,1024]{1,0:T(8,128)(2,1)S(1)}, bf16[64,1024]{1,0:T(8,128)(2,1)S(1)}, u32[]{:S(2)}, u32[]{:S(2)}) collective-permute-start(bf16[64,1024]{1,0:T(8,128)(2,1)S(1)} %add_convert_fusion), channel_id=1, source_target_pairs={{0,4},{4,8},{8,12},{12,0},{1,5},{5,9},{9,13},{13,1},{2,6},{6,10},{... | collective-permute-start | bytes 393224 | tf_op jit(solution)/shard_map/ppermute | solution.py:530
  32.9 1.5 %shard_map.113 = (bf16[8,256,512]{2,1,0:T(8,128)(2,1)S(1)}, f32[128,512]{1,0:T(8,128)S(1)}, f32[128,512]{1,0:T(8,128)S(1)}, bf16[128,512]{1,0:T(8,128)(2,1)S(1)}, bf16[128,512]{1,0:T(8,128)(2,1)S(1)}) custom-call(bf16[128,4096]{1,0:T(8,128)(2,1)S(1)} %get-tuple-element.51.q_buf.refs_0_, bf16[128,4096]{1,0:T(8,128)(2,1)S(1)} %get-tuple-element.52.g_buf.refs_1_, ...), custom_call_target="tpu_custom_call" | custom-call | flops 1048576 | bytes 4096 | tf_op jit(solution)/shard_map/pallas_call | solution.py:434
  34.4 0.1 collective-permute-start.14
  34.5 0.5 %collective-permute-start.15 = (bf16[128,512]{1,0:T(8,128)(2,1)S(1)}, bf16[128,512]{1,0:T(8,128)(2,1)S(1)}, u32[]{:S(2)}, u32[]{:S(2)}) collective-permute-start(bf16[128,512]{1,0:T(8,128)(2,1)S(1)} %get-tuple-element.85), channel_id=1, source_target_pairs={{0,1},{1,0},{2,3},{3,2},{4,5},{5,4},{6,7},{7,6},{8,9},{9,8},{10,11... | collective-permute-start | bytes 393224 | tf_op jit(solution)/shard_map/ppermute | solution.py:558
  35.0 2.8 %shard_map.114 = bf16[128,4096]{1,0:T(8,128)(2,1)} custom-call(bf16[8,256,512]{2,1,0:T(8,128)(2,1)S(1)} %get-tuple-element.79.near_slopes, bf16[8,384,512]{2,1,0:T(8,128)(2,1)S(1)} %get-tuple-element.80.far_slopes, bf16[128,512]{1,0:T(8,128)(2,1)} %key_hbm.3, bf16[128,512]{1,0:T(8,128)(2,1)S(1)} %collective-permute-done.other_key, ...), custom_call_target="tpu_custom_call" | custom-call | flops 1048576 | bytes 4096 | tf_op jit(solution)/shard_map/pallas_call | solution.py:434
  37.8 0.7 %collective-permute-done.11.refs_0_ = bf16[64,1024]{1,0:T(8,128)(2,1)S(1)} collective-permute-done((bf16[64,1024]{1,0:T(8,128)(2,1)S(1)}, bf16[64,1024]{1,0:T(8,128)(2,1)S(1)}, u32[]{:S(2)}, u32[]{:S(2)}) %collective-permute-start.11) | collective-permute-done | bytes 131104 | tf_op jit(solution)/shard_map/ppermute | solution.py:530
  38.5 3.1 %collective-permute-done.12.refs_1_ = bf16[64,1024]{1,0:T(8,128)(2,1)S(1)} collective-permute-done((bf16[64,1024]{1,0:T(8,128)(2,1)S(1)}, bf16[64,1024]{1,0:T(8,128)(2,1)S(1)}, u32[]{:S(2)}, u32[]{:S(2)}) %collective-permute-start.12) | collective-permute-done | bytes 131104 | tf_op jit(solution)/shard_map/ppermute | solution.py:530
  41.6 0.0 collective-permute-done.13.refs_2_
  41.6 0.0 collective-permute-done.14.got_key
  41.6 0.0 collective-permute-done.15.got_value
  41.6 0.8 %shard_map.115 = (bf16[128,512]{1,0:T(8,128)(2,1)}, bf16[128,512]{1,0:T(8,128)(2,1)}, bf16[64,512]{1,0:T(8,128)(2,1)}, bf16[64,512]{1,0:T(8,128)(2,1)}) custom-call(f32[128,512]{1,0:T(8,128)S(1)} %get-tuple-element.82.own_key, f32[128,512]{1,0:T(8,128)S(1)} %get-tuple-element.83.own_value, bf16[128,512]{1,0:T(8,128)(2,1)S(1)} %collective-permute-done.14.got_key, ...), custom_call_target="tpu_custom_call" | custom-call | flops 1048576 | bytes 4096 | tf_op jit(solution)/shard_map/pallas_call | solution.py:434
  (4 shorter events, 0.1 us)
Async XLA Ops:
  1.5 8.4 %collective-permute-start = (bf16[128,512]{1,0:T(8,128)(2,1)}, bf16[128,512]{1,0:T(8,128)(2,1)S(1)}, u32[]{:S(2)}, u32[]{:S(2)}) collective-permute-start(bf16[128,512]{1,0:T(8,128)(2,1)} %key_hbm.3), channel_id=1, source_target_pairs={{0,1},{1,0},{2,3},{3,2},{4,5},{5,4},{6,7},{7,6},{8,9},{9,8},{10,11... | collective-permute-start | bytes 393224 | tf_op jit(solution)/shard_map/ppermute | solution.py:468
  2.1 7.9 %collective-permute-start.1 = (bf16[128,512]{1,0:T(8,128)(2,1)}, bf16[128,512]{1,0:T(8,128)(2,1)S(1)}, u32[]{:S(2)}, u32[]{:S(2)}) collective-permute-start(bf16[128,512]{1,0:T(8,128)(2,1)} %value_hbm.1), channel_id=1, source_target_pairs={{0,1},{1,0},{2,3},{3,2},{4,5},{5,4},{6,7},{7,6},{8,9},{9,8},{10,11... | collective-permute-start | bytes 393224 | tf_op jit(solution)/shard_map/ppermute | solution.py:468
  2.1 14.0 %collective-permute-start.2 = (bf16[64,1024]{1,0:T(8,128)(2,1)S(1)}, bf16[64,1024]{1,0:T(8,128)(2,1)S(1)}, u32[]{:S(2)}, u32[]{:S(2)}) collective-permute-start(bf16[64,1024]{1,0:T(8,128)(2,1)S(1)} %pad_select_fusion), channel_id=1, source_target_pairs={{0,8},{4,12},{8,0},{12,4},{1,9},{5,13},{9,1},{13,5},{2,10},{6,14},... | collective-permute-start | bytes 393224 | tf_op jit(solution)/shard_map/ppermute | solution.py:467
  6.2 10.0 %collective-permute-start.3 = (bf16[64,1024]{1,0:T(8,128)(2,1)S(1)}, bf16[64,1024]{1,0:T(8,128)(2,1)S(1)}, u32[]{:S(2)}, u32[]{:S(2)}) collective-permute-start(bf16[64,1024]{1,0:T(8,128)(2,1)S(1)} %pad_select_fusion), channel_id=1, source_target_pairs={{0,4},{4,8},{8,12},{12,0},{1,5},{5,9},{9,13},{13,1},{2,6},{6,10},{... | collective-permute-start | bytes 393224 | tf_op jit(solution)/shard_map/ppermute | solution.py:467
  7.7 9.6 %collective-permute-start.4 = (bf16[64,1024]{1,0:T(8,128)(2,1)S(1)}, bf16[64,1024]{1,0:T(8,128)(2,1)S(1)}, u32[]{:S(2)}, u32[]{:S(2)}) collective-permute-start(bf16[64,1024]{1,0:T(8,128)(2,1)S(1)} %pad_select_fusion), channel_id=1, source_target_pairs={{0,12},{4,0},{8,4},{12,8},{1,13},{5,1},{9,5},{13,9},{2,14},{6,2},{... | collective-permute-start | bytes 393224 | tf_op jit(solution)/shard_map/ppermute | solution.py:467
  10.0 0.7 %copy-start = (s32[4]{0:T(128)S(1)}, s32[4]{0:T(128)}, u32[]{:S(2)}) copy-start(s32[4]{0:T(128)} %ratios.1) | copy-start | bytes 52
  16.1 2.8 %collective-permute-start.6 = (bf16[64,1024]{1,0:T(8,128)(2,1)S(1)}, bf16[64,1024]{1,0:T(8,128)(2,1)S(1)}, u32[]{:S(2)}, u32[]{:S(2)}) collective-permute-start(bf16[64,1024]{1,0:T(8,128)(2,1)S(1)} %collective-permute-done.2.refs_1_), channel_id=1, source_target_pairs={{0,1},{1,0},{2,3},{3,2},{4,5},{5,4},{6,7},{7,6},{8,9},{9,8},{10,11... | collective-permute-start | bytes 393224 | tf_op jit(solution)/shard_map/ppermute | solution.py:504
  17.4 1.6 %collective-permute-start.5 = (bf16[64,1024]{1,0:T(8,128)(2,1)S(1)}, bf16[64,1024]{1,0:T(8,128)(2,1)S(1)}, u32[]{:S(2)}, u32[]{:S(2)}) collective-permute-start(bf16[64,1024]{1,0:T(8,128)(2,1)S(1)} %collective-permute-done.3.refs_0_), channel_id=1, source_target_pairs={{0,1},{1,0},{2,3},{3,2},{4,5},{5,4},{6,7},{7,6},{8,9},{9,8},{10,11... | collective-permute-start | bytes 393224 | tf_op jit(solution)/shard_map/ppermute | solution.py:504
  17.9 1.3 %collective-permute-start.7 = (bf16[64,1024]{1,0:T(8,128)(2,1)S(1)}, bf16[64,1024]{1,0:T(8,128)(2,1)S(1)}, u32[]{:S(2)}, u32[]{:S(2)}) collective-permute-start(bf16[64,1024]{1,0:T(8,128)(2,1)S(1)} %collective-permute-done.4.refs_13_.refs_4_), channel_id=1, source_target_pairs={{0,1},{1,0},{2,3},{3,2},{4,5},{5,4},{6,7},{7,6},{8,9},{9,8},{10,11... | collective-permute-start | bytes 393224 | tf_op jit(solution)/shard_map/ppermute | solution.py:504
  20.5 1.4 %collective-permute-start.8 = (bf16[64,1024]{1,0:T(8,128)(2,1)S(1)}, bf16[64,1024]{1,0:T(8,128)(2,1)S(1)}, u32[]{:S(2)}, u32[]{:S(2)}) collective-permute-start(bf16[64,1024]{1,0:T(8,128)(2,1)S(1)} %get-tuple-element.68), channel_id=1, source_target_pairs={{0,1},{1,0},{2,3},{3,2},{4,5},{5,4},{6,7},{7,6},{8,9},{9,8},{10,11... | collective-permute-start | bytes 393224 | tf_op jit(solution)/shard_map/ppermute | solution.py:526
  20.7 1.3 %collective-permute-start.9 = (bf16[64,1024]{1,0:T(8,128)(2,1)S(1)}, bf16[64,1024]{1,0:T(8,128)(2,1)S(1)}, u32[]{:S(2)}, u32[]{:S(2)}) collective-permute-start(bf16[64,1024]{1,0:T(8,128)(2,1)S(1)} %get-tuple-element.70), channel_id=1, source_target_pairs={{0,1},{1,0},{2,3},{3,2},{4,5},{5,4},{6,7},{7,6},{8,9},{9,8},{10,11... | collective-permute-start | bytes 393224 | tf_op jit(solution)/shard_map/ppermute | solution.py:526
  21.0 1.3 %collective-permute-start.10 = (bf16[64,1024]{1,0:T(8,128)(2,1)S(1)}, bf16[64,1024]{1,0:T(8,128)(2,1)S(1)}, u32[]{:S(2)}, u32[]{:S(2)}) collective-permute-start(bf16[64,1024]{1,0:T(8,128)(2,1)S(1)} %get-tuple-element.72), channel_id=1, source_target_pairs={{0,1},{1,0},{2,3},{3,2},{4,5},{5,4},{6,7},{7,6},{8,9},{9,8},{10,11... | collective-permute-start | bytes 393224 | tf_op jit(solution)/shard_map/ppermute | solution.py:526
  22.4 16.1 %collective-permute-start.11 = (bf16[64,1024]{1,0:T(8,128)(2,1)S(1)}, bf16[64,1024]{1,0:T(8,128)(2,1)S(1)}, u32[]{:S(2)}, u32[]{:S(2)}) collective-permute-start(bf16[64,1024]{1,0:T(8,128)(2,1)S(1)} %add_convert_fusion.1), channel_id=1, source_target_pairs={{0,8},{4,12},{8,0},{12,4},{1,9},{5,13},{9,1},{13,5},{2,10},{6,14},... | collective-permute-start | bytes 393224 | tf_op jit(solution)/shard_map/ppermute | solution.py:530
  30.8 10.8 %collective-permute-start.12 = (bf16[64,1024]{1,0:T(8,128)(2,1)S(1)}, bf16[64,1024]{1,0:T(8,128)(2,1)S(1)}, u32[]{:S(2)}, u32[]{:S(2)}) collective-permute-start(bf16[64,1024]{1,0:T(8,128)(2,1)S(1)} %add_convert_fusion.2), channel_id=1, source_target_pairs={{0,12},{4,0},{8,4},{12,8},{1,13},{5,1},{9,5},{13,9},{2,14},{6,2},{... | collective-permute-start | bytes 393224 | tf_op jit(solution)/shard_map/ppermute | solution.py:530
  31.3 10.4 %collective-permute-start.13 = (bf16[64,1024]{1,0:T(8,128)(2,1)S(1)}, bf16[64,1024]{1,0:T(8,128)(2,1)S(1)}, u32[]{:S(2)}, u32[]{:S(2)}) collective-permute-start(bf16[64,1024]{1,0:T(8,128)(2,1)S(1)} %add_convert_fusion), channel_id=1, source_target_pairs={{0,4},{4,8},{8,12},{12,0},{1,5},{5,9},{9,13},{13,1},{2,6},{6,10},{... | collective-permute-start | bytes 393224 | tf_op jit(solution)/shard_map/ppermute | solution.py:530
  34.4 7.2 %collective-permute-start.14 = (bf16[128,512]{1,0:T(8,128)(2,1)S(1)}, bf16[128,512]{1,0:T(8,128)(2,1)S(1)}, u32[]{:S(2)}, u32[]{:S(2)}) collective-permute-start(bf16[128,512]{1,0:T(8,128)(2,1)S(1)} %get-tuple-element.84), channel_id=1, source_target_pairs={{0,1},{1,0},{2,3},{3,2},{4,5},{5,4},{6,7},{7,6},{8,9},{9,8},{10,11... | collective-permute-start | bytes 393224 | tf_op jit(solution)/shard_map/ppermute | solution.py:558
  34.5 7.2 %collective-permute-start.15 = (bf16[128,512]{1,0:T(8,128)(2,1)S(1)}, bf16[128,512]{1,0:T(8,128)(2,1)S(1)}, u32[]{:S(2)}, u32[]{:S(2)}) collective-permute-start(bf16[128,512]{1,0:T(8,128)(2,1)S(1)} %get-tuple-element.85), channel_id=1, source_target_pairs={{0,1},{1,0},{2,3},{3,2},{4,5},{5,4},{6,7},{7,6},{8,9},{9,8},{10,11... | collective-permute-start | bytes 393224 | tf_op jit(solution)/shard_map/ppermute | solution.py:558

commit v3 on v1

--- a/solution.py
+++ b/solution.py
@@ -294,9 +294,10 @@
     pipeline(chunks, products, softmax, gradients)
 
 
-def near_gradients_kernel(group, q_buf, g_buf, grown, signal, share, delta, slopes_out, own_out, sent_out, *sets):
+def near_gradients_kernel(group, q_buf, g_buf, grown, signal, share, delta, slopes_out, *refs):
+    own_outs, sent_outs, sets = refs[:2], refs[2:4], refs[4:]
     rows = q_buf.shape[0]
-    wide = own_out.shape[1] // 2
+    wide = own_outs[0].shape[1]
     per_head = group // JOIN
     chunks = wide // DH * per_head
     near = 2 * rows
@@ -329,9 +330,8 @@
             if chunk % per_head < per_head - 1:
                 totals[side] = total
                 return
-            cols = slice(side * wide + head * DH, side * wide + (head + 1) * DH)
-            own_out[:, cols] = total[:rows] * factor
-            sent_out[:, cols] = (total[rows:] * factor).astype(sent_out.dtype)
+            own_outs[side][:, head_cols(head)] = total[:rows] * factor
+            sent_outs[side][:, head_cols(head)] = (total[rows:] * factor).astype(jnp.bfloat16)
 
         return [
             functools.partial(collect, lambda cols: slopes_out[chunk, :, cols], q_buf, 0, SCALE),
@@ -376,6 +376,20 @@
         store.wait()
 
 
+def total_kernel(own_key, own_value, got_key, got_value, *refs):
+    terms, (outs, bufs, sem) = refs[:-9], (refs[-9:-5], refs[-5:-1], refs[-1])
+    wide = bufs[0].shape[1]
+    near = [own[...] + got[...].astype(jnp.float32) for own, got in ((own_key, got_key), (own_value, got_value))]
+    beacon = functools.reduce(jnp.add, [x[...].astype(jnp.float32) for x in terms])
+    stores = []
+    for at, total in enumerate((*near, beacon[:, :wide], beacon[:, wide:])):
+        bufs[at][...] = total.astype(jnp.bfloat16)
+        stores.append(pltpu.make_async_copy(bufs[at], outs[at], sem.at[at]))
+        stores[-1].start()
+    for store in stores:
+        store.wait()
+
+
 def in_hbm(x):
     return pltpu.with_memory_space_constraint(x, pltpu.HBM)
 
@@ -435,7 +449,10 @@
     )
     first = order[0]
     own[first], near_stats[2] = lax.optimization_barrier((own[first], near_stats[2]))
-    other = {k: lax.ppermute(own[k], "sub", swap) for k in order}
+    other = {first: lax.ppermute(own[first], "sub", swap)}
+    own, other = lax.optimization_barrier((own, other))
+    for k in order[1:]:
+        other[k] = lax.ppermute(own[k], "sub", swap)
     far = [x[k] for k in shifts for x in (own, other)]
     sets = [vmem((columns, width), f32)] * 2 + [vmem((columns, width), bf16)]
     share, delta, far_slopes, *grads = call(
@@ -459,14 +476,14 @@
         return (grads[k - 1] + lax.ppermute(sent[k], "sub", swap).astype(f32)).astype(bf16)
 
     pairs = {k: pair(k) for k in order}
-    pairs[order[-1]], delta = lax.optimization_barrier((pairs[order[-1]], delta))
+    pairs, delta = lax.optimization_barrier((pairs, delta))
     sums = [lax.ppermute(pairs[k], "ctx", up(-k)) for k in order]
-    near_slopes, near_grad, near_sent = call(
+    near_slopes, *near_grads = call(
         functools.partial(near_gradients_kernel, group),
         [q_in, g_in, near_stats[0], near_stats[1], share, delta],
         [vmem] * 6,
-        [((chunks, near, width), bf16), ((rows, 2 * wide), f32), ((rows, 2 * wide), bf16)],
-        [vmem] * 3,
+        [((chunks, near, width), bf16)] + [(keys.shape, f32)] * 2 + [(keys.shape, bf16)] * 2,
+        [vmem] * 5,
         [vmem((near, width), bf16)] * 2,
         8,
         product,
@@ -488,10 +505,19 @@
         12,
         product,
     )
-    near_total = (near_grad + lax.ppermute(near_sent, "sub", swap).astype(f32)).astype(bf16)
+    near_got = [lax.ppermute(x, "sub", swap) for x in near_grads[2:]]
     sums, grad_queries = lax.optimization_barrier((sums, grad_queries))
-    beacon_total = functools.reduce(jnp.add, [x.astype(f32) for x in sums]).astype(bf16)
-    outs = [x for y in (near_total, beacon_total) for x in (y[:, :wide], y[:, wide:])]
+    out_shapes = [(x.shape, bf16) for x in (keys, values, beacon_keys, beacon_values)]
+    outs = call(
+        total_kernel,
+        [*near_grads[:2], *near_got, *sums],
+        [vmem] * (4 + len(sums)),
+        out_shapes,
+        [hbm] * 4,
+        [vmem(*x) for x in out_shapes] + [pltpu.SemaphoreType.DMA((4,))],
+        4,
+        product,
+    )
     return (grad_queries, *outs)
 
 

time: 42.1 us -> 42.3 us (level); the launches traced: 41.9 us -> 41.6 us
  local copies, waits for them, and re-layouts: 2.03 us -> 0.65 us
  Pallas kernels: 9.87 us -> 10.7 us
    slice x2 -> x0, local copies, waits for them, and re-layouts: 1.38 us -> none  [local(): y[:, wide:]]
    pallas_call x4 -> x5, Pallas kernels: 9.87 us -> 10.7 us  [call(): pl.pallas_call(kernel, out_shape=[jax.ShapeDtypeStruct(*x) for x in outs]...]
    ppermute x4 -> x5, starting transfers between devices: 0.58 us -> 1.08 us  [the longest x2 0.57 us: local(): near_got = [lax.ppermute(x, 'sub', swap) for x in near_grads[2:]]]
    ppermute x3, waiting for transfers between devices: 0.52 us -> 0.96 us  [pair(): lax.ppermute(sent[k], 'sub', swap).astype(f32)]
    ppermute x4 -> x5, waiting for transfers between devices: 1.03 us -> 1.03 us  [the longest x2 1.02 us: local(): other[k] = lax.ppermute(own[k], 'sub', swap)]
  transfers between devices with their start and end apart: 15 -> 16, of which waited for: 7 -> 9; matrix products, arithmetic and copies ran while one was open for 2% -> 0% of each run, Pallas kernels for 21% -> 21%
where the time goes in v3:
time: 42.3 us; the launch traced here: 41.6 us
  starting transfers between devices  19 us (45%)
  Pallas kernels  10.7 us (25%)
  waiting for transfers between devices  9.36 us (22%)
  other arithmetic  0.99 us (2%)
  between operations  0.89 us (2%)
  local copies, waits for them, and re-layouts  0.65 us (2%)
    pallas_call x5, Pallas kernels, call(): pl.pallas_call(kernel, out_shape=[jax.ShapeDtypeStruct(*x) for x in outs]...  10.7 us
    ppermute x3, starting transfers between devices, local(): sums = [lax.ppermute(pairs[k], 'ctx', up(-k)) for k in order]  10.4 us
    ppermute x3, starting transfers between devices, local(): own = {k: lax.ppermute(beacons, 'ctx', up(k)) for k in reversed(order)}  6.04 us
    ppermute x3, waiting for transfers between devices, local(): sums = [lax.ppermute(pairs[k], 'ctx', up(-k)) for k in order]  3.76 us
    ppermute x3, waiting for transfers between devices, local(): own = {k: lax.ppermute(beacons, 'ctx', up(k)) for k in reversed(order)}  3.6 us
    ppermute x2, waiting for transfers between devices, local(): other[k] = lax.ppermute(own[k], 'sub', swap)  1.02 us
    ppermute x3, waiting for transfers between devices, pair(): lax.ppermute(sent[k], 'sub', swap).astype(f32)  0.96 us
    select_n x1, other arithmetic, local(): jnp.where(left, jnp.pad(beacon_keys, ((0, 0), (0, wide))), jnp.pad(beacon...  0.9 us
  transfers between devices with their start and end apart: 16, of which 9 were waited for; matrix products, arithmetic and copies ran while one was open for 0% of the time, Pallas kernels for 21%

profile of v3, /device:TPU:0, one launch (start us, length us, event | category | flops | bytes accessed | tf_op | source)
XLA Modules:
  0.0 41.6 jit_solution(1058239549122582448)
XLA Ops:
  0.6 0.9 %pad_select_fusion = bf16[64,1024]{1,0:T(8,128)(2,1)S(1)} fusion(bf16[64,512]{1,0:T(8,128)(2,1)} %param.11, bf16[64,512]{1,0:T(8,128)(2,1)} %param.10, pred[1024]{0:T(1024)(128)(4,1)S(1)} %iota_compare_fusion), kind=kLoop, calls=%fused_computation.3 | loop fusion | flops 65536 | bytes 263168 | tf_op jit(solution)/shard_map/jit(_where)/select_n | solution.py:428
  1.5 0.5 %collective-permute-start = (bf16[128,512]{1,0:T(8,128)(2,1)}, bf16[128,512]{1,0:T(8,128)(2,1)S(1)}, u32[]{:S(2)}, u32[]{:S(2)}) collective-permute-start(bf16[128,512]{1,0:T(8,128)(2,1)} %key_hbm.3), channel_id=1, source_target_pairs={{0,1},{1,0},{2,3},{3,2},{4,5},{5,4},{6,7},{7,6},{8,9},{9,8},{10,11... | collective-permute-start | bytes 393224 | tf_op jit(solution)/shard_map/ppermute | solution.py:431
  2.1 0.1 collective-permute-start.1
  2.1 4.0 %collective-permute-start.2 = (bf16[64,1024]{1,0:T(8,128)(2,1)S(1)}, bf16[64,1024]{1,0:T(8,128)(2,1)S(1)}, u32[]{:S(2)}, u32[]{:S(2)}) collective-permute-start(bf16[64,1024]{1,0:T(8,128)(2,1)S(1)} %pad_select_fusion), channel_id=1, source_target_pairs={{0,8},{4,12},{8,0},{12,4},{1,9},{5,13},{9,1},{13,5},{2,10},{6,14},... | collective-permute-start | bytes 393224 | tf_op jit(solution)/shard_map/ppermute | solution.py:430
  6.2 1.3 %collective-permute-start.4 = (bf16[64,1024]{1,0:T(8,128)(2,1)S(1)}, bf16[64,1024]{1,0:T(8,128)(2,1)S(1)}, u32[]{:S(2)}, u32[]{:S(2)}) collective-permute-start(bf16[64,1024]{1,0:T(8,128)(2,1)S(1)} %pad_select_fusion), channel_id=1, source_target_pairs={{0,12},{4,0},{8,4},{12,8},{1,13},{5,1},{9,5},{13,9},{2,14},{6,2},{... | collective-permute-start | bytes 393224 | tf_op jit(solution)/shard_map/ppermute | solution.py:430
  7.5 0.7 %collective-permute-start.3 = (bf16[64,1024]{1,0:T(8,128)(2,1)S(1)}, bf16[64,1024]{1,0:T(8,128)(2,1)S(1)}, u32[]{:S(2)}, u32[]{:S(2)}) collective-permute-start(bf16[64,1024]{1,0:T(8,128)(2,1)S(1)} %pad_select_fusion), channel_id=1, source_target_pairs={{0,4},{4,8},{8,12},{12,0},{1,5},{5,9},{9,13},{13,1},{2,6},{6,10},{... | collective-permute-start | bytes 393224 | tf_op jit(solution)/shard_map/ppermute | solution.py:430
  8.2 0.0 collective-permute-done.other_key
  8.2 0.0 collective-permute-done.1.other_value
  8.2 0.0 copy-start
  8.2 0.7 %copy-done = s32[4]{0:T(128)S(1)} copy-done((s32[4]{0:T(128)S(1)}, s32[4]{0:T(128)}, u32[]{:S(2)}) %copy-start) | copy-done | bytes 40
  8.8 4.3 %shard_map.110 = (bf16[128,4096]{1,0:T(8,128)(2,1)S(1)}, bf16[128,4096]{1,0:T(8,128)(2,1)S(1)}, bf16[384,128]{1,0:T(8,128)(2,1)S(1)}, f32[8,256,512]{2,1,0:T(8,1...) custom-call(s32[4]{0:T(128)S(1)} %copy-done, bf16[128,4096]{1,0:T(8,128)(2,1)} %q_hbm.1, ...), custom_call_target="tpu_custom_call" | custom-call | flops 536870912 | bytes 2097152 | tf_op jit(solution)/shard_map/pallas_call | solution.py:398
  13.1 0.4 %collective-permute-done.2.refs_9_.refs_2_ = bf16[64,1024]{1,0:T(8,128)(2,1)S(1)} collective-permute-done((bf16[64,1024]{1,0:T(8,128)(2,1)S(1)}, bf16[64,1024]{1,0:T(8,128)(2,1)S(1)}, u32[]{:S(2)}, u32[]{:S(2)}) %collective-permute-start.2) | collective-permute-done | bytes 131104 | tf_op jit(solution)/shard_map/ppermute | solution.py:430
  13.6 0.0 collective-permute-start.5
  13.6 0.0 collective-permute-done.4.refs_11_.refs_4_
  13.6 3.2 %collective-permute-done.3.refs_7_.refs_0_ = bf16[64,1024]{1,0:T(8,128)(2,1)S(1)} collective-permute-done((bf16[64,1024]{1,0:T(8,128)(2,1)S(1)}, bf16[64,1024]{1,0:T(8,128)(2,1)S(1)}, u32[]{:S(2)}, u32[]{:S(2)}) %collective-permute-start.3) | collective-permute-done | bytes 131104 | tf_op jit(solution)/shard_map/ppermute | solution.py:430
  16.7 0.0 collective-permute-done.5.refs_10_.refs_3_
  16.7 0.0 collective-permute-start.6
  16.7 0.5 %collective-permute-start.7 = (bf16[64,1024]{1,0:T(8,128)(2,1)S(1)}, bf16[64,1024]{1,0:T(8,128)(2,1)S(1)}, u32[]{:S(2)}, u32[]{:S(2)}) collective-permute-start(bf16[64,1024]{1,0:T(8,128)(2,1)S(1)} %collective-permute-done.4.refs_11_.refs_4_), channel_id=1, source_target_pairs={{0,1},{1,0},{2,3},{3,2},{4,5},{5,4},{6,7},{7,6},{8,9},{9,8},{10,11... | collective-permute-start | bytes 393224 | tf_op jit(solution)/shard_map/ppermute | solution.py:455
  17.2 0.8 %collective-permute-done.6.refs_8_.refs_1_ = bf16[64,1024]{1,0:T(8,128)(2,1)S(1)} collective-permute-done((bf16[64,1024]{1,0:T(8,128)(2,1)S(1)}, bf16[64,1024]{1,0:T(8,128)(2,1)S(1)}, u32[]{:S(2)}, u32[]{:S(2)}) %collective-permute-start.6) | collective-permute-done | bytes 131104 | tf_op jit(solution)/shard_map/ppermute | solution.py:455
  18.1 0.2 collective-permute-done.7.refs_12_.refs_5_
  18.3 1.2 %shard_map.111 = (f32[8,8,512]{2,1,0:T(8,128)S(1)}, f32[8,8,512]{2,1,0:T(8,128)S(1)}, bf16[8,384,512]{2,1,0:T(8,128)(2,1)S(1)}, f32[64,1024]{1,0:T(8,128)S(1)}, ...) custom-call(bf16[128,4096]{1,0:T(8,128)(2,1)S(1)} %get-tuple-element, ...), custom_call_target="tpu_custom_call" | custom-call | flops 1610612736 | bytes 6291456 | tf_op jit(solution)/shard_map/pallas_call | solution.py:398
  19.5 0.4 collective-permute-start.8
  19.9 0.2 collective-permute-start.9
  20.1 0.3 collective-permute-start.10
  20.4 0.5 %collective-permute-done.8 = bf16[64,1024]{1,0:T(8,128)(2,1)S(1)} collective-permute-done((bf16[64,1024]{1,0:T(8,128)(2,1)S(1)}, bf16[64,1024]{1,0:T(8,128)(2,1)S(1)}, u32[]{:S(2)}, u32[]{:S(2)}) %collective-permute-start.8) | collective-permute-done | bytes 131104 | tf_op jit(solution)/shard_map/ppermute | solution.py:476
  20.9 0.3 collective-permute-done.9
  21.3 0.2 collective-permute-done.10
  21.5 8.4 %collective-permute-start.11 = (bf16[64,1024]{1,0:T(8,128)(2,1)S(1)}, bf16[64,1024]{1,0:T(8,128)(2,1)S(1)}, u32[]{:S(2)}, u32[]{:S(2)}) collective-permute-start(bf16[64,1024]{1,0:T(8,128)(2,1)S(1)} %add_convert_fusion.1), channel_id=1, source_target_pairs={{0,8},{4,12},{8,0},{12,4},{1,9},{5,13},{9,1},{13,5},{2,10},{6,14},... | collective-permute-start | bytes 393224 | tf_op jit(solution)/shard_map/ppermute | solution.py:480
  29.8 1.1 %collective-permute-start.12 = (bf16[64,1024]{1,0:T(8,128)(2,1)S(1)}, bf16[64,1024]{1,0:T(8,128)(2,1)S(1)}, u32[]{:S(2)}, u32[]{:S(2)}) collective-permute-start(bf16[64,1024]{1,0:T(8,128)(2,1)S(1)} %add_convert_fusion.2), channel_id=1, source_target_pairs={{0,12},{4,0},{8,4},{12,8},{1,13},{5,1},{9,5},{13,9},{2,14},{6,2},{... | collective-permute-start | bytes 393224 | tf_op jit(solution)/shard_map/ppermute | solution.py:480
  30.9 1.0 %collective-permute-start.13 = (bf16[64,1024]{1,0:T(8,128)(2,1)S(1)}, bf16[64,1024]{1,0:T(8,128)(2,1)S(1)}, u32[]{:S(2)}, u32[]{:S(2)}) collective-permute-start(bf16[64,1024]{1,0:T(8,128)(2,1)S(1)} %add_convert_fusion), channel_id=1, source_target_pairs={{0,4},{4,8},{8,12},{12,0},{1,5},{5,9},{9,13},{13,1},{2,6},{6,10},{... | collective-permute-start | bytes 393224 | tf_op jit(solution)/shard_map/ppermute | solution.py:480
  31.8 1.5 %shard_map.112 = (bf16[8,256,512]{2,1,0:T(8,128)(2,1)S(1)}, f32[128,512]{1,0:T(8,128)S(1)}, f32[128,512]{1,0:T(8,128)S(1)}, bf16[128,512]{1,0:T(8,128)(2,1)S(1)}, bf16[128,512]{1,0:T(8,128)(2,1)S(1)}) custom-call(bf16[128,4096]{1,0:T(8,128)(2,1)S(1)} %get-tuple-element.49.refs_0_.q_buf, bf16[128,4096]{1,0:T(8,128)(2,1)S(1)} %get-tuple-element.50.refs_1_.g_buf, ...), custom_call_target="tpu_custom_call" | custom-call | flops 1048576 | bytes 4096 | tf_op jit(solution)/shard_map/pallas_call | solution.py:398
  33.4 0.1 collective-permute-start.14
  33.5 0.5 %collective-permute-start.15 = (bf16[128,512]{1,0:T(8,128)(2,1)S(1)}, bf16[128,512]{1,0:T(8,128)(2,1)S(1)}, u32[]{:S(2)}, u32[]{:S(2)}) collective-permute-start(bf16[128,512]{1,0:T(8,128)(2,1)S(1)} %get-tuple-element.81), channel_id=1, source_target_pairs={{0,1},{1,0},{2,3},{3,2},{4,5},{5,4},{6,7},{7,6},{8,9},{9,8},{10,11... | collective-permute-start | bytes 393224 | tf_op jit(solution)/shard_map/ppermute | solution.py:508
  34.0 2.8 %shard_map.113 = bf16[128,4096]{1,0:T(8,128)(2,1)} custom-call(bf16[8,256,512]{2,1,0:T(8,128)(2,1)S(1)} %get-tuple-element.75.near_slopes, bf16[8,384,512]{2,1,0:T(8,128)(2,1)S(1)} %get-tuple-element.76.far_slopes, bf16[128,512]{1,0:T(8,128)(2,1)} %key_hbm.3, bf16[128,512]{1,0:T(8,128)(2,1)S(1)} %collective-permute-done.other_key, ...), custom_call_target="tpu_custom_call" | custom-call | flops 1048576 | bytes 4096 | tf_op jit(solution)/shard_map/pallas_call | solution.py:398
  36.8 0.1 collective-permute-done.11.refs_0_
  36.9 0.0 collective-permute-done.12.refs_1_
  37.0 3.6 %collective-permute-done.13.refs_2_ = bf16[64,1024]{1,0:T(8,128)(2,1)S(1)} collective-permute-done((bf16[64,1024]{1,0:T(8,128)(2,1)S(1)}, bf16[64,1024]{1,0:T(8,128)(2,1)S(1)}, u32[]{:S(2)}, u32[]{:S(2)}) %collective-permute-start.13) | collective-permute-done | bytes 131104 | tf_op jit(solution)/shard_map/ppermute | solution.py:480
  40.6 0.0 collective-permute-done.14.got_key
  40.6 0.0 collective-permute-done.15.got_value
  40.6 0.8 %shard_map.114 = (bf16[128,512]{1,0:T(8,128)(2,1)}, bf16[128,512]{1,0:T(8,128)(2,1)}, bf16[64,512]{1,0:T(8,128)(2,1)}, bf16[64,512]{1,0:T(8,128)(2,1)}) custom-call(f32[128,512]{1,0:T(8,128)S(1)} %get-tuple-element.78.own_key, f32[128,512]{1,0:T(8,128)S(1)} %get-tuple-element.79.own_value, bf16[128,512]{1,0:T(8,128)(2,1)S(1)} %collective-permute-done.14.got_key, ...), custom_call_target="tpu_custom_call" | custom-call | flops 1048576 | bytes 4096 | tf_op jit(solution)/shard_map/pallas_call | solution.py:398
  (4 shorter events, 0.1 us)
Async XLA Ops:
  1.5 6.6 %collective-permute-start = (bf16[128,512]{1,0:T(8,128)(2,1)}, bf16[128,512]{1,0:T(8,128)(2,1)S(1)}, u32[]{:S(2)}, u32[]{:S(2)}) collective-permute-start(bf16[128,512]{1,0:T(8,128)(2,1)} %key_hbm.3), channel_id=1, source_target_pairs={{0,1},{1,0},{2,3},{3,2},{4,5},{5,4},{6,7},{7,6},{8,9},{9,8},{10,11... | collective-permute-start | bytes 393224 | tf_op jit(solution)/shard_map/ppermute | solution.py:431
  2.1 6.1 %collective-permute-start.1 = (bf16[128,512]{1,0:T(8,128)(2,1)}, bf16[128,512]{1,0:T(8,128)(2,1)S(1)}, u32[]{:S(2)}, u32[]{:S(2)}) collective-permute-start(bf16[128,512]{1,0:T(8,128)(2,1)} %value_hbm.1), channel_id=1, source_target_pairs={{0,1},{1,0},{2,3},{3,2},{4,5},{5,4},{6,7},{7,6},{8,9},{9,8},{10,11... | collective-permute-start | bytes 393224 | tf_op jit(solution)/shard_map/ppermute | solution.py:431
  2.1 11.4 %collective-permute-start.2 = (bf16[64,1024]{1,0:T(8,128)(2,1)S(1)}, bf16[64,1024]{1,0:T(8,128)(2,1)S(1)}, u32[]{:S(2)}, u32[]{:S(2)}) collective-permute-start(bf16[64,1024]{1,0:T(8,128)(2,1)S(1)} %pad_select_fusion), channel_id=1, source_target_pairs={{0,8},{4,12},{8,0},{12,4},{1,9},{5,13},{9,1},{13,5},{2,10},{6,14},... | collective-permute-start | bytes 393224 | tf_op jit(solution)/shard_map/ppermute | solution.py:430
  6.2 7.4 %collective-permute-start.4 = (bf16[64,1024]{1,0:T(8,128)(2,1)S(1)}, bf16[64,1024]{1,0:T(8,128)(2,1)S(1)}, u32[]{:S(2)}, u32[]{:S(2)}) collective-permute-start(bf16[64,1024]{1,0:T(8,128)(2,1)S(1)} %pad_select_fusion), channel_id=1, source_target_pairs={{0,12},{4,0},{8,4},{12,8},{1,13},{5,1},{9,5},{13,9},{2,14},{6,2},{... | collective-permute-start | bytes 393224 | tf_op jit(solution)/shard_map/ppermute | solution.py:430
  7.5 9.2 %collective-permute-start.3 = (bf16[64,1024]{1,0:T(8,128)(2,1)S(1)}, bf16[64,1024]{1,0:T(8,128)(2,1)S(1)}, u32[]{:S(2)}, u32[]{:S(2)}) collective-permute-start(bf16[64,1024]{1,0:T(8,128)(2,1)S(1)} %pad_select_fusion), channel_id=1, source_target_pairs={{0,4},{4,8},{8,12},{12,0},{1,5},{5,9},{9,13},{13,1},{2,6},{6,10},{... | collective-permute-start | bytes 393224 | tf_op jit(solution)/shard_map/ppermute | solution.py:430
  8.2 0.7 %copy-start = (s32[4]{0:T(128)S(1)}, s32[4]{0:T(128)}, u32[]{:S(2)}) copy-start(s32[4]{0:T(128)} %ratios.1) | copy-start | bytes 52
  13.6 3.2 %collective-permute-start.5 = (bf16[64,1024]{1,0:T(8,128)(2,1)S(1)}, bf16[64,1024]{1,0:T(8,128)(2,1)S(1)}, u32[]{:S(2)}, u32[]{:S(2)}) collective-permute-start(bf16[64,1024]{1,0:T(8,128)(2,1)S(1)} %collective-permute-done.2.refs_9_.refs_2_), channel_id=1, source_target_pairs={{0,1},{1,0},{2,3},{3,2},{4,5},{5,4},{6,7},{7,6},{8,9},{9,8},{10,11... | collective-permute-start | bytes 393224 | tf_op jit(solution)/shard_map/ppermute | solution.py:452
  16.7 1.3 %collective-permute-start.6 = (bf16[64,1024]{1,0:T(8,128)(2,1)S(1)}, bf16[64,1024]{1,0:T(8,128)(2,1)S(1)}, u32[]{:S(2)}, u32[]{:S(2)}) collective-permute-start(bf16[64,1024]{1,0:T(8,128)(2,1)S(1)} %collective-permute-done.3.refs_7_.refs_0_), channel_id=1, source_target_pairs={{0,1},{1,0},{2,3},{3,2},{4,5},{5,4},{6,7},{7,6},{8,9},{9,8},{10,11... | collective-permute-start | bytes 393224 | tf_op jit(solution)/shard_map/ppermute | solution.py:455
  16.7 1.5 %collective-permute-start.7 = (bf16[64,1024]{1,0:T(8,128)(2,1)S(1)}, bf16[64,1024]{1,0:T(8,128)(2,1)S(1)}, u32[]{:S(2)}, u32[]{:S(2)}) collective-permute-start(bf16[64,1024]{1,0:T(8,128)(2,1)S(1)} %collective-permute-done.4.refs_11_.refs_4_), channel_id=1, source_target_pairs={{0,1},{1,0},{2,3},{3,2},{4,5},{5,4},{6,7},{7,6},{8,9},{9,8},{10,11... | collective-permute-start | bytes 393224 | tf_op jit(solution)/shard_map/ppermute | solution.py:455
  19.5 1.4 %collective-permute-start.8 = (bf16[64,1024]{1,0:T(8,128)(2,1)S(1)}, bf16[64,1024]{1,0:T(8,128)(2,1)S(1)}, u32[]{:S(2)}, u32[]{:S(2)}) collective-permute-start(bf16[64,1024]{1,0:T(8,128)(2,1)S(1)} %get-tuple-element.64), channel_id=1, source_target_pairs={{0,1},{1,0},{2,3},{3,2},{4,5},{5,4},{6,7},{7,6},{8,9},{9,8},{10,11... | collective-permute-start | bytes 393224 | tf_op jit(solution)/shard_map/ppermute | solution.py:476
  19.9 1.3 %collective-permute-start.9 = (bf16[64,1024]{1,0:T(8,128)(2,1)S(1)}, bf16[64,1024]{1,0:T(8,128)(2,1)S(1)}, u32[]{:S(2)}, u32[]{:S(2)}) collective-permute-start(bf16[64,1024]{1,0:T(8,128)(2,1)S(1)} %get-tuple-element.66), channel_id=1, source_target_pairs={{0,1},{1,0},{2,3},{3,2},{4,5},{5,4},{6,7},{7,6},{8,9},{9,8},{10,11... | collective-permute-start | bytes 393224 | tf_op jit(solution)/shard_map/ppermute | solution.py:476
  20.1 1.3 %collective-permute-start.10 = (bf16[64,1024]{1,0:T(8,128)(2,1)S(1)}, bf16[64,1024]{1,0:T(8,128)(2,1)S(1)}, u32[]{:S(2)}, u32[]{:S(2)}) collective-permute-start(bf16[64,1024]{1,0:T(8,128)(2,1)S(1)} %get-tuple-element.68), channel_id=1, source_target_pairs={{0,1},{1,0},{2,3},{3,2},{4,5},{5,4},{6,7},{7,6},{8,9},{9,8},{10,11... | collective-permute-start | bytes 393224 | tf_op jit(solution)/shard_map/ppermute | solution.py:476
  21.5 15.5 %collective-permute-start.11 = (bf16[64,1024]{1,0:T(8,128)(2,1)S(1)}, bf16[64,1024]{1,0:T(8,128)(2,1)S(1)}, u32[]{:S(2)}, u32[]{:S(2)}) collective-permute-start(bf16[64,1024]{1,0:T(8,128)(2,1)S(1)} %add_convert_fusion.1), channel_id=1, source_target_pairs={{0,8},{4,12},{8,0},{12,4},{1,9},{5,13},{9,1},{13,5},{2,10},{6,14},... | collective-permute-start | bytes 393224 | tf_op jit(solution)/shard_map/ppermute | solution.py:480
  29.8 7.2 %collective-permute-start.12 = (bf16[64,1024]{1,0:T(8,128)(2,1)S(1)}, bf16[64,1024]{1,0:T(8,128)(2,1)S(1)}, u32[]{:S(2)}, u32[]{:S(2)}) collective-permute-start(bf16[64,1024]{1,0:T(8,128)(2,1)S(1)} %add_convert_fusion.2), channel_id=1, source_target_pairs={{0,12},{4,0},{8,4},{12,8},{1,13},{5,1},{9,5},{13,9},{2,14},{6,2},{... | collective-permute-start | bytes 393224 | tf_op jit(solution)/shard_map/ppermute | solution.py:480
  30.9 9.7 %collective-permute-start.13 = (bf16[64,1024]{1,0:T(8,128)(2,1)S(1)}, bf16[64,1024]{1,0:T(8,128)(2,1)S(1)}, u32[]{:S(2)}, u32[]{:S(2)}) collective-permute-start(bf16[64,1024]{1,0:T(8,128)(2,1)S(1)} %add_convert_fusion), channel_id=1, source_target_pairs={{0,4},{4,8},{8,12},{12,0},{1,5},{5,9},{9,13},{13,1},{2,6},{6,10},{... | collective-permute-start | bytes 393224 | tf_op jit(solution)/shard_map/ppermute | solution.py:480
  33.4 7.2 %collective-permute-start.14 = (bf16[128,512]{1,0:T(8,128)(2,1)S(1)}, bf16[128,512]{1,0:T(8,128)(2,1)S(1)}, u32[]{:S(2)}, u32[]{:S(2)}) collective-permute-start(bf16[128,512]{1,0:T(8,128)(2,1)S(1)} %get-tuple-element.80), channel_id=1, source_target_pairs={{0,1},{1,0},{2,3},{3,2},{4,5},{5,4},{6,7},{7,6},{8,9},{9,8},{10,11... | collective-permute-start | bytes 393224 | tf_op jit(solution)/shard_map/ppermute | solution.py:508
  33.5 7.1 %collective-permute-start.15 = (bf16[128,512]{1,0:T(8,128)(2,1)S(1)}, bf16[128,512]{1,0:T(8,128)(2,1)S(1)}, u32[]{:S(2)}, u32[]{:S(2)}) collective-permute-start(bf16[128,512]{1,0:T(8,128)(2,1)S(1)} %get-tuple-element.81), channel_id=1, source_target_pairs={{0,1},{1,0},{2,3},{3,2},{4,5},{5,4},{6,7},{7,6},{8,9},{9,8},{10,11... | collective-permute-start | bytes 393224 | tf_op jit(solution)/shard_map/ppermute | solution.py:508

commit v4 on v3

--- a/solution.py
+++ b/solution.py
@@ -449,10 +449,7 @@
     )
     first = order[0]
     own[first], near_stats[2] = lax.optimization_barrier((own[first], near_stats[2]))
-    other = {first: lax.ppermute(own[first], "sub", swap)}
-    own, other = lax.optimization_barrier((own, other))
-    for k in order[1:]:
-        other[k] = lax.ppermute(own[k], "sub", swap)
+    other = {k: lax.ppermute(own[k], "sub", swap) for k in order}
     far = [x[k] for k in shifts for x in (own, other)]
     sets = [vmem((columns, width), f32)] * 2 + [vmem((columns, width), bf16)]
     share, delta, far_slopes, *grads = call(
@@ -476,7 +473,7 @@
         return (grads[k - 1] + lax.ppermute(sent[k], "sub", swap).astype(f32)).astype(bf16)
 
     pairs = {k: pair(k) for k in order}
-    pairs, delta = lax.optimization_barrier((pairs, delta))
+    pairs[order[-1]], delta = lax.optimization_barrier((pairs[order[-1]], delta))
     sums = [lax.ppermute(pairs[k], "ctx", up(-k)) for k in order]
     near_slopes, *near_grads = call(
         functools.partial(near_gradients_kernel, group),

time: 42.3 us -> 41.6 us (0.983); the launches traced: 41.6 us -> 41.3 us
  waiting for transfers between devices: 9.36 us -> 8.82 us
    ppermute x3, waiting for transfers between devices: 0.96 us -> 0.52 us  [pair(): lax.ppermute(sent[k], 'sub', swap).astype(f32)]
  transfers between devices with their start and end apart: 16 -> 16, of which waited for: 9 -> 6; matrix products, arithmetic and copies ran while one was open for 0% -> 0% of each run, Pallas kernels for 21% -> 21%
where the time goes in v4:
time: 41.6 us; the launch traced here: 41.3 us
  starting transfers between devices  19.3 us (46%)
  Pallas kernels  10.7 us (26%)
  waiting for transfers between devices  8.82 us (21%)
  other arithmetic  0.99 us (2%)
  between operations  0.9 us (2%)
  local copies, waits for them, and re-layouts  0.65 us (2%)
    ppermute x3, starting transfers between devices, local(): sums = [lax.ppermute(pairs[k], 'ctx', up(-k)) for k in order]  10.7 us
    pallas_call x5, Pallas kernels, call(): pl.pallas_call(kernel, out_shape=[jax.ShapeDtypeStruct(*x) for x in outs]...  10.7 us
    ppermute x3, starting transfers between devices, local(): own = {k: lax.ppermute(beacons, 'ctx', up(k)) for k in reversed(order)}  6.04 us
    ppermute x3, waiting for transfers between devices, local(): sums = [lax.ppermute(pairs[k], 'ctx', up(-k)) for k in order]  3.67 us
    ppermute x3, waiting for transfers between devices, local(): own = {k: lax.ppermute(beacons, 'ctx', up(k)) for k in reversed(order)}  3.6 us
    ppermute x3, waiting for transfers between devices, local(): other = {k: lax.ppermute(own[k], 'sub', swap) for k in order}  1.02 us
    select_n x1, other arithmetic, local(): jnp.where(left, jnp.pad(beacon_keys, ((0, 0), (0, wide))), jnp.pad(beacon...  0.9 us
    ppermute x3, starting transfers between devices, pair(): lax.ppermute(sent[k], 'sub', swap).astype(f32)  0.9 us
  transfers between devices with their start and end apart: 16, of which 6 were waited for; matrix products, arithmetic and copies ran while one was open for 0% of the time, Pallas kernels for 21%

profile of v4, /device:TPU:0, one launch (start us, length us, event | category | flops | bytes accessed | tf_op | source)
XLA Modules:
  0.0 41.3 jit_solution(17436626697011280751)
XLA Ops:
  0.6 0.9 %pad_select_fusion = bf16[64,1024]{1,0:T(8,128)(2,1)S(1)} fusion(bf16[64,512]{1,0:T(8,128)(2,1)} %param.11, bf16[64,512]{1,0:T(8,128)(2,1)} %param.10, pred[1024]{0:T(1024)(128)(4,1)S(1)} %iota_compare_fusion), kind=kLoop, calls=%fused_computation.3 | loop fusion | flops 65536 | bytes 263168 | tf_op jit(solution)/shard_map/jit(_where)/select_n | solution.py:428
  1.5 0.5 %collective-permute-start = (bf16[128,512]{1,0:T(8,128)(2,1)}, bf16[128,512]{1,0:T(8,128)(2,1)S(1)}, u32[]{:S(2)}, u32[]{:S(2)}) collective-permute-start(bf16[128,512]{1,0:T(8,128)(2,1)} %key_hbm.3), channel_id=1, source_target_pairs={{0,1},{1,0},{2,3},{3,2},{4,5},{5,4},{6,7},{7,6},{8,9},{9,8},{10,11... | collective-permute-start | bytes 393224 | tf_op jit(solution)/shard_map/ppermute | solution.py:431
  2.1 0.1 collective-permute-start.1
  2.1 4.0 %collective-permute-start.2 = (bf16[64,1024]{1,0:T(8,128)(2,1)S(1)}, bf16[64,1024]{1,0:T(8,128)(2,1)S(1)}, u32[]{:S(2)}, u32[]{:S(2)}) collective-permute-start(bf16[64,1024]{1,0:T(8,128)(2,1)S(1)} %pad_select_fusion), channel_id=1, source_target_pairs={{0,8},{4,12},{8,0},{12,4},{1,9},{5,13},{9,1},{13,5},{2,10},{6,14},... | collective-permute-start | bytes 393224 | tf_op jit(solution)/shard_map/ppermute | solution.py:430
  6.2 1.3 %collective-permute-start.6 = (bf16[64,1024]{1,0:T(8,128)(2,1)S(1)}, bf16[64,1024]{1,0:T(8,128)(2,1)S(1)}, u32[]{:S(2)}, u32[]{:S(2)}) collective-permute-start(bf16[64,1024]{1,0:T(8,128)(2,1)S(1)} %pad_select_fusion), channel_id=1, source_target_pairs={{0,12},{4,0},{8,4},{12,8},{1,13},{5,1},{9,5},{13,9},{2,14},{6,2},{... | collective-permute-start | bytes 393224 | tf_op jit(solution)/shard_map/ppermute | solution.py:430
  7.5 0.7 %collective-permute-start.3 = (bf16[64,1024]{1,0:T(8,128)(2,1)S(1)}, bf16[64,1024]{1,0:T(8,128)(2,1)S(1)}, u32[]{:S(2)}, u32[]{:S(2)}) collective-permute-start(bf16[64,1024]{1,0:T(8,128)(2,1)S(1)} %pad_select_fusion), channel_id=1, source_target_pairs={{0,4},{4,8},{8,12},{12,0},{1,5},{5,9},{9,13},{13,1},{2,6},{6,10},{... | collective-permute-start | bytes 393224 | tf_op jit(solution)/shard_map/ppermute | solution.py:430
  8.2 0.0 collective-permute-done.other_key
  8.2 0.0 collective-permute-done.1.other_value
  8.2 0.0 copy-start
  8.2 0.7 %copy-done = s32[4]{0:T(128)S(1)} copy-done((s32[4]{0:T(128)S(1)}, s32[4]{0:T(128)}, u32[]{:S(2)}) %copy-start) | copy-done | bytes 40
  8.8 4.3 %shard_map.110 = (bf16[128,4096]{1,0:T(8,128)(2,1)S(1)}, bf16[128,4096]{1,0:T(8,128)(2,1)S(1)}, bf16[384,128]{1,0:T(8,128)(2,1)S(1)}, f32[8,256,512]{2,1,0:T(8,1...) custom-call(s32[4]{0:T(128)S(1)} %copy-done, bf16[128,4096]{1,0:T(8,128)(2,1)} %q_hbm.1, ...), custom_call_target="tpu_custom_call" | custom-call | flops 536870912 | bytes 2097152 | tf_op jit(solution)/shard_map/pallas_call | solution.py:398
  13.1 0.4 %collective-permute-done.2.refs_9_.refs_2_ = bf16[64,1024]{1,0:T(8,128)(2,1)S(1)} collective-permute-done((bf16[64,1024]{1,0:T(8,128)(2,1)S(1)}, bf16[64,1024]{1,0:T(8,128)(2,1)S(1)}, u32[]{:S(2)}, u32[]{:S(2)}) %collective-permute-start.2) | collective-permute-done | bytes 131104 | tf_op jit(solution)/shard_map/ppermute | solution.py:430
  13.6 0.0 collective-permute-done.6.refs_11_.refs_4_
  13.6 0.0 collective-permute-start.7
  13.6 3.2 %collective-permute-done.3.refs_7_.refs_0_ = bf16[64,1024]{1,0:T(8,128)(2,1)S(1)} collective-permute-done((bf16[64,1024]{1,0:T(8,128)(2,1)S(1)}, bf16[64,1024]{1,0:T(8,128)(2,1)S(1)}, u32[]{:S(2)}, u32[]{:S(2)}) %collective-permute-start.3) | collective-permute-done | bytes 131104 | tf_op jit(solution)/shard_map/ppermute | solution.py:430
  16.7 0.0 collective-permute-start.4
  16.7 0.5 %collective-permute-start.5 = (bf16[64,1024]{1,0:T(8,128)(2,1)S(1)}, bf16[64,1024]{1,0:T(8,128)(2,1)S(1)}, u32[]{:S(2)}, u32[]{:S(2)}) collective-permute-start(bf16[64,1024]{1,0:T(8,128)(2,1)S(1)} %collective-permute-done.2.refs_9_.refs_2_), channel_id=1, source_target_pairs={{0,1},{1,0},{2,3},{3,2},{4,5},{5,4},{6,7},{7,6},{8,9},{9,8},{10,11... | collective-permute-start | bytes 393224 | tf_op jit(solution)/shard_map/ppermute | solution.py:452
  17.2 0.0 collective-permute-done.7.refs_12_.refs_5_
  17.2 0.8 %collective-permute-done.4.refs_8_.refs_1_ = bf16[64,1024]{1,0:T(8,128)(2,1)S(1)} collective-permute-done((bf16[64,1024]{1,0:T(8,128)(2,1)S(1)}, bf16[64,1024]{1,0:T(8,128)(2,1)S(1)}, u32[]{:S(2)}, u32[]{:S(2)}) %collective-permute-start.4) | collective-permute-done | bytes 131104 | tf_op jit(solution)/shard_map/ppermute | solution.py:452
  18.1 0.2 collective-permute-done.5.refs_10_.refs_3_
  18.3 1.2 %shard_map.111 = (f32[8,8,512]{2,1,0:T(8,128)S(1)}, f32[8,8,512]{2,1,0:T(8,128)S(1)}, bf16[8,384,512]{2,1,0:T(8,128)(2,1)S(1)}, f32[64,1024]{1,0:T(8,128)S(1)}, ...) custom-call(bf16[128,4096]{1,0:T(8,128)(2,1)S(1)} %get-tuple-element, ...), custom_call_target="tpu_custom_call" | custom-call | flops 1610612736 | bytes 6291456 | tf_op jit(solution)/shard_map/pallas_call | solution.py:398
  19.5 0.4 collective-permute-start.8
  19.9 0.2 collective-permute-start.10
  20.1 0.3 collective-permute-start.12
  20.4 0.5 %collective-permute-done.8 = bf16[64,1024]{1,0:T(8,128)(2,1)S(1)} collective-permute-done((bf16[64,1024]{1,0:T(8,128)(2,1)S(1)}, bf16[64,1024]{1,0:T(8,128)(2,1)S(1)}, u32[]{:S(2)}, u32[]{:S(2)}) %collective-permute-start.8) | collective-permute-done | bytes 131104 | tf_op jit(solution)/shard_map/ppermute | solution.py:473
  20.9 8.4 %collective-permute-start.9 = (bf16[64,1024]{1,0:T(8,128)(2,1)S(1)}, bf16[64,1024]{1,0:T(8,128)(2,1)S(1)}, u32[]{:S(2)}, u32[]{:S(2)}) collective-permute-start(bf16[64,1024]{1,0:T(8,128)(2,1)S(1)} %add_convert_fusion.2), channel_id=1, source_target_pairs={{0,8},{4,12},{8,0},{12,4},{1,9},{5,13},{9,1},{13,5},{2,10},{6,14},... | collective-permute-start | bytes 393224 | tf_op jit(solution)/shard_map/ppermute | solution.py:477
  29.3 0.0 collective-permute-done.10
  29.3 0.2 collective-permute-start.11
  29.5 0.0 collective-permute-done.12
  29.5 2.2 %collective-permute-start.13 = (bf16[64,1024]{1,0:T(8,128)(2,1)S(1)}, bf16[64,1024]{1,0:T(8,128)(2,1)S(1)}, u32[]{:S(2)}, u32[]{:S(2)}) collective-permute-start(bf16[64,1024]{1,0:T(8,128)(2,1)S(1)} %add_convert_fusion), channel_id=1, source_target_pairs={{0,4},{4,8},{8,12},{12,0},{1,5},{5,9},{9,13},{13,1},{2,6},{6,10},{... | collective-permute-start | bytes 393224 | tf_op jit(solution)/shard_map/ppermute | solution.py:477
  31.7 1.5 %shard_map.112 = (bf16[8,256,512]{2,1,0:T(8,128)(2,1)S(1)}, f32[128,512]{1,0:T(8,128)S(1)}, f32[128,512]{1,0:T(8,128)S(1)}, bf16[128,512]{1,0:T(8,128)(2,1)S(1)}, bf16[128,512]{1,0:T(8,128)(2,1)S(1)}) custom-call(bf16[128,4096]{1,0:T(8,128)(2,1)S(1)} %get-tuple-element.43.refs_0_.q_buf, bf16[128,4096]{1,0:T(8,128)(2,1)S(1)} %get-tuple-element.44.refs_1_.g_buf, ...), custom_call_target="tpu_custom_call" | custom-call | flops 1048576 | bytes 4096 | tf_op jit(solution)/shard_map/pallas_call | solution.py:398
  33.3 0.1 collective-permute-start.14
  33.3 0.5 %collective-permute-start.15 = (bf16[128,512]{1,0:T(8,128)(2,1)S(1)}, bf16[128,512]{1,0:T(8,128)(2,1)S(1)}, u32[]{:S(2)}, u32[]{:S(2)}) collective-permute-start(bf16[128,512]{1,0:T(8,128)(2,1)S(1)} %get-tuple-element.69), channel_id=1, source_target_pairs={{0,1},{1,0},{2,3},{3,2},{4,5},{5,4},{6,7},{7,6},{8,9},{9,8},{10,11... | collective-permute-start | bytes 393224 | tf_op jit(solution)/shard_map/ppermute | solution.py:505
  33.8 2.8 %shard_map.113 = bf16[128,4096]{1,0:T(8,128)(2,1)} custom-call(bf16[8,256,512]{2,1,0:T(8,128)(2,1)S(1)} %get-tuple-element.63.near_slopes, bf16[8,384,512]{2,1,0:T(8,128)(2,1)S(1)} %get-tuple-element.64.far_slopes, bf16[128,512]{1,0:T(8,128)(2,1)} %key_hbm.3, bf16[128,512]{1,0:T(8,128)(2,1)S(1)} %collective-permute-done.other_key, ...), custom_call_target="tpu_custom_call" | custom-call | flops 1048576 | bytes 4096 | tf_op jit(solution)/shard_map/pallas_call | solution.py:398
  36.7 0.0 collective-permute-done.9.refs_0_
  36.7 3.7 %collective-permute-done.11.refs_1_ = bf16[64,1024]{1,0:T(8,128)(2,1)S(1)} collective-permute-done((bf16[64,1024]{1,0:T(8,128)(2,1)S(1)}, bf16[64,1024]{1,0:T(8,128)(2,1)S(1)}, u32[]{:S(2)}, u32[]{:S(2)}) %collective-permute-start.11) | collective-permute-done | bytes 131104 | tf_op jit(solution)/shard_map/ppermute | solution.py:477
  40.4 0.0 collective-permute-done.13.refs_2_
  40.4 0.0 collective-permute-done.14.got_key
  40.4 0.0 collective-permute-done.15.got_value
  40.4 0.8 %shard_map.114 = (bf16[128,512]{1,0:T(8,128)(2,1)}, bf16[128,512]{1,0:T(8,128)(2,1)}, bf16[64,512]{1,0:T(8,128)(2,1)}, bf16[64,512]{1,0:T(8,128)(2,1)}) custom-call(f32[128,512]{1,0:T(8,128)S(1)} %get-tuple-element.66.own_key, f32[128,512]{1,0:T(8,128)S(1)} %get-tuple-element.67.own_value, bf16[128,512]{1,0:T(8,128)(2,1)S(1)} %collective-permute-done.14.got_key, ...), custom_call_target="tpu_custom_call" | custom-call | flops 1048576 | bytes 4096 | tf_op jit(solution)/shard_map/pallas_call | solution.py:398
  (4 shorter events, 0.1 us)
Async XLA Ops:
  1.5 6.6 %collective-permute-start = (bf16[128,512]{1,0:T(8,128)(2,1)}, bf16[128,512]{1,0:T(8,128)(2,1)S(1)}, u32[]{:S(2)}, u32[]{:S(2)}) collective-permute-start(bf16[128,512]{1,0:T(8,128)(2,1)} %key_hbm.3), channel_id=1, source_target_pairs={{0,1},{1,0},{2,3},{3,2},{4,5},{5,4},{6,7},{7,6},{8,9},{9,8},{10,11... | collective-permute-start | bytes 393224 | tf_op jit(solution)/shard_map/ppermute | solution.py:431
  2.1 6.1 %collective-permute-start.1 = (bf16[128,512]{1,0:T(8,128)(2,1)}, bf16[128,512]{1,0:T(8,128)(2,1)S(1)}, u32[]{:S(2)}, u32[]{:S(2)}) collective-permute-start(bf16[128,512]{1,0:T(8,128)(2,1)} %value_hbm.1), channel_id=1, source_target_pairs={{0,1},{1,0},{2,3},{3,2},{4,5},{5,4},{6,7},{7,6},{8,9},{9,8},{10,11... | collective-permute-start | bytes 393224 | tf_op jit(solution)/shard_map/ppermute | solution.py:431
  2.1 11.4 %collective-permute-start.2 = (bf16[64,1024]{1,0:T(8,128)(2,1)S(1)}, bf16[64,1024]{1,0:T(8,128)(2,1)S(1)}, u32[]{:S(2)}, u32[]{:S(2)}) collective-permute-start(bf16[64,1024]{1,0:T(8,128)(2,1)S(1)} %pad_select_fusion), channel_id=1, source_target_pairs={{0,8},{4,12},{8,0},{12,4},{1,9},{5,13},{9,1},{13,5},{2,10},{6,14},... | collective-permute-start | bytes 393224 | tf_op jit(solution)/shard_map/ppermute | solution.py:430
  6.2 7.4 %collective-permute-start.6 = (bf16[64,1024]{1,0:T(8,128)(2,1)S(1)}, bf16[64,1024]{1,0:T(8,128)(2,1)S(1)}, u32[]{:S(2)}, u32[]{:S(2)}) collective-permute-start(bf16[64,1024]{1,0:T(8,128)(2,1)S(1)} %pad_select_fusion), channel_id=1, source_target_pairs={{0,12},{4,0},{8,4},{12,8},{1,13},{5,1},{9,5},{13,9},{2,14},{6,2},{... | collective-permute-start | bytes 393224 | tf_op jit(solution)/shard_map/ppermute | solution.py:430
  7.5 9.2 %collective-permute-start.3 = (bf16[64,1024]{1,0:T(8,128)(2,1)S(1)}, bf16[64,1024]{1,0:T(8,128)(2,1)S(1)}, u32[]{:S(2)}, u32[]{:S(2)}) collective-permute-start(bf16[64,1024]{1,0:T(8,128)(2,1)S(1)} %pad_select_fusion), channel_id=1, source_target_pairs={{0,4},{4,8},{8,12},{12,0},{1,5},{5,9},{9,13},{13,1},{2,6},{6,10},{... | collective-permute-start | bytes 393224 | tf_op jit(solution)/shard_map/ppermute | solution.py:430
  8.2 0.7 %copy-start = (s32[4]{0:T(128)S(1)}, s32[4]{0:T(128)}, u32[]{:S(2)}) copy-start(s32[4]{0:T(128)} %ratios.1) | copy-start | bytes 52
  13.6 3.7 %collective-permute-start.7 = (bf16[64,1024]{1,0:T(8,128)(2,1)S(1)}, bf16[64,1024]{1,0:T(8,128)(2,1)S(1)}, u32[]{:S(2)}, u32[]{:S(2)}) collective-permute-start(bf16[64,1024]{1,0:T(8,128)(2,1)S(1)} %collective-permute-done.6.refs_11_.refs_4_), channel_id=1, source_target_pairs={{0,1},{1,0},{2,3},{3,2},{4,5},{5,4},{6,7},{7,6},{8,9},{9,8},{10,11... | collective-permute-start | bytes 393224 | tf_op jit(solution)/shard_map/ppermute | solution.py:452
  16.7 1.3 %collective-permute-start.4 = (bf16[64,1024]{1,0:T(8,128)(2,1)S(1)}, bf16[64,1024]{1,0:T(8,128)(2,1)S(1)}, u32[]{:S(2)}, u32[]{:S(2)}) collective-permute-start(bf16[64,1024]{1,0:T(8,128)(2,1)S(1)} %collective-permute-done.3.refs_7_.refs_0_), channel_id=1, source_target_pairs={{0,1},{1,0},{2,3},{3,2},{4,5},{5,4},{6,7},{7,6},{8,9},{9,8},{10,11... | collective-permute-start | bytes 393224 | tf_op jit(solution)/shard_map/ppermute | solution.py:452
  16.7 1.5 %collective-permute-start.5 = (bf16[64,1024]{1,0:T(8,128)(2,1)S(1)}, bf16[64,1024]{1,0:T(8,128)(2,1)S(1)}, u32[]{:S(2)}, u32[]{:S(2)}) collective-permute-start(bf16[64,1024]{1,0:T(8,128)(2,1)S(1)} %collective-permute-done.2.refs_9_.refs_2_), channel_id=1, source_target_pairs={{0,1},{1,0},{2,3},{3,2},{4,5},{5,4},{6,7},{7,6},{8,9},{9,8},{10,11... | collective-permute-start | bytes 393224 | tf_op jit(solution)/shard_map/ppermute | solution.py:452
  19.5 1.4 %collective-permute-start.8 = (bf16[64,1024]{1,0:T(8,128)(2,1)S(1)}, bf16[64,1024]{1,0:T(8,128)(2,1)S(1)}, u32[]{:S(2)}, u32[]{:S(2)}) collective-permute-start(bf16[64,1024]{1,0:T(8,128)(2,1)S(1)} %get-tuple-element.54), channel_id=1, source_target_pairs={{0,1},{1,0},{2,3},{3,2},{4,5},{5,4},{6,7},{7,6},{8,9},{9,8},{10,11... | collective-permute-start | bytes 393224 | tf_op jit(solution)/shard_map/ppermute | solution.py:473
  19.9 9.4 %collective-permute-start.10 = (bf16[64,1024]{1,0:T(8,128)(2,1)S(1)}, bf16[64,1024]{1,0:T(8,128)(2,1)S(1)}, u32[]{:S(2)}, u32[]{:S(2)}) collective-permute-start(bf16[64,1024]{1,0:T(8,128)(2,1)S(1)} %get-tuple-element.56), channel_id=1, source_target_pairs={{0,1},{1,0},{2,3},{3,2},{4,5},{5,4},{6,7},{7,6},{8,9},{9,8},{10,11... | collective-permute-start | bytes 393224 | tf_op jit(solution)/shard_map/ppermute | solution.py:473
  20.1 9.4 %collective-permute-start.12 = (bf16[64,1024]{1,0:T(8,128)(2,1)S(1)}, bf16[64,1024]{1,0:T(8,128)(2,1)S(1)}, u32[]{:S(2)}, u32[]{:S(2)}) collective-permute-start(bf16[64,1024]{1,0:T(8,128)(2,1)S(1)} %get-tuple-element.58), channel_id=1, source_target_pairs={{0,1},{1,0},{2,3},{3,2},{4,5},{5,4},{6,7},{7,6},{8,9},{9,8},{10,11... | collective-permute-start | bytes 393224 | tf_op jit(solution)/shard_map/ppermute | solution.py:473
  20.9 15.7 %collective-permute-start.9 = (bf16[64,1024]{1,0:T(8,128)(2,1)S(1)}, bf16[64,1024]{1,0:T(8,128)(2,1)S(1)}, u32[]{:S(2)}, u32[]{:S(2)}) collective-permute-start(bf16[64,1024]{1,0:T(8,128)(2,1)S(1)} %add_convert_fusion.2), channel_id=1, source_target_pairs={{0,8},{4,12},{8,0},{12,4},{1,9},{5,13},{9,1},{13,5},{2,10},{6,14},... | collective-permute-start | bytes 393224 | tf_op jit(solution)/shard_map/ppermute | solution.py:477
  29.3 11.0 %collective-permute-start.11 = (bf16[64,1024]{1,0:T(8,128)(2,1)S(1)}, bf16[64,1024]{1,0:T(8,128)(2,1)S(1)}, u32[]{:S(2)}, u32[]{:S(2)}) collective-permute-start(bf16[64,1024]{1,0:T(8,128)(2,1)S(1)} %add_convert_fusion.1), channel_id=1, source_target_pairs={{0,12},{4,0},{8,4},{12,8},{1,13},{5,1},{9,5},{13,9},{2,14},{6,2},{... | collective-permute-start | bytes 393224 | tf_op jit(solution)/shard_map/ppermute | solution.py:477
  29.5 10.8 %collective-permute-start.13 = (bf16[64,1024]{1,0:T(8,128)(2,1)S(1)}, bf16[64,1024]{1,0:T(8,128)(2,1)S(1)}, u32[]{:S(2)}, u32[]{:S(2)}) collective-permute-start(bf16[64,1024]{1,0:T(8,128)(2,1)S(1)} %add_convert_fusion), channel_id=1, source_target_pairs={{0,4},{4,8},{8,12},{12,0},{1,5},{5,9},{9,13},{13,1},{2,6},{6,10},{... | collective-permute-start | bytes 393224 | tf_op jit(solution)/shard_map/ppermute | solution.py:477
  33.3 7.1 %collective-permute-start.14 = (bf16[128,512]{1,0:T(8,128)(2,1)S(1)}, bf16[128,512]{1,0:T(8,128)(2,1)S(1)}, u32[]{:S(2)}, u32[]{:S(2)}) collective-permute-start(bf16[128,512]{1,0:T(8,128)(2,1)S(1)} %get-tuple-element.68), channel_id=1, source_target_pairs={{0,1},{1,0},{2,3},{3,2},{4,5},{5,4},{6,7},{7,6},{8,9},{9,8},{10,11... | collective-permute-start | bytes 393224 | tf_op jit(solution)/shard_map/ppermute | solution.py:505
  33.3 7.0 %collective-permute-start.15 = (bf16[128,512]{1,0:T(8,128)(2,1)S(1)}, bf16[128,512]{1,0:T(8,128)(2,1)S(1)}, u32[]{:S(2)}, u32[]{:S(2)}) collective-permute-start(bf16[128,512]{1,0:T(8,128)(2,1)S(1)} %get-tuple-element.69), channel_id=1, source_target_pairs={{0,1},{1,0},{2,3},{3,2},{4,5},{5,4},{6,7},{7,6},{8,9},{9,8},{10,11... | collective-permute-start | bytes 393224 | tf_op jit(solution)/shard_map/ppermute | solution.py:505

commit v5 on v4

--- a/solution.py
+++ b/solution.py
@@ -474,7 +474,8 @@
 
     pairs = {k: pair(k) for k in order}
     pairs[order[-1]], delta = lax.optimization_barrier((pairs[order[-1]], delta))
-    sums = [lax.ppermute(pairs[k], "ctx", up(-k)) for k in order]
+    down = {k: up(-k) for k in order} | {last: [(last, 0)]}
+    sums = [lax.ppermute(pairs[k], "ctx", down[k]) for k in order]
     near_slopes, *near_grads = call(
         functools.partial(near_gradients_kernel, group),
         [q_in, g_in, near_stats[0], near_stats[1], share, delta],

time: 41.6 us -> 41.6 us (level)
  waiting for transfers between devices: 8.82 us -> 9.48 us
  starting transfers between devices: 19.3 us -> 18.7 us
    ppermute x3, starting transfers between devices: 10.7 us -> 10 us  [local(): sums = [lax.ppermute(pairs[k], 'ctx', down[k]) for k in order]]
    ppermute x3, waiting for transfers between devices: 3.67 us -> 4.33 us  [local(): sums = [lax.ppermute(pairs[k], 'ctx', down[k]) for k in order]]
  transfers between devices with their start and end apart: 16 -> 16, of which waited for: 6 -> 7; matrix products, arithmetic and copies ran while one was open for 0% -> 0% of each run, Pallas kernels for 21% -> 21%
where the time goes in v5:
time: 41.6 us; the launch traced here: 41.3 us
  starting transfers between devices  18.7 us (45%)
  Pallas kernels  10.7 us (26%)
  waiting for transfers between devices  9.48 us (23%)
  other arithmetic  0.99 us (2%)
  between operations  0.9 us (2%)
  local copies, waits for them, and re-layouts  0.65 us (2%)
    pallas_call x5, Pallas kernels, call(): pl.pallas_call(kernel, out_shape=[jax.ShapeDtypeStruct(*x) for x in outs]...  10.7 us
    ppermute x3, starting transfers between devices, local(): sums = [lax.ppermute(pairs[k], 'ctx', down[k]) for k in order]  10 us
    ppermute x3, starting transfers between devices, local(): own = {k: lax.ppermute(beacons, 'ctx', up(k)) for k in reversed(order)}  6.04 us
    ppermute x3, waiting for transfers between devices, local(): sums = [lax.ppermute(pairs[k], 'ctx', down[k]) for k in order]  4.33 us
    ppermute x3, waiting for transfers between devices, local(): own = {k: lax.ppermute(beacons, 'ctx', up(k)) for k in reversed(order)}  3.6 us
    ppermute x3, waiting for transfers between devices, local(): other = {k: lax.ppermute(own[k], 'sub', swap) for k in order}  1.02 us
    select_n x1, other arithmetic, local(): jnp.where(left, jnp.pad(beacon_keys, ((0, 0), (0, wide))), jnp.pad(beacon...  0.9 us
    ppermute x3, starting transfers between devices, pair(): lax.ppermute(sent[k], 'sub', swap).astype(f32)  0.9 us
  transfers between devices with their start and end apart: 16, of which 7 were waited for; matrix products, arithmetic and copies ran while one was open for 0% of the time, Pallas kernels for 21%

profile of v5, /device:TPU:0, one launch (start us, length us, event | category | flops | bytes accessed | tf_op | source)
XLA Modules:
  0.0 41.3 jit_solution(4591069213004074894)
XLA Ops:
  0.6 0.9 %pad_select_fusion = bf16[64,1024]{1,0:T(8,128)(2,1)S(1)} fusion(bf16[64,512]{1,0:T(8,128)(2,1)} %param.11, bf16[64,512]{1,0:T(8,128)(2,1)} %param.10, pred[1024]{0:T(1024)(128)(4,1)S(1)} %iota_compare_fusion), kind=kLoop, calls=%fused_computation.3 | loop fusion | flops 65536 | bytes 263168 | tf_op jit(solution)/shard_map/jit(_where)/select_n | solution.py:428
  1.5 0.5 %collective-permute-start = (bf16[128,512]{1,0:T(8,128)(2,1)}, bf16[128,512]{1,0:T(8,128)(2,1)S(1)}, u32[]{:S(2)}, u32[]{:S(2)}) collective-permute-start(bf16[128,512]{1,0:T(8,128)(2,1)} %key_hbm.3), channel_id=1, source_target_pairs={{0,1},{1,0},{2,3},{3,2},{4,5},{5,4},{6,7},{7,6},{8,9},{9,8},{10,11... | collective-permute-start | bytes 393224 | tf_op jit(solution)/shard_map/ppermute | solution.py:431
  2.1 0.1 collective-permute-start.1
  2.1 4.0 %collective-permute-start.2 = (bf16[64,1024]{1,0:T(8,128)(2,1)S(1)}, bf16[64,1024]{1,0:T(8,128)(2,1)S(1)}, u32[]{:S(2)}, u32[]{:S(2)}) collective-permute-start(bf16[64,1024]{1,0:T(8,128)(2,1)S(1)} %pad_select_fusion), channel_id=1, source_target_pairs={{0,8},{4,12},{8,0},{12,4},{1,9},{5,13},{9,1},{13,5},{2,10},{6,14},... | collective-permute-start | bytes 393224 | tf_op jit(solution)/shard_map/ppermute | solution.py:430
  6.2 1.3 %collective-permute-start.6 = (bf16[64,1024]{1,0:T(8,128)(2,1)S(1)}, bf16[64,1024]{1,0:T(8,128)(2,1)S(1)}, u32[]{:S(2)}, u32[]{:S(2)}) collective-permute-start(bf16[64,1024]{1,0:T(8,128)(2,1)S(1)} %pad_select_fusion), channel_id=1, source_target_pairs={{0,12},{4,0},{8,4},{12,8},{1,13},{5,1},{9,5},{13,9},{2,14},{6,2},{... | collective-permute-start | bytes 393224 | tf_op jit(solution)/shard_map/ppermute | solution.py:430
  7.5 0.7 %collective-permute-start.3 = (bf16[64,1024]{1,0:T(8,128)(2,1)S(1)}, bf16[64,1024]{1,0:T(8,128)(2,1)S(1)}, u32[]{:S(2)}, u32[]{:S(2)}) collective-permute-start(bf16[64,1024]{1,0:T(8,128)(2,1)S(1)} %pad_select_fusion), channel_id=1, source_target_pairs={{0,4},{4,8},{8,12},{12,0},{1,5},{5,9},{9,13},{13,1},{2,6},{6,10},{... | collective-permute-start | bytes 393224 | tf_op jit(solution)/shard_map/ppermute | solution.py:430
  8.2 0.0 collective-permute-done.other_key
  8.2 0.0 collective-permute-done.1.other_value
  8.2 0.0 copy-start
  8.2 0.7 %copy-done = s32[4]{0:T(128)S(1)} copy-done((s32[4]{0:T(128)S(1)}, s32[4]{0:T(128)}, u32[]{:S(2)}) %copy-start) | copy-done | bytes 40
  8.8 4.3 %shard_map.110 = (bf16[128,4096]{1,0:T(8,128)(2,1)S(1)}, bf16[128,4096]{1,0:T(8,128)(2,1)S(1)}, bf16[384,128]{1,0:T(8,128)(2,1)S(1)}, f32[8,256,512]{2,1,0:T(8,1...) custom-call(s32[4]{0:T(128)S(1)} %copy-done, bf16[128,4096]{1,0:T(8,128)(2,1)} %q_hbm.1, ...), custom_call_target="tpu_custom_call" | custom-call | flops 536870912 | bytes 2097152 | tf_op jit(solution)/shard_map/pallas_call | solution.py:398
  13.1 0.4 %collective-permute-done.2.refs_9_.refs_2_ = bf16[64,1024]{1,0:T(8,128)(2,1)S(1)} collective-permute-done((bf16[64,1024]{1,0:T(8,128)(2,1)S(1)}, bf16[64,1024]{1,0:T(8,128)(2,1)S(1)}, u32[]{:S(2)}, u32[]{:S(2)}) %collective-permute-start.2) | collective-permute-done | bytes 131104 | tf_op jit(solution)/shard_map/ppermute | solution.py:430
  13.6 0.0 collective-permute-done.6.refs_11_.refs_4_
  13.6 0.0 collective-permute-start.7
  13.6 3.2 %collective-permute-done.3.refs_7_.refs_0_ = bf16[64,1024]{1,0:T(8,128)(2,1)S(1)} collective-permute-done((bf16[64,1024]{1,0:T(8,128)(2,1)S(1)}, bf16[64,1024]{1,0:T(8,128)(2,1)S(1)}, u32[]{:S(2)}, u32[]{:S(2)}) %collective-permute-start.3) | collective-permute-done | bytes 131104 | tf_op jit(solution)/shard_map/ppermute | solution.py:430
  16.7 0.0 collective-permute-start.4
  16.7 0.5 %collective-permute-start.5 = (bf16[64,1024]{1,0:T(8,128)(2,1)S(1)}, bf16[64,1024]{1,0:T(8,128)(2,1)S(1)}, u32[]{:S(2)}, u32[]{:S(2)}) collective-permute-start(bf16[64,1024]{1,0:T(8,128)(2,1)S(1)} %collective-permute-done.2.refs_9_.refs_2_), channel_id=1, source_target_pairs={{0,1},{1,0},{2,3},{3,2},{4,5},{5,4},{6,7},{7,6},{8,9},{9,8},{10,11... | collective-permute-start | bytes 393224 | tf_op jit(solution)/shard_map/ppermute | solution.py:452
  17.2 0.0 collective-permute-done.7.refs_12_.refs_5_
  17.2 0.8 %collective-permute-done.4.refs_8_.refs_1_ = bf16[64,1024]{1,0:T(8,128)(2,1)S(1)} collective-permute-done((bf16[64,1024]{1,0:T(8,128)(2,1)S(1)}, bf16[64,1024]{1,0:T(8,128)(2,1)S(1)}, u32[]{:S(2)}, u32[]{:S(2)}) %collective-permute-start.4) | collective-permute-done | bytes 131104 | tf_op jit(solution)/shard_map/ppermute | solution.py:452
  18.1 0.2 collective-permute-done.5.refs_10_.refs_3_
  18.3 1.2 %shard_map.111 = (f32[8,8,512]{2,1,0:T(8,128)S(1)}, f32[8,8,512]{2,1,0:T(8,128)S(1)}, bf16[8,384,512]{2,1,0:T(8,128)(2,1)S(1)}, f32[64,1024]{1,0:T(8,128)S(1)}, ...) custom-call(bf16[128,4096]{1,0:T(8,128)(2,1)S(1)} %get-tuple-element, ...), custom_call_target="tpu_custom_call" | custom-call | flops 1610612736 | bytes 6291456 | tf_op jit(solution)/shard_map/pallas_call | solution.py:398
  19.5 0.4 collective-permute-start.8
  19.9 0.2 collective-permute-start.10
  20.1 0.3 collective-permute-start.12
  20.4 0.5 %collective-permute-done.8 = bf16[64,1024]{1,0:T(8,128)(2,1)S(1)} collective-permute-done((bf16[64,1024]{1,0:T(8,128)(2,1)S(1)}, bf16[64,1024]{1,0:T(8,128)(2,1)S(1)}, u32[]{:S(2)}, u32[]{:S(2)}) %collective-permute-start.8) | collective-permute-done | bytes 131104 | tf_op jit(solution)/shard_map/ppermute | solution.py:473
  20.9 8.4 %collective-permute-start.9 = (bf16[64,1024]{1,0:T(8,128)(2,1)S(1)}, bf16[64,1024]{1,0:T(8,128)(2,1)S(1)}, u32[]{:S(2)}, u32[]{:S(2)}) collective-permute-start(bf16[64,1024]{1,0:T(8,128)(2,1)S(1)} %add_convert_fusion.2), channel_id=1, source_target_pairs={{0,8},{4,12},{8,0},{12,4},{1,9},{5,13},{9,1},{13,5},{2,10},{6,14},... | collective-permute-start | bytes 393224 | tf_op jit(solution)/shard_map/ppermute | solution.py:478
  29.3 0.0 collective-permute-done.10
  29.3 0.2 collective-permute-start.11
  29.5 0.0 collective-permute-done.12
  29.5 1.5 %collective-permute-start.13 = (bf16[64,1024]{1,0:T(8,128)(2,1)S(1)}, bf16[64,1024]{1,0:T(8,128)(2,1)S(1)}, u32[]{:S(2)}, u32[]{:S(2)}) collective-permute-start(bf16[64,1024]{1,0:T(8,128)(2,1)S(1)} %add_convert_fusion), channel_id=1, source_target_pairs={{12,0},{13,1},{14,2},{15,3},{28,16},{29,17},{30,18},{31,19}} | collective-permute-start | bytes 393224 | tf_op jit(solution)/shard_map/ppermute | solution.py:478
  31.1 1.5 %shard_map.112 = (bf16[8,256,512]{2,1,0:T(8,128)(2,1)S(1)}, f32[128,512]{1,0:T(8,128)S(1)}, f32[128,512]{1,0:T(8,128)S(1)}, bf16[128,512]{1,0:T(8,128)(2,1)S(1)}, bf16[128,512]{1,0:T(8,128)(2,1)S(1)}) custom-call(bf16[128,4096]{1,0:T(8,128)(2,1)S(1)} %get-tuple-element.43.refs_0_.q_buf, bf16[128,4096]{1,0:T(8,128)(2,1)S(1)} %get-tuple-element.44.refs_1_.g_buf, ...), custom_call_target="tpu_custom_call" | custom-call | flops 1048576 | bytes 4096 | tf_op jit(solution)/shard_map/pallas_call | solution.py:398
  32.6 0.1 collective-permute-start.14
  32.7 0.5 %collective-permute-start.15 = (bf16[128,512]{1,0:T(8,128)(2,1)S(1)}, bf16[128,512]{1,0:T(8,128)(2,1)S(1)}, u32[]{:S(2)}, u32[]{:S(2)}) collective-permute-start(bf16[128,512]{1,0:T(8,128)(2,1)S(1)} %get-tuple-element.69), channel_id=1, source_target_pairs={{0,1},{1,0},{2,3},{3,2},{4,5},{5,4},{6,7},{7,6},{8,9},{9,8},{10,11... | collective-permute-start | bytes 393224 | tf_op jit(solution)/shard_map/ppermute | solution.py:506
  33.2 2.8 %shard_map.113 = bf16[128,4096]{1,0:T(8,128)(2,1)} custom-call(bf16[8,256,512]{2,1,0:T(8,128)(2,1)S(1)} %get-tuple-element.63.near_slopes, bf16[8,384,512]{2,1,0:T(8,128)(2,1)S(1)} %get-tuple-element.64.far_slopes, bf16[128,512]{1,0:T(8,128)(2,1)} %key_hbm.3, bf16[128,512]{1,0:T(8,128)(2,1)S(1)} %collective-permute-done.other_key, ...), custom_call_target="tpu_custom_call" | custom-call | flops 1048576 | bytes 4096 | tf_op jit(solution)/shard_map/pallas_call | solution.py:398
  36.0 0.2 collective-permute-done.9.refs_0_
  36.2 4.1 %collective-permute-done.11.refs_1_ = bf16[64,1024]{1,0:T(8,128)(2,1)S(1)} collective-permute-done((bf16[64,1024]{1,0:T(8,128)(2,1)S(1)}, bf16[64,1024]{1,0:T(8,128)(2,1)S(1)}, u32[]{:S(2)}, u32[]{:S(2)}) %collective-permute-start.11) | collective-permute-done | bytes 131104 | tf_op jit(solution)/shard_map/ppermute | solution.py:478
  40.4 0.0 collective-permute-done.13.refs_2_
  40.4 0.0 collective-permute-done.14.got_key
  40.4 0.0 collective-permute-done.15.got_value
  40.4 0.8 %shard_map.114 = (bf16[128,512]{1,0:T(8,128)(2,1)}, bf16[128,512]{1,0:T(8,128)(2,1)}, bf16[64,512]{1,0:T(8,128)(2,1)}, bf16[64,512]{1,0:T(8,128)(2,1)}) custom-call(f32[128,512]{1,0:T(8,128)S(1)} %get-tuple-element.66.own_key, f32[128,512]{1,0:T(8,128)S(1)} %get-tuple-element.67.own_value, bf16[128,512]{1,0:T(8,128)(2,1)S(1)} %collective-permute-done.14.got_key, ...), custom_call_target="tpu_custom_call" | custom-call | flops 1048576 | bytes 4096 | tf_op jit(solution)/shard_map/pallas_call | solution.py:398
  (4 shorter events, 0.1 us)
Async XLA Ops:
  1.5 6.6 %collective-permute-start = (bf16[128,512]{1,0:T(8,128)(2,1)}, bf16[128,512]{1,0:T(8,128)(2,1)S(1)}, u32[]{:S(2)}, u32[]{:S(2)}) collective-permute-start(bf16[128,512]{1,0:T(8,128)(2,1)} %key_hbm.3), channel_id=1, source_target_pairs={{0,1},{1,0},{2,3},{3,2},{4,5},{5,4},{6,7},{7,6},{8,9},{9,8},{10,11... | collective-permute-start | bytes 393224 | tf_op jit(solution)/shard_map/ppermute | solution.py:431
  2.1 6.1 %collective-permute-start.1 = (bf16[128,512]{1,0:T(8,128)(2,1)}, bf16[128,512]{1,0:T(8,128)(2,1)S(1)}, u32[]{:S(2)}, u32[]{:S(2)}) collective-permute-start(bf16[128,512]{1,0:T(8,128)(2,1)} %value_hbm.1), channel_id=1, source_target_pairs={{0,1},{1,0},{2,3},{3,2},{4,5},{5,4},{6,7},{7,6},{8,9},{9,8},{10,11... | collective-permute-start | bytes 393224 | tf_op jit(solution)/shard_map/ppermute | solution.py:431
  2.1 11.4 %collective-permute-start.2 = (bf16[64,1024]{1,0:T(8,128)(2,1)S(1)}, bf16[64,1024]{1,0:T(8,128)(2,1)S(1)}, u32[]{:S(2)}, u32[]{:S(2)}) collective-permute-start(bf16[64,1024]{1,0:T(8,128)(2,1)S(1)} %pad_select_fusion), channel_id=1, source_target_pairs={{0,8},{4,12},{8,0},{12,4},{1,9},{5,13},{9,1},{13,5},{2,10},{6,14},... | collective-permute-start | bytes 393224 | tf_op jit(solution)/shard_map/ppermute | solution.py:430
  6.2 7.4 %collective-permute-start.6 = (bf16[64,1024]{1,0:T(8,128)(2,1)S(1)}, bf16[64,1024]{1,0:T(8,128)(2,1)S(1)}, u32[]{:S(2)}, u32[]{:S(2)}) collective-permute-start(bf16[64,1024]{1,0:T(8,128)(2,1)S(1)} %pad_select_fusion), channel_id=1, source_target_pairs={{0,12},{4,0},{8,4},{12,8},{1,13},{5,1},{9,5},{13,9},{2,14},{6,2},{... | collective-permute-start | bytes 393224 | tf_op jit(solution)/shard_map/ppermute | solution.py:430
  7.5 9.2 %collective-permute-start.3 = (bf16[64,1024]{1,0:T(8,128)(2,1)S(1)}, bf16[64,1024]{1,0:T(8,128)(2,1)S(1)}, u32[]{:S(2)}, u32[]{:S(2)}) collective-permute-start(bf16[64,1024]{1,0:T(8,128)(2,1)S(1)} %pad_select_fusion), channel_id=1, source_target_pairs={{0,4},{4,8},{8,12},{12,0},{1,5},{5,9},{9,13},{13,1},{2,6},{6,10},{... | collective-permute-start | bytes 393224 | tf_op jit(solution)/shard_map/ppermute | solution.py:430
  8.2 0.7 %copy-start = (s32[4]{0:T(128)S(1)}, s32[4]{0:T(128)}, u32[]{:S(2)}) copy-start(s32[4]{0:T(128)} %ratios.1) | copy-start | bytes 52
  13.6 3.7 %collective-permute-start.7 = (bf16[64,1024]{1,0:T(8,128)(2,1)S(1)}, bf16[64,1024]{1,0:T(8,128)(2,1)S(1)}, u32[]{:S(2)}, u32[]{:S(2)}) collective-permute-start(bf16[64,1024]{1,0:T(8,128)(2,1)S(1)} %collective-permute-done.6.refs_11_.refs_4_), channel_id=1, source_target_pairs={{0,1},{1,0},{2,3},{3,2},{4,5},{5,4},{6,7},{7,6},{8,9},{9,8},{10,11... | collective-permute-start | bytes 393224 | tf_op jit(solution)/shard_map/ppermute | solution.py:452
  16.7 1.3 %collective-permute-start.4 = (bf16[64,1024]{1,0:T(8,128)(2,1)S(1)}, bf16[64,1024]{1,0:T(8,128)(2,1)S(1)}, u32[]{:S(2)}, u32[]{:S(2)}) collective-permute-start(bf16[64,1024]{1,0:T(8,128)(2,1)S(1)} %collective-permute-done.3.refs_7_.refs_0_), channel_id=1, source_target_pairs={{0,1},{1,0},{2,3},{3,2},{4,5},{5,4},{6,7},{7,6},{8,9},{9,8},{10,11... | collective-permute-start | bytes 393224 | tf_op jit(solution)/shard_map/ppermute | solution.py:452
  16.7 1.5 %collective-permute-start.5 = (bf16[64,1024]{1,0:T(8,128)(2,1)S(1)}, bf16[64,1024]{1,0:T(8,128)(2,1)S(1)}, u32[]{:S(2)}, u32[]{:S(2)}) collective-permute-start(bf16[64,1024]{1,0:T(8,128)(2,1)S(1)} %collective-permute-done.2.refs_9_.refs_2_), channel_id=1, source_target_pairs={{0,1},{1,0},{2,3},{3,2},{4,5},{5,4},{6,7},{7,6},{8,9},{9,8},{10,11... | collective-permute-start | bytes 393224 | tf_op jit(solution)/shard_map/ppermute | solution.py:452
  19.5 1.4 %collective-permute-start.8 = (bf16[64,1024]{1,0:T(8,128)(2,1)S(1)}, bf16[64,1024]{1,0:T(8,128)(2,1)S(1)}, u32[]{:S(2)}, u32[]{:S(2)}) collective-permute-start(bf16[64,1024]{1,0:T(8,128)(2,1)S(1)} %get-tuple-element.54), channel_id=1, source_target_pairs={{0,1},{1,0},{2,3},{3,2},{4,5},{5,4},{6,7},{7,6},{8,9},{9,8},{10,11... | collective-permute-start | bytes 393224 | tf_op jit(solution)/shard_map/ppermute | solution.py:473
  19.9 9.4 %collective-permute-start.10 = (bf16[64,1024]{1,0:T(8,128)(2,1)S(1)}, bf16[64,1024]{1,0:T(8,128)(2,1)S(1)}, u32[]{:S(2)}, u32[]{:S(2)}) collective-permute-start(bf16[64,1024]{1,0:T(8,128)(2,1)S(1)} %get-tuple-element.56), channel_id=1, source_target_pairs={{0,1},{1,0},{2,3},{3,2},{4,5},{5,4},{6,7},{7,6},{8,9},{9,8},{10,11... | collective-permute-start | bytes 393224 | tf_op jit(solution)/shard_map/ppermute | solution.py:473
  20.1 9.4 %collective-permute-start.12 = (bf16[64,1024]{1,0:T(8,128)(2,1)S(1)}, bf16[64,1024]{1,0:T(8,128)(2,1)S(1)}, u32[]{:S(2)}, u32[]{:S(2)}) collective-permute-start(bf16[64,1024]{1,0:T(8,128)(2,1)S(1)} %get-tuple-element.58), channel_id=1, source_target_pairs={{0,1},{1,0},{2,3},{3,2},{4,5},{5,4},{6,7},{7,6},{8,9},{9,8},{10,11... | collective-permute-start | bytes 393224 | tf_op jit(solution)/shard_map/ppermute | solution.py:473
  20.9 15.3 %collective-permute-start.9 = (bf16[64,1024]{1,0:T(8,128)(2,1)S(1)}, bf16[64,1024]{1,0:T(8,128)(2,1)S(1)}, u32[]{:S(2)}, u32[]{:S(2)}) collective-permute-start(bf16[64,1024]{1,0:T(8,128)(2,1)S(1)} %add_convert_fusion.2), channel_id=1, source_target_pairs={{0,8},{4,12},{8,0},{12,4},{1,9},{5,13},{9,1},{13,5},{2,10},{6,14},... | collective-permute-start | bytes 393224 | tf_op jit(solution)/shard_map/ppermute | solution.py:478
  29.3 11.0 %collective-permute-start.11 = (bf16[64,1024]{1,0:T(8,128)(2,1)S(1)}, bf16[64,1024]{1,0:T(8,128)(2,1)S(1)}, u32[]{:S(2)}, u32[]{:S(2)}) collective-permute-start(bf16[64,1024]{1,0:T(8,128)(2,1)S(1)} %add_convert_fusion.1), channel_id=1, source_target_pairs={{0,12},{4,0},{8,4},{12,8},{1,13},{5,1},{9,5},{13,9},{2,14},{6,2},{... | collective-permute-start | bytes 393224 | tf_op jit(solution)/shard_map/ppermute | solution.py:478
  29.5 10.8 %collective-permute-start.13 = (bf16[64,1024]{1,0:T(8,128)(2,1)S(1)}, bf16[64,1024]{1,0:T(8,128)(2,1)S(1)}, u32[]{:S(2)}, u32[]{:S(2)}) collective-permute-start(bf16[64,1024]{1,0:T(8,128)(2,1)S(1)} %add_convert_fusion), channel_id=1, source_target_pairs={{12,0},{13,1},{14,2},{15,3},{28,16},{29,17},{30,18},{31,19}} | collective-permute-start | bytes 393224 | tf_op jit(solution)/shard_map/ppermute | solution.py:478
  32.6 7.8 %collective-permute-start.14 = (bf16[128,512]{1,0:T(8,128)(2,1)S(1)}, bf16[128,512]{1,0:T(8,128)(2,1)S(1)}, u32[]{:S(2)}, u32[]{:S(2)}) collective-permute-start(bf16[128,512]{1,0:T(8,128)(2,1)S(1)} %get-tuple-element.68), channel_id=1, source_target_pairs={{0,1},{1,0},{2,3},{3,2},{4,5},{5,4},{6,7},{7,6},{8,9},{9,8},{10,11... | collective-permute-start | bytes 393224 | tf_op jit(solution)/shard_map/ppermute | solution.py:506
  32.7 7.7 %collective-permute-start.15 = (bf16[128,512]{1,0:T(8,128)(2,1)S(1)}, bf16[128,512]{1,0:T(8,128)(2,1)S(1)}, u32[]{:S(2)}, u32[]{:S(2)}) collective-permute-start(bf16[128,512]{1,0:T(8,128)(2,1)S(1)} %get-tuple-element.69), channel_id=1, source_target_pairs={{0,1},{1,0},{2,3},{3,2},{4,5},{5,4},{6,7},{7,6},{8,9},{9,8},{10,11... | collective-permute-start | bytes 393224 | tf_op jit(solution)/shard_map/ppermute | solution.py:506

commit v6 on v5

--- a/solution.py
+++ b/solution.py
@@ -449,7 +449,11 @@
     )
     first = order[0]
     own[first], near_stats[2] = lax.optimization_barrier((own[first], near_stats[2]))
-    other = {k: lax.ppermute(own[k], "sub", swap) for k in order}
+    other = {k: lax.ppermute(own[k], "sub", swap) for k in {first, last}}
+    middle = [k for k in order if k not in other]
+    kept, other[first] = lax.optimization_barrier(([own[k] for k in middle], other[first]))
+    own |= dict(zip(middle, kept))
+    other |= {k: lax.ppermute(own[k], "sub", swap) for k in middle}
     far = [x[k] for k in shifts for x in (own, other)]
     sets = [vmem((columns, width), f32)] * 2 + [vmem((columns, width), bf16)]
     share, delta, far_slopes, *grads = call(

time: 41.6 us -> 40.9 us (0.983)
  waiting for transfers between devices: 9.48 us -> 8.01 us
  starting transfers between devices: 18.7 us -> 19.5 us
    ppermute x3, waiting for transfers between devices: 4.33 us -> 2.87 us  [local(): sums = [lax.ppermute(pairs[k], 'ctx', down[k]) for k in order]]
    ppermute x3, starting transfers between devices: 10 us -> 11 us  [local(): sums = [lax.ppermute(pairs[k], 'ctx', down[k]) for k in order]]
    ppermute x3, waiting for transfers between devices: 3.6 us -> 3.09 us  [local(): own = {k: lax.ppermute(beacons, 'ctx', up(k)) for k in reversed(order)}]
  transfers between devices with their start and end apart: 16 -> 16, of which waited for: 7 -> 5; matrix products, arithmetic and copies ran while one was open for 0% -> 0% of each run, Pallas kernels for 21% -> 21%
where the time goes in v6:
time: 40.9 us; the launch traced here: 40.7 us
  starting transfers between devices  19.5 us (48%)
  Pallas kernels  10.7 us (26%)
  waiting for transfers between devices  8.01 us (20%)
  other arithmetic  0.99 us (2%)
  between operations  0.91 us (2%)
  local copies, waits for them, and re-layouts  0.65 us (2%)
    ppermute x3, starting transfers between devices, local(): sums = [lax.ppermute(pairs[k], 'ctx', down[k]) for k in order]  11 us
    pallas_call x5, Pallas kernels, call(): pl.pallas_call(kernel, out_shape=[jax.ShapeDtypeStruct(*x) for x in outs]...  10.7 us
    ppermute x3, starting transfers between devices, local(): own = {k: lax.ppermute(beacons, 'ctx', up(k)) for k in reversed(order)}  6.04 us
    ppermute x3, waiting for transfers between devices, local(): own = {k: lax.ppermute(beacons, 'ctx', up(k)) for k in reversed(order)}  3.09 us
    ppermute x3, waiting for transfers between devices, local(): sums = [lax.ppermute(pairs[k], 'ctx', down[k]) for k in order]  2.87 us
    ppermute x1, waiting for transfers between devices, local(): other |= {k: lax.ppermute(own[k], 'sub', swap) for k in middle}  1.34 us
    select_n x1, other arithmetic, local(): jnp.where(left, jnp.pad(beacon_keys, ((0, 0), (0, wide))), jnp.pad(beacon...  0.9 us
  transfers between devices with their start and end apart: 16, of which 5 were waited for; matrix products, arithmetic and copies ran while one was open for 0% of the time, Pallas kernels for 21%

profile of v6, /device:TPU:0, one launch (start us, length us, event | category | flops | bytes accessed | tf_op | source)
XLA Modules:
  0.0 40.7 jit_solution(18273978688864964658)
XLA Ops:
  0.6 0.9 %pad_select_fusion = bf16[64,1024]{1,0:T(8,128)(2,1)S(1)} fusion(bf16[64,512]{1,0:T(8,128)(2,1)} %param.11, bf16[64,512]{1,0:T(8,128)(2,1)} %param.10, pred[1024]{0:T(1024)(128)(4,1)S(1)} %iota_compare_fusion), kind=kLoop, calls=%fused_computation.3 | loop fusion | flops 65536 | bytes 263168 | tf_op jit(solution)/shard_map/jit(_where)/select_n | solution.py:428
  1.5 0.5 %collective-permute-start = (bf16[128,512]{1,0:T(8,128)(2,1)}, bf16[128,512]{1,0:T(8,128)(2,1)S(1)}, u32[]{:S(2)}, u32[]{:S(2)}) collective-permute-start(bf16[128,512]{1,0:T(8,128)(2,1)} %key_hbm.3), channel_id=1, source_target_pairs={{0,1},{1,0},{2,3},{3,2},{4,5},{5,4},{6,7},{7,6},{8,9},{9,8},{10,11... | collective-permute-start | bytes 393224 | tf_op jit(solution)/shard_map/ppermute | solution.py:431
  2.1 0.1 collective-permute-start.1
  2.1 4.0 %collective-permute-start.2 = (bf16[64,1024]{1,0:T(8,128)(2,1)S(1)}, bf16[64,1024]{1,0:T(8,128)(2,1)S(1)}, u32[]{:S(2)}, u32[]{:S(2)}) collective-permute-start(bf16[64,1024]{1,0:T(8,128)(2,1)S(1)} %pad_select_fusion), channel_id=1, source_target_pairs={{0,8},{4,12},{8,0},{12,4},{1,9},{5,13},{9,1},{13,5},{2,10},{6,14},... | collective-permute-start | bytes 393224 | tf_op jit(solution)/shard_map/ppermute | solution.py:430
  6.2 1.3 %collective-permute-start.6 = (bf16[64,1024]{1,0:T(8,128)(2,1)S(1)}, bf16[64,1024]{1,0:T(8,128)(2,1)S(1)}, u32[]{:S(2)}, u32[]{:S(2)}) collective-permute-start(bf16[64,1024]{1,0:T(8,128)(2,1)S(1)} %pad_select_fusion), channel_id=1, source_target_pairs={{0,12},{4,0},{8,4},{12,8},{1,13},{5,1},{9,5},{13,9},{2,14},{6,2},{... | collective-permute-start | bytes 393224 | tf_op jit(solution)/shard_map/ppermute | solution.py:430
  7.5 0.7 %collective-permute-start.3 = (bf16[64,1024]{1,0:T(8,128)(2,1)S(1)}, bf16[64,1024]{1,0:T(8,128)(2,1)S(1)}, u32[]{:S(2)}, u32[]{:S(2)}) collective-permute-start(bf16[64,1024]{1,0:T(8,128)(2,1)S(1)} %pad_select_fusion), channel_id=1, source_target_pairs={{0,4},{4,8},{8,12},{12,0},{1,5},{5,9},{9,13},{13,1},{2,6},{6,10},{... | collective-permute-start | bytes 393224 | tf_op jit(solution)/shard_map/ppermute | solution.py:430
  8.2 0.0 collective-permute-done.other_key
  8.2 0.0 collective-permute-done.1.other_value
  8.2 0.0 copy-start
  8.2 0.7 %copy-done = s32[4]{0:T(128)S(1)} copy-done((s32[4]{0:T(128)S(1)}, s32[4]{0:T(128)}, u32[]{:S(2)}) %copy-start) | copy-done | bytes 40
  8.8 4.3 %shard_map.110 = (bf16[128,4096]{1,0:T(8,128)(2,1)S(1)}, bf16[128,4096]{1,0:T(8,128)(2,1)S(1)}, bf16[384,128]{1,0:T(8,128)(2,1)S(1)}, f32[8,256,512]{2,1,0:T(8,1...) custom-call(s32[4]{0:T(128)S(1)} %copy-done, bf16[128,4096]{1,0:T(8,128)(2,1)} %q_hbm.1, ...), custom_call_target="tpu_custom_call" | custom-call | flops 536870912 | bytes 2097152 | tf_op jit(solution)/shard_map/pallas_call | solution.py:398
  13.1 0.4 %collective-permute-done.2.refs_9_.refs_2_ = bf16[64,1024]{1,0:T(8,128)(2,1)S(1)} collective-permute-done((bf16[64,1024]{1,0:T(8,128)(2,1)S(1)}, bf16[64,1024]{1,0:T(8,128)(2,1)S(1)}, u32[]{:S(2)}, u32[]{:S(2)}) %collective-permute-start.2) | collective-permute-done | bytes 131104 | tf_op jit(solution)/shard_map/ppermute | solution.py:430
  13.6 0.0 collective-permute-start.4
  13.6 0.0 collective-permute-done.6.refs_11_.refs_4_
  13.6 0.5 %collective-permute-start.7 = (bf16[64,1024]{1,0:T(8,128)(2,1)S(1)}, bf16[64,1024]{1,0:T(8,128)(2,1)S(1)}, u32[]{:S(2)}, u32[]{:S(2)}) collective-permute-start(bf16[64,1024]{1,0:T(8,128)(2,1)S(1)} %collective-permute-done.6.refs_11_.refs_4_), channel_id=1, source_target_pairs={{0,1},{1,0},{2,3},{3,2},{4,5},{5,4},{6,7},{7,6},{8,9},{9,8},{10,11... | collective-permute-start | bytes 393224 | tf_op jit(solution)/shard_map/ppermute | solution.py:452
  14.1 2.6 %collective-permute-done.3.refs_7_.refs_0_ = bf16[64,1024]{1,0:T(8,128)(2,1)S(1)} collective-permute-done((bf16[64,1024]{1,0:T(8,128)(2,1)S(1)}, bf16[64,1024]{1,0:T(8,128)(2,1)S(1)}, u32[]{:S(2)}, u32[]{:S(2)}) %collective-permute-start.3) | collective-permute-done | bytes 131104 | tf_op jit(solution)/shard_map/ppermute | solution.py:430
  16.7 0.0 collective-permute-done.4.refs_10_.refs_3_
  16.7 0.0 collective-permute-start.5
  16.7 0.0 collective-permute-done.7.refs_12_.refs_5_
  16.7 1.3 %collective-permute-done.5.refs_8_.refs_1_ = bf16[64,1024]{1,0:T(8,128)(2,1)S(1)} collective-permute-done((bf16[64,1024]{1,0:T(8,128)(2,1)S(1)}, bf16[64,1024]{1,0:T(8,128)(2,1)S(1)}, u32[]{:S(2)}, u32[]{:S(2)}) %collective-permute-start.5) | collective-permute-done | bytes 131104 | tf_op jit(solution)/shard_map/ppermute | solution.py:456
  18.1 1.2 %shard_map.111 = (f32[8,8,512]{2,1,0:T(8,128)S(1)}, f32[8,8,512]{2,1,0:T(8,128)S(1)}, bf16[8,384,512]{2,1,0:T(8,128)(2,1)S(1)}, f32[64,1024]{1,0:T(8,128)S(1)}, ...) custom-call(bf16[128,4096]{1,0:T(8,128)(2,1)S(1)} %get-tuple-element, ...), custom_call_target="tpu_custom_call" | custom-call | flops 1610612736 | bytes 6291456 | tf_op jit(solution)/shard_map/pallas_call | solution.py:398
  19.3 0.2 collective-permute-start.8
  19.5 0.4 collective-permute-start.10
  19.9 0.1 collective-permute-start.12
  20.0 0.7 %collective-permute-done.8 = bf16[64,1024]{1,0:T(8,128)(2,1)S(1)} collective-permute-done((bf16[64,1024]{1,0:T(8,128)(2,1)S(1)}, bf16[64,1024]{1,0:T(8,128)(2,1)S(1)}, u32[]{:S(2)}, u32[]{:S(2)}) %collective-permute-start.8) | collective-permute-done | bytes 131104 | tf_op jit(solution)/shard_map/ppermute | solution.py:477
  20.8 8.4 %collective-permute-start.9 = (bf16[64,1024]{1,0:T(8,128)(2,1)S(1)}, bf16[64,1024]{1,0:T(8,128)(2,1)S(1)}, u32[]{:S(2)}, u32[]{:S(2)}) collective-permute-start(bf16[64,1024]{1,0:T(8,128)(2,1)S(1)} %add_convert_fusion.2), channel_id=1, source_target_pairs={{0,8},{4,12},{8,0},{12,4},{1,9},{5,13},{9,1},{13,5},{2,10},{6,14},... | collective-permute-start | bytes 393224 | tf_op jit(solution)/shard_map/ppermute | solution.py:482
  29.1 0.0 collective-permute-done.10
  29.1 1.1 %collective-permute-start.11 = (bf16[64,1024]{1,0:T(8,128)(2,1)S(1)}, bf16[64,1024]{1,0:T(8,128)(2,1)S(1)}, u32[]{:S(2)}, u32[]{:S(2)}) collective-permute-start(bf16[64,1024]{1,0:T(8,128)(2,1)S(1)} %add_convert_fusion.1), channel_id=1, source_target_pairs={{0,12},{4,0},{8,4},{12,8},{1,13},{5,1},{9,5},{13,9},{2,14},{6,2},{... | collective-permute-start | bytes 393224 | tf_op jit(solution)/shard_map/ppermute | solution.py:482
  30.3 0.0 collective-permute-done.12
  30.3 1.5 %collective-permute-start.13 = (bf16[64,1024]{1,0:T(8,128)(2,1)S(1)}, bf16[64,1024]{1,0:T(8,128)(2,1)S(1)}, u32[]{:S(2)}, u32[]{:S(2)}) collective-permute-start(bf16[64,1024]{1,0:T(8,128)(2,1)S(1)} %add_convert_fusion), channel_id=1, source_target_pairs={{12,0},{13,1},{14,2},{15,3},{28,16},{29,17},{30,18},{31,19}} | collective-permute-start | bytes 393224 | tf_op jit(solution)/shard_map/ppermute | solution.py:482
  31.8 1.5 %shard_map.112 = (bf16[8,256,512]{2,1,0:T(8,128)(2,1)S(1)}, f32[128,512]{1,0:T(8,128)S(1)}, f32[128,512]{1,0:T(8,128)S(1)}, bf16[128,512]{1,0:T(8,128)(2,1)S(1)}, bf16[128,512]{1,0:T(8,128)(2,1)S(1)}) custom-call(bf16[128,4096]{1,0:T(8,128)(2,1)S(1)} %get-tuple-element.45.refs_0_.q_buf, bf16[128,4096]{1,0:T(8,128)(2,1)S(1)} %get-tuple-element.46.refs_1_.g_buf, ...), custom_call_target="tpu_custom_call" | custom-call | flops 1048576 | bytes 4096 | tf_op jit(solution)/shard_map/pallas_call | solution.py:398
  33.4 0.1 collective-permute-start.14
  33.5 0.5 %collective-permute-start.15 = (bf16[128,512]{1,0:T(8,128)(2,1)S(1)}, bf16[128,512]{1,0:T(8,128)(2,1)S(1)}, u32[]{:S(2)}, u32[]{:S(2)}) collective-permute-start(bf16[128,512]{1,0:T(8,128)(2,1)S(1)} %get-tuple-element.73), channel_id=1, source_target_pairs={{0,1},{1,0},{2,3},{3,2},{4,5},{5,4},{6,7},{7,6},{8,9},{9,8},{10,11... | collective-permute-start | bytes 393224 | tf_op jit(solution)/shard_map/ppermute | solution.py:510
  34.0 2.8 %shard_map.113 = bf16[128,4096]{1,0:T(8,128)(2,1)} custom-call(bf16[8,256,512]{2,1,0:T(8,128)(2,1)S(1)} %get-tuple-element.67.near_slopes, bf16[8,384,512]{2,1,0:T(8,128)(2,1)S(1)} %get-tuple-element.68.far_slopes, bf16[128,512]{1,0:T(8,128)(2,1)} %key_hbm.3, bf16[128,512]{1,0:T(8,128)(2,1)S(1)} %collective-permute-done.other_key, ...), custom_call_target="tpu_custom_call" | custom-call | flops 1048576 | bytes 4096 | tf_op jit(solution)/shard_map/pallas_call | solution.py:398
  36.8 0.0 collective-permute-done.9.refs_0_
  36.8 0.0 collective-permute-done.11.refs_1_
  36.8 2.9 %collective-permute-done.13.refs_2_ = bf16[64,1024]{1,0:T(8,128)(2,1)S(1)} collective-permute-done((bf16[64,1024]{1,0:T(8,128)(2,1)S(1)}, bf16[64,1024]{1,0:T(8,128)(2,1)S(1)}, u32[]{:S(2)}, u32[]{:S(2)}) %collective-permute-start.13) | collective-permute-done | bytes 131104 | tf_op jit(solution)/shard_map/ppermute | solution.py:482
  39.7 0.0 collective-permute-done.14.got_key
  39.7 0.0 collective-permute-done.15.got_value
  39.7 0.8 %shard_map.114 = (bf16[128,512]{1,0:T(8,128)(2,1)}, bf16[128,512]{1,0:T(8,128)(2,1)}, bf16[64,512]{1,0:T(8,128)(2,1)}, bf16[64,512]{1,0:T(8,128)(2,1)}) custom-call(f32[128,512]{1,0:T(8,128)S(1)} %get-tuple-element.70.own_key, f32[128,512]{1,0:T(8,128)S(1)} %get-tuple-element.71.own_value, bf16[128,512]{1,0:T(8,128)(2,1)S(1)} %collective-permute-done.14.got_key, ...), custom_call_target="tpu_custom_call" | custom-call | flops 1048576 | bytes 4096 | tf_op jit(solution)/shard_map/pallas_call | solution.py:398
  (4 shorter events, 0.1 us)
Async XLA Ops:
  1.5 6.6 %collective-permute-start = (bf16[128,512]{1,0:T(8,128)(2,1)}, bf16[128,512]{1,0:T(8,128)(2,1)S(1)}, u32[]{:S(2)}, u32[]{:S(2)}) collective-permute-start(bf16[128,512]{1,0:T(8,128)(2,1)} %key_hbm.3), channel_id=1, source_target_pairs={{0,1},{1,0},{2,3},{3,2},{4,5},{5,4},{6,7},{7,6},{8,9},{9,8},{10,11... | collective-permute-start | bytes 393224 | tf_op jit(solution)/shard_map/ppermute | solution.py:431
  2.1 6.1 %collective-permute-start.1 = (bf16[128,512]{1,0:T(8,128)(2,1)}, bf16[128,512]{1,0:T(8,128)(2,1)S(1)}, u32[]{:S(2)}, u32[]{:S(2)}) collective-permute-start(bf16[128,512]{1,0:T(8,128)(2,1)} %value_hbm.1), channel_id=1, source_target_pairs={{0,1},{1,0},{2,3},{3,2},{4,5},{5,4},{6,7},{7,6},{8,9},{9,8},{10,11... | collective-permute-start | bytes 393224 | tf_op jit(solution)/shard_map/ppermute | solution.py:431
  2.1 11.4 %collective-permute-start.2 = (bf16[64,1024]{1,0:T(8,128)(2,1)S(1)}, bf16[64,1024]{1,0:T(8,128)(2,1)S(1)}, u32[]{:S(2)}, u32[]{:S(2)}) collective-permute-start(bf16[64,1024]{1,0:T(8,128)(2,1)S(1)} %pad_select_fusion), channel_id=1, source_target_pairs={{0,8},{4,12},{8,0},{12,4},{1,9},{5,13},{9,1},{13,5},{2,10},{6,14},... | collective-permute-start | bytes 393224 | tf_op jit(solution)/shard_map/ppermute | solution.py:430
  6.2 7.4 %collective-permute-start.6 = (bf16[64,1024]{1,0:T(8,128)(2,1)S(1)}, bf16[64,1024]{1,0:T(8,128)(2,1)S(1)}, u32[]{:S(2)}, u32[]{:S(2)}) collective-permute-start(bf16[64,1024]{1,0:T(8,128)(2,1)S(1)} %pad_select_fusion), channel_id=1, source_target_pairs={{0,12},{4,0},{8,4},{12,8},{1,13},{5,1},{9,5},{13,9},{2,14},{6,2},{... | collective-permute-start | bytes 393224 | tf_op jit(solution)/shard_map/ppermute | solution.py:430
  7.5 9.2 %collective-permute-start.3 = (bf16[64,1024]{1,0:T(8,128)(2,1)S(1)}, bf16[64,1024]{1,0:T(8,128)(2,1)S(1)}, u32[]{:S(2)}, u32[]{:S(2)}) collective-permute-start(bf16[64,1024]{1,0:T(8,128)(2,1)S(1)} %pad_select_fusion), channel_id=1, source_target_pairs={{0,4},{4,8},{8,12},{12,0},{1,5},{5,9},{9,13},{13,1},{2,6},{6,10},{... | collective-permute-start | bytes 393224 | tf_op jit(solution)/shard_map/ppermute | solution.py:430
  8.2 0.7 %copy-start = (s32[4]{0:T(128)S(1)}, s32[4]{0:T(128)}, u32[]{:S(2)}) copy-start(s32[4]{0:T(128)} %ratios.1) | copy-start | bytes 52
  13.6 3.2 %collective-permute-start.4 = (bf16[64,1024]{1,0:T(8,128)(2,1)S(1)}, bf16[64,1024]{1,0:T(8,128)(2,1)S(1)}, u32[]{:S(2)}, u32[]{:S(2)}) collective-permute-start(bf16[64,1024]{1,0:T(8,128)(2,1)S(1)} %collective-permute-done.2.refs_9_.refs_2_), channel_id=1, source_target_pairs={{0,1},{1,0},{2,3},{3,2},{4,5},{5,4},{6,7},{7,6},{8,9},{9,8},{10,11... | collective-permute-start | bytes 393224 | tf_op jit(solution)/shard_map/ppermute | solution.py:452
  13.6 3.2 %collective-permute-start.7 = (bf16[64,1024]{1,0:T(8,128)(2,1)S(1)}, bf16[64,1024]{1,0:T(8,128)(2,1)S(1)}, u32[]{:S(2)}, u32[]{:S(2)}) collective-permute-start(bf16[64,1024]{1,0:T(8,128)(2,1)S(1)} %collective-permute-done.6.refs_11_.refs_4_), channel_id=1, source_target_pairs={{0,1},{1,0},{2,3},{3,2},{4,5},{5,4},{6,7},{7,6},{8,9},{9,8},{10,11... | collective-permute-start | bytes 393224 | tf_op jit(solution)/shard_map/ppermute | solution.py:452
  16.7 1.3 %collective-permute-start.5 = (bf16[64,1024]{1,0:T(8,128)(2,1)S(1)}, bf16[64,1024]{1,0:T(8,128)(2,1)S(1)}, u32[]{:S(2)}, u32[]{:S(2)}) collective-permute-start(bf16[64,1024]{1,0:T(8,128)(2,1)S(1)} %collective-permute-done.3.refs_7_.refs_0_), channel_id=1, source_target_pairs={{0,1},{1,0},{2,3},{3,2},{4,5},{5,4},{6,7},{7,6},{8,9},{9,8},{10,11... | collective-permute-start | bytes 393224 | tf_op jit(solution)/shard_map/ppermute | solution.py:456
  19.3 1.4 %collective-permute-start.8 = (bf16[64,1024]{1,0:T(8,128)(2,1)S(1)}, bf16[64,1024]{1,0:T(8,128)(2,1)S(1)}, u32[]{:S(2)}, u32[]{:S(2)}) collective-permute-start(bf16[64,1024]{1,0:T(8,128)(2,1)S(1)} %get-tuple-element.58), channel_id=1, source_target_pairs={{0,1},{1,0},{2,3},{3,2},{4,5},{5,4},{6,7},{7,6},{8,9},{9,8},{10,11... | collective-permute-start | bytes 393224 | tf_op jit(solution)/shard_map/ppermute | solution.py:477
  19.5 9.6 %collective-permute-start.10 = (bf16[64,1024]{1,0:T(8,128)(2,1)S(1)}, bf16[64,1024]{1,0:T(8,128)(2,1)S(1)}, u32[]{:S(2)}, u32[]{:S(2)}) collective-permute-start(bf16[64,1024]{1,0:T(8,128)(2,1)S(1)} %get-tuple-element.60), channel_id=1, source_target_pairs={{0,1},{1,0},{2,3},{3,2},{4,5},{5,4},{6,7},{7,6},{8,9},{9,8},{10,11... | collective-permute-start | bytes 393224 | tf_op jit(solution)/shard_map/ppermute | solution.py:477
  19.9 10.4 %collective-permute-start.12 = (bf16[64,1024]{1,0:T(8,128)(2,1)S(1)}, bf16[64,1024]{1,0:T(8,128)(2,1)S(1)}, u32[]{:S(2)}, u32[]{:S(2)}) collective-permute-start(bf16[64,1024]{1,0:T(8,128)(2,1)S(1)} %get-tuple-element.62), channel_id=1, source_target_pairs={{0,1},{1,0},{2,3},{3,2},{4,5},{5,4},{6,7},{7,6},{8,9},{9,8},{10,11... | collective-permute-start | bytes 393224 | tf_op jit(solution)/shard_map/ppermute | solution.py:477
  20.8 16.1 %collective-permute-start.9 = (bf16[64,1024]{1,0:T(8,128)(2,1)S(1)}, bf16[64,1024]{1,0:T(8,128)(2,1)S(1)}, u32[]{:S(2)}, u32[]{:S(2)}) collective-permute-start(bf16[64,1024]{1,0:T(8,128)(2,1)S(1)} %add_convert_fusion.2), channel_id=1, source_target_pairs={{0,8},{4,12},{8,0},{12,4},{1,9},{5,13},{9,1},{13,5},{2,10},{6,14},... | collective-permute-start | bytes 393224 | tf_op jit(solution)/shard_map/ppermute | solution.py:482
  29.1 7.7 %collective-permute-start.11 = (bf16[64,1024]{1,0:T(8,128)(2,1)S(1)}, bf16[64,1024]{1,0:T(8,128)(2,1)S(1)}, u32[]{:S(2)}, u32[]{:S(2)}) collective-permute-start(bf16[64,1024]{1,0:T(8,128)(2,1)S(1)} %add_convert_fusion.1), channel_id=1, source_target_pairs={{0,12},{4,0},{8,4},{12,8},{1,13},{5,1},{9,5},{13,9},{2,14},{6,2},{... | collective-permute-start | bytes 393224 | tf_op jit(solution)/shard_map/ppermute | solution.py:482
  30.3 9.4 %collective-permute-start.13 = (bf16[64,1024]{1,0:T(8,128)(2,1)S(1)}, bf16[64,1024]{1,0:T(8,128)(2,1)S(1)}, u32[]{:S(2)}, u32[]{:S(2)}) collective-permute-start(bf16[64,1024]{1,0:T(8,128)(2,1)S(1)} %add_convert_fusion), channel_id=1, source_target_pairs={{12,0},{13,1},{14,2},{15,3},{28,16},{29,17},{30,18},{31,19}} | collective-permute-start | bytes 393224 | tf_op jit(solution)/shard_map/ppermute | solution.py:482
  33.4 6.3 %collective-permute-start.14 = (bf16[128,512]{1,0:T(8,128)(2,1)S(1)}, bf16[128,512]{1,0:T(8,128)(2,1)S(1)}, u32[]{:S(2)}, u32[]{:S(2)}) collective-permute-start(bf16[128,512]{1,0:T(8,128)(2,1)S(1)} %get-tuple-element.72), channel_id=1, source_target_pairs={{0,1},{1,0},{2,3},{3,2},{4,5},{5,4},{6,7},{7,6},{8,9},{9,8},{10,11... | collective-permute-start | bytes 393224 | tf_op jit(solution)/shard_map/ppermute | solution.py:510
  33.5 6.2 %collective-permute-start.15 = (bf16[128,512]{1,0:T(8,128)(2,1)S(1)}, bf16[128,512]{1,0:T(8,128)(2,1)S(1)}, u32[]{:S(2)}, u32[]{:S(2)}) collective-permute-start(bf16[128,512]{1,0:T(8,128)(2,1)S(1)} %get-tuple-element.73), channel_id=1, source_target_pairs={{0,1},{1,0},{2,3},{3,2},{4,5},{5,4},{6,7},{7,6},{8,9},{9,8},{10,11... | collective-permute-start | bytes 393224 | tf_op jit(solution)/shard_map/ppermute | solution.py:510

commit v7 on v6

--- a/solution.py
+++ b/solution.py
@@ -15,7 +15,7 @@
 NT = (((1,), (1,)), ((), ()))
 HIDDEN = -3e38
 JOIN = 4
-BLOCK = 16
+BLOCK = 32
 SCALE = DH ** (-0.5)
 LOG_SCALE = SCALE * math.log2(math.e)
 

time: 40.9 us -> 40.9 us (level)
  no operation moved by 1% of the time
where the time goes in v7:
time: 40.9 us; the launch traced here: 40.6 us
  starting transfers between devices  19.4 us (47%)
  Pallas kernels  10.7 us (26%)
  waiting for transfers between devices  8.02 us (20%)
  other arithmetic  0.99 us (2%)
  between operations  0.91 us (2%)
  local copies, waits for them, and re-layouts  0.65 us (2%)
    ppermute x3, starting transfers between devices, local(): sums = [lax.ppermute(pairs[k], 'ctx', down[k]) for k in order]  10.9 us
    pallas_call x5, Pallas kernels, call(): pl.pallas_call(kernel, out_shape=[jax.ShapeDtypeStruct(*x) for x in outs]...  10.7 us
    ppermute x3, starting transfers between devices, local(): own = {k: lax.ppermute(beacons, 'ctx', up(k)) for k in reversed(order)}  6.04 us
    ppermute x3, waiting for transfers between devices, local(): own = {k: lax.ppermute(beacons, 'ctx', up(k)) for k in reversed(order)}  3.09 us
    ppermute x3, waiting for transfers between devices, local(): sums = [lax.ppermute(pairs[k], 'ctx', down[k]) for k in order]  2.88 us
    ppermute x1, waiting for transfers between devices, local(): other |= {k: lax.ppermute(own[k], 'sub', swap) for k in middle}  1.34 us
    select_n x1, other arithmetic, local(): jnp.where(left, jnp.pad(beacon_keys, ((0, 0), (0, wide))), jnp.pad(beacon...  0.9 us
  transfers between devices with their start and end apart: 16, of which 5 were waited for; matrix products, arithmetic and copies ran while one was open for 0% of the time, Pallas kernels for 21%

profile of v7, /device:TPU:0, one launch (start us, length us, event | category | flops | bytes accessed | tf_op | source)
XLA Modules:
  0.0 40.6 jit_solution(3965308538084498345)
XLA Ops:
  0.6 0.9 %pad_select_fusion = bf16[64,1024]{1,0:T(8,128)(2,1)S(1)} fusion(bf16[64,512]{1,0:T(8,128)(2,1)} %param.11, bf16[64,512]{1,0:T(8,128)(2,1)} %param.10, pred[1024]{0:T(1024)(128)(4,1)S(1)} %iota_compare_fusion), kind=kLoop, calls=%fused_computation.3 | loop fusion | flops 65536 | bytes 263168 | tf_op jit(solution)/shard_map/jit(_where)/select_n | solution.py:428
  1.5 0.5 %collective-permute-start = (bf16[128,512]{1,0:T(8,128)(2,1)}, bf16[128,512]{1,0:T(8,128)(2,1)S(1)}, u32[]{:S(2)}, u32[]{:S(2)}) collective-permute-start(bf16[128,512]{1,0:T(8,128)(2,1)} %key_hbm.3), channel_id=1, source_target_pairs={{0,1},{1,0},{2,3},{3,2},{4,5},{5,4},{6,7},{7,6},{8,9},{9,8},{10,11... | collective-permute-start | bytes 393224 | tf_op jit(solution)/shard_map/ppermute | solution.py:431
  2.1 0.1 collective-permute-start.1
  2.1 4.0 %collective-permute-start.2 = (bf16[64,1024]{1,0:T(8,128)(2,1)S(1)}, bf16[64,1024]{1,0:T(8,128)(2,1)S(1)}, u32[]{:S(2)}, u32[]{:S(2)}) collective-permute-start(bf16[64,1024]{1,0:T(8,128)(2,1)S(1)} %pad_select_fusion), channel_id=1, source_target_pairs={{0,8},{4,12},{8,0},{12,4},{1,9},{5,13},{9,1},{13,5},{2,10},{6,14},... | collective-permute-start | bytes 393224 | tf_op jit(solution)/shard_map/ppermute | solution.py:430
  6.2 1.3 %collective-permute-start.6 = (bf16[64,1024]{1,0:T(8,128)(2,1)S(1)}, bf16[64,1024]{1,0:T(8,128)(2,1)S(1)}, u32[]{:S(2)}, u32[]{:S(2)}) collective-permute-start(bf16[64,1024]{1,0:T(8,128)(2,1)S(1)} %pad_select_fusion), channel_id=1, source_target_pairs={{0,12},{4,0},{8,4},{12,8},{1,13},{5,1},{9,5},{13,9},{2,14},{6,2},{... | collective-permute-start | bytes 393224 | tf_op jit(solution)/shard_map/ppermute | solution.py:430
  7.5 0.7 %collective-permute-start.3 = (bf16[64,1024]{1,0:T(8,128)(2,1)S(1)}, bf16[64,1024]{1,0:T(8,128)(2,1)S(1)}, u32[]{:S(2)}, u32[]{:S(2)}) collective-permute-start(bf16[64,1024]{1,0:T(8,128)(2,1)S(1)} %pad_select_fusion), channel_id=1, source_target_pairs={{0,4},{4,8},{8,12},{12,0},{1,5},{5,9},{9,13},{13,1},{2,6},{6,10},{... | collective-permute-start | bytes 393224 | tf_op jit(solution)/shard_map/ppermute | solution.py:430
  8.2 0.0 collective-permute-done.other_key
  8.2 0.0 collective-permute-done.1.other_value
  8.2 0.0 copy-start
  8.2 0.7 %copy-done = s32[4]{0:T(128)S(1)} copy-done((s32[4]{0:T(128)S(1)}, s32[4]{0:T(128)}, u32[]{:S(2)}) %copy-start) | copy-done | bytes 40
  8.8 4.3 %shard_map.110 = (bf16[128,4096]{1,0:T(8,128)(2,1)S(1)}, bf16[128,4096]{1,0:T(8,128)(2,1)S(1)}, bf16[384,128]{1,0:T(8,128)(2,1)S(1)}, f32[8,256,512]{2,1,0:T(8,1...) custom-call(s32[4]{0:T(128)S(1)} %copy-done, bf16[128,4096]{1,0:T(8,128)(2,1)} %q_hbm.1, ...), custom_call_target="tpu_custom_call" | custom-call | flops 536870912 | bytes 2097152 | tf_op jit(solution)/shard_map/pallas_call | solution.py:398
  13.1 0.4 %collective-permute-done.2.refs_9_.refs_2_ = bf16[64,1024]{1,0:T(8,128)(2,1)S(1)} collective-permute-done((bf16[64,1024]{1,0:T(8,128)(2,1)S(1)}, bf16[64,1024]{1,0:T(8,128)(2,1)S(1)}, u32[]{:S(2)}, u32[]{:S(2)}) %collective-permute-start.2) | collective-permute-done | bytes 131104 | tf_op jit(solution)/shard_map/ppermute | solution.py:430
  13.6 0.0 collective-permute-start.4
  13.6 0.0 collective-permute-done.6.refs_11_.refs_4_
  13.6 0.5 %collective-permute-start.7 = (bf16[64,1024]{1,0:T(8,128)(2,1)S(1)}, bf16[64,1024]{1,0:T(8,128)(2,1)S(1)}, u32[]{:S(2)}, u32[]{:S(2)}) collective-permute-start(bf16[64,1024]{1,0:T(8,128)(2,1)S(1)} %collective-permute-done.6.refs_11_.refs_4_), channel_id=1, source_target_pairs={{0,1},{1,0},{2,3},{3,2},{4,5},{5,4},{6,7},{7,6},{8,9},{9,8},{10,11... | collective-permute-start | bytes 393224 | tf_op jit(solution)/shard_map/ppermute | solution.py:452
  14.1 2.6 %collective-permute-done.3.refs_7_.refs_0_ = bf16[64,1024]{1,0:T(8,128)(2,1)S(1)} collective-permute-done((bf16[64,1024]{1,0:T(8,128)(2,1)S(1)}, bf16[64,1024]{1,0:T(8,128)(2,1)S(1)}, u32[]{:S(2)}, u32[]{:S(2)}) %collective-permute-start.3) | collective-permute-done | bytes 131104 | tf_op jit(solution)/shard_map/ppermute | solution.py:430
  16.7 0.0 collective-permute-done.4.refs_10_.refs_3_
  16.7 0.0 collective-permute-start.5
  16.7 0.0 collective-permute-done.7.refs_12_.refs_5_
  16.7 1.3 %collective-permute-done.5.refs_8_.refs_1_ = bf16[64,1024]{1,0:T(8,128)(2,1)S(1)} collective-permute-done((bf16[64,1024]{1,0:T(8,128)(2,1)S(1)}, bf16[64,1024]{1,0:T(8,128)(2,1)S(1)}, u32[]{:S(2)}, u32[]{:S(2)}) %collective-permute-start.5) | collective-permute-done | bytes 131104 | tf_op jit(solution)/shard_map/ppermute | solution.py:456
  18.1 1.2 %shard_map.111 = (f32[8,8,512]{2,1,0:T(8,128)S(1)}, f32[8,8,512]{2,1,0:T(8,128)S(1)}, bf16[8,384,512]{2,1,0:T(8,128)(2,1)S(1)}, f32[64,1024]{1,0:T(8,128)S(1)}, ...) custom-call(bf16[128,4096]{1,0:T(8,128)(2,1)S(1)} %get-tuple-element, ...), custom_call_target="tpu_custom_call" | custom-call | flops 1610612736 | bytes 6291456 | tf_op jit(solution)/shard_map/pallas_call | solution.py:398
  19.3 0.2 collective-permute-start.8
  19.5 0.4 collective-permute-start.10
  19.9 0.1 collective-permute-start.12
  20.0 0.7 %collective-permute-done.8 = bf16[64,1024]{1,0:T(8,128)(2,1)S(1)} collective-permute-done((bf16[64,1024]{1,0:T(8,128)(2,1)S(1)}, bf16[64,1024]{1,0:T(8,128)(2,1)S(1)}, u32[]{:S(2)}, u32[]{:S(2)}) %collective-permute-start.8) | collective-permute-done | bytes 131104 | tf_op jit(solution)/shard_map/ppermute | solution.py:477
  20.8 8.4 %collective-permute-start.9 = (bf16[64,1024]{1,0:T(8,128)(2,1)S(1)}, bf16[64,1024]{1,0:T(8,128)(2,1)S(1)}, u32[]{:S(2)}, u32[]{:S(2)}) collective-permute-start(bf16[64,1024]{1,0:T(8,128)(2,1)S(1)} %add_convert_fusion.2), channel_id=1, source_target_pairs={{0,8},{4,12},{8,0},{12,4},{1,9},{5,13},{9,1},{13,5},{2,10},{6,14},... | collective-permute-start | bytes 393224 | tf_op jit(solution)/shard_map/ppermute | solution.py:482
  29.1 0.0 collective-permute-done.10
  29.2 1.1 %collective-permute-start.11 = (bf16[64,1024]{1,0:T(8,128)(2,1)S(1)}, bf16[64,1024]{1,0:T(8,128)(2,1)S(1)}, u32[]{:S(2)}, u32[]{:S(2)}) collective-permute-start(bf16[64,1024]{1,0:T(8,128)(2,1)S(1)} %add_convert_fusion.1), channel_id=1, source_target_pairs={{0,12},{4,0},{8,4},{12,8},{1,13},{5,1},{9,5},{13,9},{2,14},{6,2},{... | collective-permute-start | bytes 393224 | tf_op jit(solution)/shard_map/ppermute | solution.py:482
  30.2 0.0 collective-permute-done.12
  30.3 1.5 %collective-permute-start.13 = (bf16[64,1024]{1,0:T(8,128)(2,1)S(1)}, bf16[64,1024]{1,0:T(8,128)(2,1)S(1)}, u32[]{:S(2)}, u32[]{:S(2)}) collective-permute-start(bf16[64,1024]{1,0:T(8,128)(2,1)S(1)} %add_convert_fusion), channel_id=1, source_target_pairs={{12,0},{13,1},{14,2},{15,3},{28,16},{29,17},{30,18},{31,19}} | collective-permute-start | bytes 393224 | tf_op jit(solution)/shard_map/ppermute | solution.py:482
  31.8 1.5 %shard_map.112 = (bf16[8,256,512]{2,1,0:T(8,128)(2,1)S(1)}, f32[128,512]{1,0:T(8,128)S(1)}, f32[128,512]{1,0:T(8,128)S(1)}, bf16[128,512]{1,0:T(8,128)(2,1)S(1)}, bf16[128,512]{1,0:T(8,128)(2,1)S(1)}) custom-call(bf16[128,4096]{1,0:T(8,128)(2,1)S(1)} %get-tuple-element.45.refs_0_.q_buf, bf16[128,4096]{1,0:T(8,128)(2,1)S(1)} %get-tuple-element.46.refs_1_.g_buf, ...), custom_call_target="tpu_custom_call" | custom-call | flops 1048576 | bytes 4096 | tf_op jit(solution)/shard_map/pallas_call | solution.py:398
  33.3 0.1 collective-permute-start.14
  33.4 0.5 %collective-permute-start.15 = (bf16[128,512]{1,0:T(8,128)(2,1)S(1)}, bf16[128,512]{1,0:T(8,128)(2,1)S(1)}, u32[]{:S(2)}, u32[]{:S(2)}) collective-permute-start(bf16[128,512]{1,0:T(8,128)(2,1)S(1)} %get-tuple-element.73), channel_id=1, source_target_pairs={{0,1},{1,0},{2,3},{3,2},{4,5},{5,4},{6,7},{7,6},{8,9},{9,8},{10,11... | collective-permute-start | bytes 393224 | tf_op jit(solution)/shard_map/ppermute | solution.py:510
  33.9 2.8 %shard_map.113 = bf16[128,4096]{1,0:T(8,128)(2,1)} custom-call(bf16[8,256,512]{2,1,0:T(8,128)(2,1)S(1)} %get-tuple-element.67.near_slopes, bf16[8,384,512]{2,1,0:T(8,128)(2,1)S(1)} %get-tuple-element.68.far_slopes, bf16[128,512]{1,0:T(8,128)(2,1)} %key_hbm.3, bf16[128,512]{1,0:T(8,128)(2,1)S(1)} %collective-permute-done.other_key, ...), custom_call_target="tpu_custom_call" | custom-call | flops 1048576 | bytes 4096 | tf_op jit(solution)/shard_map/pallas_call | solution.py:398
  36.7 0.0 collective-permute-done.9.refs_0_
  36.7 0.0 collective-permute-done.11.refs_1_
  36.8 2.9 %collective-permute-done.13.refs_2_ = bf16[64,1024]{1,0:T(8,128)(2,1)S(1)} collective-permute-done((bf16[64,1024]{1,0:T(8,128)(2,1)S(1)}, bf16[64,1024]{1,0:T(8,128)(2,1)S(1)}, u32[]{:S(2)}, u32[]{:S(2)}) %collective-permute-start.13) | collective-permute-done | bytes 131104 | tf_op jit(solution)/shard_map/ppermute | solution.py:482
  39.6 0.0 collective-permute-done.14.got_key
  39.6 0.0 collective-permute-done.15.got_value
  39.6 0.8 %shard_map.114 = (bf16[128,512]{1,0:T(8,128)(2,1)}, bf16[128,512]{1,0:T(8,128)(2,1)}, bf16[64,512]{1,0:T(8,128)(2,1)}, bf16[64,512]{1,0:T(8,128)(2,1)}) custom-call(f32[128,512]{1,0:T(8,128)S(1)} %get-tuple-element.70.own_key, f32[128,512]{1,0:T(8,128)S(1)} %get-tuple-element.71.own_value, bf16[128,512]{1,0:T(8,128)(2,1)S(1)} %collective-permute-done.14.got_key, ...), custom_call_target="tpu_custom_call" | custom-call | flops 1048576 | bytes 4096 | tf_op jit(solution)/shard_map/pallas_call | solution.py:398
  (4 shorter events, 0.1 us)
Async XLA Ops:
  1.5 6.6 %collective-permute-start = (bf16[128,512]{1,0:T(8,128)(2,1)}, bf16[128,512]{1,0:T(8,128)(2,1)S(1)}, u32[]{:S(2)}, u32[]{:S(2)}) collective-permute-start(bf16[128,512]{1,0:T(8,128)(2,1)} %key_hbm.3), channel_id=1, source_target_pairs={{0,1},{1,0},{2,3},{3,2},{4,5},{5,4},{6,7},{7,6},{8,9},{9,8},{10,11... | collective-permute-start | bytes 393224 | tf_op jit(solution)/shard_map/ppermute | solution.py:431
  2.1 6.1 %collective-permute-start.1 = (bf16[128,512]{1,0:T(8,128)(2,1)}, bf16[128,512]{1,0:T(8,128)(2,1)S(1)}, u32[]{:S(2)}, u32[]{:S(2)}) collective-permute-start(bf16[128,512]{1,0:T(8,128)(2,1)} %value_hbm.1), channel_id=1, source_target_pairs={{0,1},{1,0},{2,3},{3,2},{4,5},{5,4},{6,7},{7,6},{8,9},{9,8},{10,11... | collective-permute-start | bytes 393224 | tf_op jit(solution)/shard_map/ppermute | solution.py:431
  2.1 11.4 %collective-permute-start.2 = (bf16[64,1024]{1,0:T(8,128)(2,1)S(1)}, bf16[64,1024]{1,0:T(8,128)(2,1)S(1)}, u32[]{:S(2)}, u32[]{:S(2)}) collective-permute-start(bf16[64,1024]{1,0:T(8,128)(2,1)S(1)} %pad_select_fusion), channel_id=1, source_target_pairs={{0,8},{4,12},{8,0},{12,4},{1,9},{5,13},{9,1},{13,5},{2,10},{6,14},... | collective-permute-start | bytes 393224 | tf_op jit(solution)/shard_map/ppermute | solution.py:430
  6.2 7.4 %collective-permute-start.6 = (bf16[64,1024]{1,0:T(8,128)(2,1)S(1)}, bf16[64,1024]{1,0:T(8,128)(2,1)S(1)}, u32[]{:S(2)}, u32[]{:S(2)}) collective-permute-start(bf16[64,1024]{1,0:T(8,128)(2,1)S(1)} %pad_select_fusion), channel_id=1, source_target_pairs={{0,12},{4,0},{8,4},{12,8},{1,13},{5,1},{9,5},{13,9},{2,14},{6,2},{... | collective-permute-start | bytes 393224 | tf_op jit(solution)/shard_map/ppermute | solution.py:430
  7.5 9.2 %collective-permute-start.3 = (bf16[64,1024]{1,0:T(8,128)(2,1)S(1)}, bf16[64,1024]{1,0:T(8,128)(2,1)S(1)}, u32[]{:S(2)}, u32[]{:S(2)}) collective-permute-start(bf16[64,1024]{1,0:T(8,128)(2,1)S(1)} %pad_select_fusion), channel_id=1, source_target_pairs={{0,4},{4,8},{8,12},{12,0},{1,5},{5,9},{9,13},{13,1},{2,6},{6,10},{... | collective-permute-start | bytes 393224 | tf_op jit(solution)/shard_map/ppermute | solution.py:430
  8.2 0.7 %copy-start = (s32[4]{0:T(128)S(1)}, s32[4]{0:T(128)}, u32[]{:S(2)}) copy-start(s32[4]{0:T(128)} %ratios.1) | copy-start | bytes 52
  13.6 3.2 %collective-permute-start.4 = (bf16[64,1024]{1,0:T(8,128)(2,1)S(1)}, bf16[64,1024]{1,0:T(8,128)(2,1)S(1)}, u32[]{:S(2)}, u32[]{:S(2)}) collective-permute-start(bf16[64,1024]{1,0:T(8,128)(2,1)S(1)} %collective-permute-done.2.refs_9_.refs_2_), channel_id=1, source_target_pairs={{0,1},{1,0},{2,3},{3,2},{4,5},{5,4},{6,7},{7,6},{8,9},{9,8},{10,11... | collective-permute-start | bytes 393224 | tf_op jit(solution)/shard_map/ppermute | solution.py:452
  13.6 3.2 %collective-permute-start.7 = (bf16[64,1024]{1,0:T(8,128)(2,1)S(1)}, bf16[64,1024]{1,0:T(8,128)(2,1)S(1)}, u32[]{:S(2)}, u32[]{:S(2)}) collective-permute-start(bf16[64,1024]{1,0:T(8,128)(2,1)S(1)} %collective-permute-done.6.refs_11_.refs_4_), channel_id=1, source_target_pairs={{0,1},{1,0},{2,3},{3,2},{4,5},{5,4},{6,7},{7,6},{8,9},{9,8},{10,11... | collective-permute-start | bytes 393224 | tf_op jit(solution)/shard_map/ppermute | solution.py:452
  16.7 1.3 %collective-permute-start.5 = (bf16[64,1024]{1,0:T(8,128)(2,1)S(1)}, bf16[64,1024]{1,0:T(8,128)(2,1)S(1)}, u32[]{:S(2)}, u32[]{:S(2)}) collective-permute-start(bf16[64,1024]{1,0:T(8,128)(2,1)S(1)} %collective-permute-done.3.refs_7_.refs_0_), channel_id=1, source_target_pairs={{0,1},{1,0},{2,3},{3,2},{4,5},{5,4},{6,7},{7,6},{8,9},{9,8},{10,11... | collective-permute-start | bytes 393224 | tf_op jit(solution)/shard_map/ppermute | solution.py:456
  19.3 1.4 %collective-permute-start.8 = (bf16[64,1024]{1,0:T(8,128)(2,1)S(1)}, bf16[64,1024]{1,0:T(8,128)(2,1)S(1)}, u32[]{:S(2)}, u32[]{:S(2)}) collective-permute-start(bf16[64,1024]{1,0:T(8,128)(2,1)S(1)} %get-tuple-element.58), channel_id=1, source_target_pairs={{0,1},{1,0},{2,3},{3,2},{4,5},{5,4},{6,7},{7,6},{8,9},{9,8},{10,11... | collective-permute-start | bytes 393224 | tf_op jit(solution)/shard_map/ppermute | solution.py:477
  19.5 9.6 %collective-permute-start.10 = (bf16[64,1024]{1,0:T(8,128)(2,1)S(1)}, bf16[64,1024]{1,0:T(8,128)(2,1)S(1)}, u32[]{:S(2)}, u32[]{:S(2)}) collective-permute-start(bf16[64,1024]{1,0:T(8,128)(2,1)S(1)} %get-tuple-element.60), channel_id=1, source_target_pairs={{0,1},{1,0},{2,3},{3,2},{4,5},{5,4},{6,7},{7,6},{8,9},{9,8},{10,11... | collective-permute-start | bytes 393224 | tf_op jit(solution)/shard_map/ppermute | solution.py:477
  19.9 10.3 %collective-permute-start.12 = (bf16[64,1024]{1,0:T(8,128)(2,1)S(1)}, bf16[64,1024]{1,0:T(8,128)(2,1)S(1)}, u32[]{:S(2)}, u32[]{:S(2)}) collective-permute-start(bf16[64,1024]{1,0:T(8,128)(2,1)S(1)} %get-tuple-element.62), channel_id=1, source_target_pairs={{0,1},{1,0},{2,3},{3,2},{4,5},{5,4},{6,7},{7,6},{8,9},{9,8},{10,11... | collective-permute-start | bytes 393224 | tf_op jit(solution)/shard_map/ppermute | solution.py:477
  20.8 16.0 %collective-permute-start.9 = (bf16[64,1024]{1,0:T(8,128)(2,1)S(1)}, bf16[64,1024]{1,0:T(8,128)(2,1)S(1)}, u32[]{:S(2)}, u32[]{:S(2)}) collective-permute-start(bf16[64,1024]{1,0:T(8,128)(2,1)S(1)} %add_convert_fusion.2), channel_id=1, source_target_pairs={{0,8},{4,12},{8,0},{12,4},{1,9},{5,13},{9,1},{13,5},{2,10},{6,14},... | collective-permute-start | bytes 393224 | tf_op jit(solution)/shard_map/ppermute | solution.py:482
  29.2 7.6 %collective-permute-start.11 = (bf16[64,1024]{1,0:T(8,128)(2,1)S(1)}, bf16[64,1024]{1,0:T(8,128)(2,1)S(1)}, u32[]{:S(2)}, u32[]{:S(2)}) collective-permute-start(bf16[64,1024]{1,0:T(8,128)(2,1)S(1)} %add_convert_fusion.1), channel_id=1, source_target_pairs={{0,12},{4,0},{8,4},{12,8},{1,13},{5,1},{9,5},{13,9},{2,14},{6,2},{... | collective-permute-start | bytes 393224 | tf_op jit(solution)/shard_map/ppermute | solution.py:482
  30.3 9.4 %collective-permute-start.13 = (bf16[64,1024]{1,0:T(8,128)(2,1)S(1)}, bf16[64,1024]{1,0:T(8,128)(2,1)S(1)}, u32[]{:S(2)}, u32[]{:S(2)}) collective-permute-start(bf16[64,1024]{1,0:T(8,128)(2,1)S(1)} %add_convert_fusion), channel_id=1, source_target_pairs={{12,0},{13,1},{14,2},{15,3},{28,16},{29,17},{30,18},{31,19}} | collective-permute-start | bytes 393224 | tf_op jit(solution)/shard_map/ppermute | solution.py:482
  33.3 6.3 %collective-permute-start.14 = (bf16[128,512]{1,0:T(8,128)(2,1)S(1)}, bf16[128,512]{1,0:T(8,128)(2,1)S(1)}, u32[]{:S(2)}, u32[]{:S(2)}) collective-permute-start(bf16[128,512]{1,0:T(8,128)(2,1)S(1)} %get-tuple-element.72), channel_id=1, source_target_pairs={{0,1},{1,0},{2,3},{3,2},{4,5},{5,4},{6,7},{7,6},{8,9},{9,8},{10,11... | collective-permute-start | bytes 393224 | tf_op jit(solution)/shard_map/ppermute | solution.py:510
  33.4 6.2 %collective-permute-start.15 = (bf16[128,512]{1,0:T(8,128)(2,1)S(1)}, bf16[128,512]{1,0:T(8,128)(2,1)S(1)}, u32[]{:S(2)}, u32[]{:S(2)}) collective-permute-start(bf16[128,512]{1,0:T(8,128)(2,1)S(1)} %get-tuple-element.73), channel_id=1, source_target_pairs={{0,1},{1,0},{2,3},{3,2},{4,5},{5,4},{6,7},{7,6},{8,9},{9,8},{10,11... | collective-permute-start | bytes 393224 | tf_op jit(solution)/shard_map/ppermute | solution.py:510
